TPU v7x, 256 devices: a whole 4x4x8 slice. The times are simulated.
256 devices in a mesh: slab: 128 (over z, x, y), ch: 2 (over core).
Axes of the slice: x: 4, y: 4, z: 8, core: 2. Of those that a mesh axis runs over, the one named last changes fastest.
Arguments:
- features: bfloat16 [6144, 64, 256], P('slab', None, 'ch'), may hold values from -6 to 6
- cotangent: bfloat16 [6144, 64, 256], P('slab', None, 'ch'), may hold values from -6 to 6
- weight: bfloat16 [27, 256, 256], P(None, 'ch'), may hold values from -0.078125 to 0.078125
- gain: float32 [256], P('ch'), may hold values from 0.1 to 1.9
- shift: float32 [256], P('ch'), may hold values from -3 to 3
- counts: int32 [128], P('slab'), may hold values from 6 to 48, as said below
- neighbours: int32 [6144, 27], P('slab'), may hold values from 0 to 144, as said below
Outputs:
- grad_features: bfloat16 [6144, 64, 256], P('slab', None, 'ch')
- grad_weight: float32 [27, 256, 256], P(None, 'ch')
- grad_gain: float32 [256], P('ch')
- grad_shift: float32 [256], P('ch')
Inputs may be any that keep to these rules, and one draw needn't show every extreme that they name: `counts`: occupied blocks fill the first slots of each slab's list; some slab has exactly 48. `neighbours`: entries are as the steps state; a slot that is not occupied has 144 in every entry; entries of the first slab never name the slab before it, those of the last never the slab after it.
All inputs are finite; a program needn't handle non-finite values.
Results may differ from a plain program's by a relative error of at most 0.003.
Values may be sent and summed in bfloat16 or wider, within the bound.
No kernel may reach another device: no remote copies, remote signals or barrier semaphores. Data moves between devices by JAX's collectives and lax.ppermute only.
A program may use at most 128 MiB of HBM per device.

v0:
```python
import jax
import jax.numpy as jnp
from jax import lax
from jax.sharding import PartitionSpec as P

GROUP_CH = 8


def extended_2(cells, sides, width):
    for axis, dim in sides:
        count = lax.axis_size(axis)
        ends = count - 1
        head = lax.slice_in_dim(cells, 0, width, axis=dim)
        tail = lax.slice_in_dim(cells, cells.shape[dim] - width, cells.shape[dim], axis=dim)
        cells = jnp.concatenate(
            [
                lax.ppermute(tail, axis, [(i, (i + 1) % count) for i in range(ends)]),
                cells,
                lax.ppermute(head, axis, [((i + 1) % count, i) for i in range(ends)]),
            ],
            axis=dim,
        )
    return cells


def windows(extended, index_rows):
    count = index_rows.shape[0]
    chans = extended.shape[2]
    blocks = jnp.take(extended, index_rows.reshape(-1), axis=0).reshape(
        count, 3, 3, 3, 4, 4, 4, chans
    )
    grid = blocks.transpose(0, 1, 4, 2, 5, 3, 6, 7).reshape(count, 12, 12, 12, chans)
    return grid[:, 3:9, 3:9, 3:9, :]


def block_terms(grid, act_rows, weight):
    chans = grid.shape[4]
    grads = jnp.zeros((act_rows.shape[0], weight.shape[1]), jnp.float32)
    pieces = []
    for offset in range(27):
        step_x = offset // 9 - 1
        step_y = offset // 3 % 3 - 1
        step_z = offset % 3 - 1
        window = grid[
            :, 1 - step_x : 5 - step_x, 1 - step_y : 5 - step_y, 1 - step_z : 5 - step_z, :
        ].reshape(-1, chans)
        grads = grads + lax.dot_general(
            window, weight[offset], (((1,), (1,)), ((), ())), preferred_element_type=jnp.float32
        )
        pieces.append(
            lax.dot_general(
                act_rows, window, (((0,), (0,)), ((), ())), preferred_element_type=jnp.float32
            )
        )
    return (grads, jnp.stack(pieces))


def body(features, cotangent, weight, gain, shift, counts, neighbours):
    slots = features.shape[0]
    width = features.shape[2]
    groups = width // GROUP_CH
    occupied = (jnp.arange(slots, dtype=jnp.int32) < counts[0]).astype(jnp.float32)[:, None, None]
    values = features.astype(jnp.float32)
    local_count = counts[0].astype(jnp.float32) * 64.0

    def group_sum(array):
        return array.reshape(slots, 64, groups, GROUP_CH).sum(axis=(0, 1, 3))

    def spread_out(vector):
        return jnp.repeat(vector, GROUP_CH)[None, None, :]

    total, number = lax.psum((group_sum(values * occupied), local_count), "slab")
    voxels = number * GROUP_CH
    mean = total / voxels
    centred = (values - spread_out(mean)) * occupied
    spread = lax.psum(group_sum(centred * centred), "slab")
    variance = spread / voxels
    rstd = lax.rsqrt(variance + 1e-05)
    normed = (values - spread_out(mean)) * spread_out(rstd)
    pre = normed * gain + shift
    act = (jax.nn.silu(pre) * occupied).astype(jnp.bfloat16)
    joined = lax.all_gather(cotangent, "ch", axis=2, tiled=True)
    beside_all = extended_2(joined, (("slab", 0),), slots)
    chans = beside_all.shape[2]
    extended = jnp.concatenate([beside_all, jnp.zeros((1, 64, chans), jnp.bfloat16)], axis=0)
    count_groups = slots // 8

    def step(carry, inputs):
        index_rows, act_rows = inputs
        grads, pieces = block_terms(windows(extended, index_rows), act_rows, weight)
        return (carry + pieces, grads)

    weight_term, grad_act = lax.scan(
        step,
        jnp.zeros((27, width, chans), jnp.float32),
        (neighbours.reshape(count_groups, 8, 27), act.reshape(count_groups, 8 * 64, width)),
    )
    grad_act = grad_act.reshape(slots, 64, width)
    sig = jax.nn.sigmoid(pre)
    grad_pre = occupied * grad_act * sig * (1.0 + pre * (1.0 - sig))
    grad_shift, grad_gain = lax.psum(
        (jnp.sum(grad_pre, axis=(0, 1)), jnp.sum(grad_pre * normed, axis=(0, 1))), "slab"
    )
    first = (gain * grad_shift).reshape(groups, GROUP_CH).sum(axis=1)
    second = (gain * grad_gain).reshape(groups, GROUP_CH).sum(axis=1)
    inner = gain * grad_pre - spread_out(first) / voxels - normed * spread_out(second) / voxels
    grad_features = (occupied * (cotangent.astype(jnp.float32) + spread_out(rstd) * inner)).astype(
        jnp.bfloat16
    )
    grad_weight = lax.psum(weight_term, "slab")
    return (grad_features, grad_weight, grad_gain, grad_shift)


def solution(mesh):
    in_specs = (
        P("slab", None, "ch"),
        P("slab", None, "ch"),
        P(None, "ch", None),
        P("ch"),
        P("ch"),
        P("slab"),
        P("slab", None),
    )
    out_specs = (P("slab", None, "ch"), P(None, "ch", None), P("ch"), P("ch"))
    return jax.shard_map(body, mesh=mesh, in_specs=in_specs, out_specs=out_specs, check_vma=False)
```

profile of v0, /device:TPU:2, one launch (start us, length us, event | category | flops | bytes accessed | tf_op | source)
XLA Modules:
  0.0 2200.4 jit_solution(11580857882089120880)
XLA Ops:
  8.0 19.8 all-gather.2.cloned.1.call-done
  27.8 4.8 collective-permute-start.1
  37.1 362.9 %all-reduce.1 = (f32[16]{0:T(128)S(1)}, f32[]{:T(128)}) all-reduce(f32[16]{0:T(128)S(1)} %reduce_sum.70, f32[]{:T(128)S(6)} %mul.105), channel_id=1, replica_groups=mesh['slab'=128,'ch'=2] {'slab'}, use_global_device_ids=true, to_apply=%region_2.0 | all-reduce | flops 17 | bytes 136 | tf_op jit(solution)/shard_map/psum | solution.py:72
  401.7 342.1 %psum.44 = f32[16]{0:T(128)S(1)} all-reduce(f32[16]{0:T(128)S(1)} %reduce_sum.73), channel_id=1, replica_groups=mesh['slab'=128,'ch'=2] {'slab'}, use_global_device_ids=true, to_apply=%region_6.7 | all-reduce | flops 16 | bytes 128 | tf_op jit(solution)/shard_map/psum | solution.py:76
  744.9 3.9 maximum_maximum_fusion
  748.8 1089.5 %while.13 = (s32[]{:T(128)}, f32[27,128,256]{2,1,0:T(8,128)}, f32[6,512,128]{2,1,0:T(8,128)}, bf16[6,512,128]{2,1,0:T(8,128)(2,1)S(1)}, s32[6,8,27]{2,1,0:T(8,12...) while((s32[]{:T(128)}, f32[27,128,256]{2,1,0:T(8,128)}, ...), condition=%wide.region_8.9_spmd.clone, body=%wide.region_7.8_spmd.clone.sunk | while | flops 1818954624 | bytes 199049936 | solution.py:93
  749.3 10.6 gather_fusion
  759.9 12.5 gather.13
  772.4 9.4 select_bitcast_fusion.2
  781.8 10.7 copy.75
  792.7 2.1 fusion.452
  829.4 2.0 convolution_add_fusion.59
  861.0 2.0 convolution_add_fusion.65
  931.1 10.5 gather_fusion
  941.7 12.5 gather.13
  954.2 9.4 select_bitcast_fusion.2
  963.6 10.7 copy.75
  974.5 2.1 fusion.452
  1011.2 2.0 convolution_add_fusion.59
  1042.8 2.0 convolution_add_fusion.65
  1112.9 10.2 gather_fusion
  1123.1 12.5 gather.13
  1135.6 9.4 select_bitcast_fusion.2
  1145.0 10.7 copy.75
  1155.9 2.1 fusion.452
  1192.7 2.0 convolution_add_fusion.59
  1224.2 2.0 convolution_add_fusion.65
  1294.3 10.2 gather_fusion
  1304.5 12.5 gather.13
  1317.0 9.4 select_bitcast_fusion.2
  1326.4 10.7 copy.75
  1337.3 2.1 fusion.452
  1374.1 2.0 convolution_add_fusion.59
  1475.8 10.2 gather_fusion
  1486.0 12.5 gather.13
  1498.5 9.4 select_bitcast_fusion.2
  1507.9 10.7 copy.75
  1518.8 2.1 fusion.452
  1555.5 2.0 convolution_add_fusion.59
  1657.2 10.2 gather_fusion
  1667.4 12.5 gather.13
  1679.9 9.4 select_bitcast_fusion.2
  1689.3 10.7 copy.75
  1700.2 2.1 fusion.452
  1736.9 2.0 convolution_add_fusion.59
  1839.4 2.4 fusion.137
  1841.8 345.2 %all-reduce = (f32[128]{0:T(128)S(1)}, f32[128]{0:T(128)S(1)}) all-reduce(f32[128]{0:T(128)S(1)} %get-tuple-element.69, f32[128]{0:T(128)S(1)} %get-tuple-element.68), channel_id=1, replica_groups=mesh['slab'=128,'ch'=2] {'slab'}, use_global_device_ids=true, to_apply=%region_13.14 | all-reduce | flops 256 | bytes 2048 | tf_op jit(solution)/shard_map/psum | solution.py:101
  2189.4 4.2 copy.141
  (1070 shorter events, 807.1 us)
Async XLA Ops:
  7.2 393.7 %copy-start.25 = (bf16[48,64,128]{2,1,0:T(8,128)(2,1)S(1)}, bf16[48,64,128]{2,1,0:T(8,128)(2,1)}, u32[]{:S(2)}) copy-start(bf16[48,64,128]{2,1,0:T(8,128)(2,1)} %param.9) | copy-start | bytes 2359300
  7.2 736.8 %copy-start.29 = (s32[48,27]{0,1:T(8,128)S(1)}, s32[48,27]{0,1:T(8,128)}, u32[]{:S(2)}) copy-start(s32[48,27]{0,1:T(8,128)} %param.15) | copy-start | bytes 15556
  7.2 737.0 %copy-start.34 = (f32[128]{0:T(128)S(1)}, f32[128]{0:T(128)}, u32[]{:S(2)}) copy-start(f32[128]{0:T(128)} %param.12) | copy-start | bytes 1540
  7.2 737.0 %copy-start.38 = (f32[128]{0:T(128)S(1)}, f32[128]{0:T(128)}, u32[]{:S(2)}) copy-start(f32[128]{0:T(128)} %param.13) | copy-start | bytes 1540
  7.2 20.6 all-gather.2.cloned.1.call-start
  7.9 2181.4 %all-reduce.4.cloned.1.call-start = ((), (), s32[]{:S(2)}) async-start(), calls=%async_computation.1 | async-start | bytes 7077888 | tf_op jit(solution)/shard_map/psum | solution.py:110
  27.8 717.0 %copy-start.28 = (bf16[48,64,256]{2,1,0:T(8,128)(2,1)S(1)}, bf16[48,64,256]{2,1,0:T(8,128)(2,1)}, u32[]{:S(2)}) copy-start(bf16[48,64,256]{2,1,0:T(8,128)(2,1)} %all-gather.2.cloned.1.call-done) | copy-start | bytes 4718596
  27.8 717.0 %collective-permute-start.1 = (bf16[48,64,256]{2,1,0:T(8,128)(2,1)}, bf16[48,64,256]{2,1,0:T(8,128)(2,1)}, u32[]{:S(2)}, u32[]{:S(2)}) collective-permute-start(bf16[48,64,256]{2,1,0:T(8,128)(2,1)} %all-gather.2.cloned.1.call-done), channel_id=1, source_target_pairs={{2,0},{4,2},{6,4},{8,6},{10,8},{12,10},{14,12},{16,14},{18,16},{20... | collective-permute-start | bytes 4718600 | tf_op jit(solution)/shard_map/ppermute | solution.py:19
  32.6 712.2 %collective-permute-start = (bf16[48,64,256]{2,1,0:T(8,128)(2,1)}, bf16[48,64,256]{2,1,0:T(8,128)(2,1)}, u32[]{:S(2)}, u32[]{:S(2)}) collective-permute-start(bf16[48,64,256]{2,1,0:T(8,128)(2,1)} %all-gather.2.cloned.1.call-done), channel_id=1, source_target_pairs={{0,2},{2,4},{4,6},{6,8},{8,10},{10,12},{12,14},{14,16},{16,18},{18... | collective-permute-start | bytes 4718600 | tf_op jit(solution)/shard_map/ppermute | solution.py:17
  35.2 713.5 %copy-start.30 = (f32[48]{0:T(128)}, f32[48]{0:T(128)S(1)}, u32[]{:S(2)}) copy-start(f32[48]{0:T(128)S(1)} %compare_convert_fusion) | copy-start | bytes 580
  400.9 347.9 %copy-start.32 = (f32[128]{0:T(128)}, f32[128]{0:T(128)S(1)}, u32[]{:S(2)}) copy-start(f32[128]{0:T(128)S(1)} %sub.28) | copy-start | bytes 1540
  829.4 11.0 copy-start.2
  845.2 11.0 copy-start.6
  861.0 11.0 copy-start.10
  876.8 11.0 copy-start.14
  892.6 11.0 copy-start.18
  908.4 7.5 copy-start.22
  1011.2 11.0 copy-start.2
  1027.0 11.0 copy-start.6
  1042.8 11.0 copy-start.10
  1058.6 11.0 copy-start.14
  1074.4 11.0 copy-start.18
  1090.2 7.5 copy-start.22
  1192.6 11.0 copy-start.2
  1208.4 11.0 copy-start.6
  1224.2 11.0 copy-start.10
  1240.0 11.0 copy-start.14
  1255.8 11.0 copy-start.18
  1271.6 7.5 copy-start.22
  1374.1 11.0 copy-start.2
  1389.9 11.0 copy-start.6
  1405.7 11.0 copy-start.10
  1421.5 11.0 copy-start.14
  1437.3 11.0 copy-start.18
  1453.0 7.5 copy-start.22
  1555.5 11.0 copy-start.2
  1571.3 11.0 copy-start.6
  1587.1 11.0 copy-start.10
  1602.9 11.0 copy-start.14
  1618.7 11.0 copy-start.18
  1634.4 7.5 copy-start.22
  1736.9 11.0 copy-start.2
  1752.7 11.0 copy-start.6
  1768.5 11.0 copy-start.10
  1784.3 11.0 copy-start.14
  1800.1 11.0 copy-start.18
  1815.9 7.5 copy-start.22
  1839.4 348.4 %copy-start.27 = (bf16[48,64,128]{2,1,0:T(8,128)(2,1)S(1)}, bf16[48,64,128]{2,1,0:T(8,128)(2,1)}, u32[]{:S(2)}) copy-start(bf16[48,64,128]{2,1,0:T(8,128)(2,1)} %param.10) | copy-start | bytes 2359300
  (123 other events, 223.1 us)
Sparse Core Ops, SparseCore 0:
  9.8 17.9 all-gather.1
  1838.4 241.8 all-reduce.3
where the time goes:
time: 2230 us; the launch traced here: 2200 us
  blocking collectives  1050 us (47%)
  local copies, waits for them, and re-layouts  675 us (30%)
  matrix products  353 us (16%)
  other arithmetic  75.1 us (3%)
    psum x1, blocking collectives, body(): lax.psum((group_sum(values * occupied), local_count), 'slab')  363 us
    psum x1, blocking collectives, body(): lax.psum((jnp.sum(grad_pre, axis=(0, 1)), jnp.sum(grad_pre * normed, axis...  345 us
    psum x1, blocking collectives, body(): spread = lax.psum(group_sum(centred * centred), 'slab')  342 us
    dot_general x162, matrix products, block_terms(): lax.dot_general(window, weight[offset], (((1,), (1,)), ((), ())), preferr...  315 us
    slice x174, local copies, waits for them, and re-layouts, block_terms(): grid[:, 1 - step_x:5 - step_x, 1 - step_y:5 - step_y, 1 - step_z:5 - step...  242 us
    reshape x162, local copies, waits for them, and re-layouts, block_terms(): window = grid[:, 1 - step_x:5 - step_x, 1 - step_y:5 - step_y, 1 - step_z...  210 us
    gather x12, local copies, waits for them, and re-layouts, windows(): jnp.take(extended, index_rows.reshape(-1), axis=0)  137 us
    transpose x6, local copies, waits for them, and re-layouts, windows(): blocks.transpose(0, 1, 4, 2, 5, 3, 6, 7).reshape(count, 12, 12, 12, chans)  64.3 us
  transfers between devices with their start and end apart: 4, of which 1 were waited for; matrix products, arithmetic and copies ran while one was open for 0% of the time, Pallas kernels for 0%

commit v1 on v0

v1 whole, which is shorter than its diff:
```python
import functools

import jax
import jax.numpy as jnp
from jax import lax
from jax.experimental import pallas as pl
from jax.experimental.pallas import tpu as pltpu
from jax.sharding import Mesh
from jax.sharding import PartitionSpec as P

GROUP_CH = 8
CUT = {128: (8, 4, 4), 8: (2, 2, 2), 4: (2, 2, 1)}
SLABS = ("z", "x", "y")
PLANE = ("x", "y")
F32 = jnp.float32
BF16 = jnp.bfloat16
VMEM = pl.BlockSpec(memory_space=pltpu.VMEM)
SMEM = pl.BlockSpec(memory_space=pltpu.SMEM)
ANY = pl.BlockSpec(memory_space=pl.ANY)


def call(kernel, out_shape, in_specs, scratch=(), flops=0, bytes_accessed=0):
    several = isinstance(out_shape, (list, tuple))
    return pl.pallas_call(
        kernel,
        out_shape=out_shape,
        in_specs=in_specs,
        out_specs=[VMEM] * len(out_shape) if several else VMEM,
        scratch_shapes=list(scratch),
        compiler_params=pltpu.CompilerParams(vmem_limit_bytes=48 * 1024 * 1024),
        cost_estimate=pl.CostEstimate(
            flops=flops, bytes_accessed=bytes_accessed, transcendentals=0
        ),
    )


def exact_dot(left, right):
    return jnp.dot(left, right, precision=lax.Precision.HIGHEST, preferred_element_type=F32)


def iota(shape, dim):
    return lax.broadcasted_iota(jnp.int32, shape, dim)


def turned(rows_ref, out_ref):
    slots = out_ref.shape[1]
    for voxel in range(64):
        out_ref[voxel] = rows_ref[pl.ds(voxel, slots, stride=64), :].astype(out_ref.dtype)


def turn_kernel(in_ref, out_ref, low_ref, high_ref, rows_ref):
    rows_ref[...] = in_ref[...].astype(F32)
    turned(rows_ref, out_ref)
    low_ref[...] = out_ref[0:16]
    high_ref[...] = out_ref[48:64]


def sums_kernel(counts_ref, in_ref, out_ref, sent_ref, rows_ref):
    slots = out_ref.shape[1]
    count = counts_ref[0]
    rows_ref[...] = in_ref[...].astype(F32)

    def over_slots(term):
        total = jnp.zeros((8, 128), F32)
        for slot in range(slots):
            rows = term(rows_ref[slot * 64 : slot * 64 + 64, :]).reshape(8, 8, 128).sum(axis=0)
            total = total + jnp.where(slot < count, rows, 0.0)
        return jnp.broadcast_to(jnp.sum(total, axis=0, keepdims=True), (8, 128))

    lane_in, lane_out = iota((128, 128), 0), iota((128, 128), 1)
    same = (lane_in // GROUP_CH == lane_out // GROUP_CH).astype(F32)
    to_sum = (lane_in // GROUP_CH == lane_out).astype(F32)
    to_square = (lane_in // GROUP_CH + 16 == lane_out).astype(F32)
    total = over_slots(lambda rows: rows)
    entries = count.astype(F32) * (64.0 * GROUP_CH)
    mean = (exact_dot(total, same) / entries)[0:1]

    def centred(rows):
        apart = rows - mean
        return apart * apart

    squares = over_slots(centred)
    row = exact_dot(total, to_sum) + exact_dot(squares, to_square)
    row = row + jnp.where(iota((8, 128), 1) == 32, count.astype(F32), 0.0)
    sent_ref[...] = jnp.broadcast_to(row[0:1].reshape(1, 1, 128), sent_ref.shape)
    turned(rows_ref, out_ref)


def halo_kernel(
    core_ref,
    near_ref,
    own_ref,
    own_other_ref,
    before_ref,
    before_other_ref,
    after_ref,
    after_other_ref,
    grid_ref,
    low_ref,
    high_ref,
    pick_ref,
    sems,
):
    slots = near_ref.shape[0]
    core = core_ref[0]
    mine = pl.ds(pl.multiple_of(core * 128, 128), 128)
    other = pl.ds(pl.multiple_of((1 - core) * 128, 128), 128)
    centre = grid_ref.at[1:5, 1:5, 1:5]
    copies = [
        pltpu.make_async_copy(own_ref, centre.at[:, :, :, :, mine], sems.at[0]),
        pltpu.make_async_copy(own_other_ref, centre.at[:, :, :, :, other], sems.at[1]),
        pltpu.make_async_copy(before_ref, low_ref.at[:, :, :, mine], sems.at[2]),
        pltpu.make_async_copy(before_other_ref, low_ref.at[:, :, :, other], sems.at[3]),
        pltpu.make_async_copy(after_ref, high_ref.at[:, :, :, mine], sems.at[4]),
        pltpu.make_async_copy(after_other_ref, high_ref.at[:, :, :, other], sems.at[5]),
    ]
    for copy in copies:
        copy.start()
    near = near_ref[...]
    columns = iota((slots, 3 * slots), 1)
    for offset in range(27):
        pick_ref[offset] = (near[:, offset : offset + 1] == columns).astype(F32)
    for copy in copies:
        copy.wait()

    def side(at):
        return -1 if at == 0 else (1 if at == 5 else 0)

    def source(at):
        return {0: 4, 5: 1}.get(at, at)

    places = [(a, b, c) for a in range(6) for b in range(6) for c in range(6)]
    for a, b, c in places:
        dx, dy, dz = side(a), side(b), side(c)
        if (dx, dy, dz) == (0, 0, 0):
            continue
        offset = 9 * (dx + 1) + 3 * (dy + 1) + dz + 1
        inside = grid_ref[source(a), source(b), source(c)]
        if dx == 0:
            pick = pick_ref[offset, :, slots : 2 * slots]
            table = inside
        elif dx < 0:
            pick = pick_ref[offset, :, 0 : 2 * slots]
            table = jnp.concatenate([low_ref[source(b) - 1, source(c) - 1], inside], axis=0)
        else:
            pick = pick_ref[offset, :, slots : 3 * slots]
            table = jnp.concatenate([inside, high_ref[source(b) - 1, source(c) - 1]], axis=0)
        grid_ref[a, b, c] = jnp.dot(pick.astype(BF16), table, preferred_element_type=F32).astype(
            BF16
        )


def window(grid_ref, plane, turn):
    slots = grid_ref.shape[3]
    block = grid_ref[plane, pl.ds(2 - turn // 3, 4), pl.ds(2 - turn % 3, 4)]
    return block.reshape(16 * slots, 256)


def planes_of(plane):
    return max(0, plane - 2), min(3, plane) + 1


def weight_grad_kernel(
    counts_ref,
    table_ref,
    gain_ref,
    shift_ref,
    values_ref,
    grid_hbm,
    out_ref,
    norm_ref,
    grid_ref,
    act_ref,
    total_ref,
    sem,
):
    slots = values_ref.shape[1]
    copy = pltpu.make_async_copy(grid_hbm, grid_ref, sem)
    copy.start()
    table = table_ref[...]
    held = jnp.sum(table, axis=0)
    voxels = held[:, 32:33] * (64.0 * GROUP_CH)
    entries = table[:, :, 32:33] * (64.0 * GROUP_CH)
    mean = held / voxels
    apart = table / entries - mean.reshape(1, 1, 128)
    between = jnp.sum(apart * apart * entries, axis=0)
    lane_in, lane_out = iota((128, 128), 0), iota((128, 128), 1)
    from_sum = (lane_in == lane_out // GROUP_CH).astype(F32)
    from_square = (lane_in == lane_out // GROUP_CH + 16).astype(F32)

    def spread(row, matrix):
        return exact_dot(jnp.broadcast_to(row, (8, 128)), matrix)[0:1]

    mean = spread(mean, from_sum)
    variance = (spread(between, from_sum) + spread(held, from_square)) / voxels
    rstd = lax.rsqrt(variance + 1e-05)
    norm_ref[0:1, :] = mean
    norm_ref[1:2, :] = rstd
    norm_ref[2:3, :] = jnp.broadcast_to(voxels, (1, 128))
    norm_ref[3:8, :] = jnp.zeros((5, 128), F32)
    gain, shift = gain_ref[...], shift_ref[...]
    live = iota((slots, 128), 0) < counts_ref[0]
    for plane in range(4):
        pieces = []
        for voxel in range(plane * 16, plane * 16 + 16):
            normed = (values_ref[voxel].astype(F32) - mean) * rstd
            pre = normed * gain + shift
            pieces.append(jnp.where(live, pre / (1.0 + jnp.exp(-pre)), 0.0))
        rows = jnp.concatenate(pieces, axis=0)
        act_ref[plane * 128 : plane * 128 + 128, :] = rows.T.astype(BF16)
    copy.wait()

    @pl.loop(0, 9)
    def _(turn):
        for plane in range(6):
            first, last = planes_of(plane)
            part = jnp.dot(
                act_ref[first * 128 : last * 128, :],
                window(grid_ref, plane, turn),
                preferred_element_type=F32,
            )
            for at in range(first, last):
                step = at - plane + 2
                term = part[(at - first) * 128 : (at - first) * 128 + 128]
                if at == 0:
                    total_ref[step] = term
                else:
                    total_ref[step] += term
        for step in range(3):
            out_ref[step, turn] = total_ref[step].astype(BF16)


def act_grad_kernel(
    counts_ref,
    norm_ref,
    gain_ref,
    shift_ref,
    values_ref,
    weight_ref,
    grid_ref,
    out_ref,
    sums_ref,
    total_ref,
):
    slots = values_ref.shape[1]
    total_ref[...] = jnp.zeros_like(total_ref)

    @pl.loop(0, 9)
    def _(turn):
        for plane in range(6):
            first, last = planes_of(plane)
            low, high = first - plane + 2, last - plane + 2
            part = lax.dot_general(
                window(grid_ref, plane, turn),
                weight_ref[low:high, turn].reshape((high - low) * 128, 256),
                (((1,), (1,)), ((), ())),
                preferred_element_type=F32,
            )
            for at in range(first, last):
                term = part[:, (at - first) * 128 : (at - first) * 128 + 128]
                total_ref[at] += term.reshape(16, slots, 128)

    mean, rstd = norm_ref[0:1, :], norm_ref[1:2, :]
    gain, shift = gain_ref[...], shift_ref[...]
    live = iota((slots, 128), 0) < counts_ref[0]
    shift_sum = jnp.zeros((8, 128), F32)
    gain_sum = jnp.zeros((8, 128), F32)
    for voxel in range(64):
        normed = (values_ref[voxel].astype(F32) - mean) * rstd
        pre = normed * gain + shift
        sig = 1.0 / (1.0 + jnp.exp(-pre))
        grad = total_ref[voxel // 16, voxel % 16] * sig * (1.0 + pre * (1.0 - sig))
        grad = jnp.where(live, grad, 0.0)
        out_ref[voxel] = grad
        shift_sum = shift_sum + grad.reshape(slots // 8, 8, 128).sum(axis=0)
        gain_sum = gain_sum + (grad * normed).reshape(slots // 8, 8, 128).sum(axis=0)
    sums_ref[:, 0:128] = jnp.sum(shift_sum, axis=0, keepdims=True)
    sums_ref[:, 128:256] = jnp.sum(gain_sum, axis=0, keepdims=True)


def last_kernel(
    counts_ref, norm_ref, gain_ref, sums_ref, values_ref, cotangent_ref, grad_ref, out_ref
):
    slots = grad_ref.shape[0] // 64
    mean, rstd, voxels = norm_ref[0:1, :], norm_ref[1:2, :], norm_ref[2:3, :]
    gain = gain_ref[...]
    lane_in, lane_out = iota((128, 128), 0), iota((128, 128), 1)
    same = (lane_in // GROUP_CH == lane_out // GROUP_CH).astype(F32)

    def grouped(row):
        return exact_dot(jnp.broadcast_to(row, (8, 128)), same)[0:1]

    first = grouped(gain * sums_ref[:, 0:128]) / voxels
    second = grouped(gain * sums_ref[:, 128:256]) / voxels
    for slot in range(slots):
        rows = slice(slot * 64, slot * 64 + 64)
        normed = (values_ref[rows, :].astype(F32) - mean) * rstd
        grad = grad_ref[pl.ds(slot, 64, stride=slots), :]
        inner = gain * grad - first - normed * second
        result = cotangent_ref[rows, :].astype(F32) + rstd * inner
        out_ref[rows, :] = jnp.where(slot < counts_ref[0], result, 0.0).astype(BF16)


def body(features, cotangent, weight, gain, shift, counts, neighbours):
    slots, voxels, width = features.shape
    rows = slots * voxels
    n_plane = lax.axis_size("x") * lax.axis_size("y")
    n_line = lax.axis_size("z")
    n_slab = n_plane * n_line
    core = lax.axis_index("ch").astype(jnp.int32).reshape(1)
    swap = [(0, 1), (1, 0)]
    turned_shape = jax.ShapeDtypeStruct((voxels, slots, width), BF16)
    face_shape = jax.ShapeDtypeStruct((16, slots, width), BF16)
    rows_scratch = pltpu.VMEM((rows, width), F32)
    gain_row, shift_row = gain.reshape(1, width), shift.reshape(1, width)

    own, low, high = call(
        turn_kernel, [turned_shape, face_shape, face_shape], [VMEM], [rows_scratch]
    )(cotangent.reshape(rows, width))
    before = lax.ppermute(high, SLABS, [(i, i + 1) for i in range(n_slab - 1)])
    after = lax.ppermute(low, SLABS, [(i + 1, i) for i in range(n_slab - 1)])
    own_other = lax.ppermute(own, "ch", swap)
    values, sent = call(
        sums_kernel,
        [turned_shape, jax.ShapeDtypeStruct((n_slab, 1, 128), F32)],
        [SMEM, VMEM],
        [rows_scratch],
    )(counts, features.reshape(rows, width))
    table = lax.all_to_all(sent, SLABS, 0, 0, tiled=True)
    before_other = lax.ppermute(before, "ch", swap)
    after_other = lax.ppermute(after, "ch", swap)

    cube = (4, 4, 4, slots, width)
    face = (4, 4, slots, width)
    grid_shape = (6, 6, 6, slots, 2 * width)
    grid = call(
        halo_kernel,
        jax.ShapeDtypeStruct(grid_shape, BF16),
        [SMEM, VMEM] + [ANY] * 6,
        [
            pltpu.VMEM((4, 4, slots, 2 * width), BF16),
            pltpu.VMEM((4, 4, slots, 2 * width), BF16),
            pltpu.VMEM((27, slots, 3 * slots), F32),
            pltpu.SemaphoreType.DMA((6,)),
        ],
        flops=10**9,
    )(
        core,
        neighbours,
        own.reshape(cube),
        own_other.reshape(cube),
        before.reshape(face),
        before_other.reshape(face),
        after.reshape(face),
        after_other.reshape(face),
    )

    weight_term, norm = call(
        weight_grad_kernel,
        [
            jax.ShapeDtypeStruct((3, 9, width, 2 * width), BF16),
            jax.ShapeDtypeStruct((8, 128), F32),
        ],
        [SMEM, VMEM, VMEM, VMEM, VMEM, ANY],
        [
            pltpu.VMEM(grid_shape, BF16),
            pltpu.VMEM((4 * width, 16 * slots), BF16),
            pltpu.VMEM((3, width, 2 * width), F32),
            pltpu.SemaphoreType.DMA,
        ],
        flops=2 * rows * 27 * width * 2 * width,
    )(counts, table, gain_row, shift_row, values, grid)
    piece = 27 * width // n_plane
    parts = lax.all_to_all(
        weight_term.reshape(n_plane, piece, 2 * width), PLANE, 0, 0, tiled=True
    )

    grad_pre, sums = call(
        act_grad_kernel,
        [
            jax.ShapeDtypeStruct((voxels, slots, width), F32),
            jax.ShapeDtypeStruct((1, 2 * width), F32),
        ],
        [SMEM] + [VMEM] * 6,
        [pltpu.VMEM((4, 16, slots, width), F32)],
        flops=2 * rows * 27 * width * 2 * width,
    )(
        counts,
        norm,
        gain_row,
        shift_row,
        values,
        weight.reshape(3, 9, width, 2 * width),
        grid,
    )

    part = jnp.sum(parts.astype(F32), axis=0).reshape(n_line, piece // n_line, 2 * width)
    part = jnp.concatenate(
        [part, jnp.broadcast_to(sums.reshape(1, 1, 2 * width), (n_line, 1, 2 * width))], axis=1
    )
    part = jnp.sum(lax.all_to_all(part, "z", 0, 0, tiled=True), axis=0)
    final, line_sums = part[:-1].astype(BF16), part[-1:]
    line = jnp.broadcast_to(final[None], (n_line,) + final.shape)
    line = lax.all_to_all(line, "z", 0, 0, tiled=True).reshape(piece, 2 * width)
    split = []
    rest = line_sums
    for _ in range(3):
        top = lax.reduce_precision(rest, 8, 7)
        split.append(top.astype(BF16))
        rest = rest - top
    line = jnp.concatenate([line] + split + [jnp.zeros((5, 2 * width), BF16)], axis=0)
    plane = jnp.broadcast_to(line[None], (n_plane,) + line.shape)
    plane = lax.all_to_all(plane, PLANE, 0, 0, tiled=True)
    grad_weight = plane[:, :piece].astype(F32).reshape(27, width, 2 * width)
    totals = jnp.sum(plane[:, piece : piece + 3].astype(F32), axis=(0, 1)).reshape(1, 2 * width)

    grad_features = call(
        last_kernel,
        jax.ShapeDtypeStruct((rows, width), BF16),
        [SMEM] + [VMEM] * 6,
    )(
        counts,
        norm,
        gain_row,
        totals,
        features.reshape(rows, width),
        cotangent.reshape(rows, width),
        grad_pre.reshape(rows, width),
    )
    return (
        grad_features.reshape(features.shape),
        grad_weight,
        totals[0, width:],
        totals[0, :width],
    )


def solution(mesh):
    slabs = mesh.devices.shape[0]
    inner = Mesh(mesh.devices.reshape(CUT[slabs] + (2,)), SLABS + ("ch",))
    in_specs = (
        P(SLABS, None, "ch"),
        P(SLABS, None, "ch"),
        P(None, "ch", None),
        P("ch"),
        P("ch"),
        P(SLABS),
        P(SLABS, None),
    )
    out_specs = (P(SLABS, None, "ch"), P(None, "ch", None), P("ch"), P("ch"))
    return jax.shard_map(body, mesh=inner, in_specs=in_specs, out_specs=out_specs, check_vma=False)
```

time: 2230 us -> 150 us (0.07); the launches traced: 2200 us -> 150 us
  blocking collectives: 1050 us -> 39.1 us
  local copies, waits for them, and re-layouts: 675 us -> 6.15 us
  matrix products: 353 us -> 0 us
  other arithmetic: 75.1 us -> 4.05 us
  Pallas kernels: 0 us -> 34.5 us
  starting transfers between devices: 6.76 us -> 31.3 us
    psum x3 -> x0, blocking collectives: 1050 us -> none  [the longest x1 363 us: body(): lax.psum((group_sum(values * occupied), local_count), 'slab')]
    dot_general x324 -> x0, matrix products: 353 us -> none  [the longest x162 315 us: block_terms(): lax.dot_general(window, weight[offset], (((1,), (1,)), ((), ())), preferr...]
    slice x174 -> x2, local copies, waits for them, and re-layouts: 242 us -> 0.12 us  [the longest x1 0.12 us: body(): grad_weight = plane[:, :piece].astype(F32).reshape(27, width, 2 * width)]
    reshape x176 -> x2, local copies, waits for them, and re-layouts: 211 us -> 0.08 us  [the longest x1 0.05 us: body(): line = lax.all_to_all(line, 'z', 0, 0, tiled=True).reshape(piece, 2 * width)]
    gather x12 -> x0, local copies, waits for them, and re-layouts: 137 us -> none  [windows(): jnp.take(extended, index_rows.reshape(-1), axis=0)]
    transpose x6 -> x0, local copies, waits for them, and re-layouts: 64.3 us -> none  [windows(): blocks.transpose(0, 1, 4, 2, 5, 3, 6, 7).reshape(count, 12, 12, 12, chans)]
    transpose x6 -> x0, other arithmetic: 56.4 us -> none  [windows(): blocks.transpose(0, 1, 4, 2, 5, 3, 6, 7).reshape(count, 12, 12, 12, chans)]
    all_to_all x0 -> x2, blocking collectives: none -> 39.1 us  [the longest x1 25.8 us: body(): plane = lax.all_to_all(plane, PLANE, 0, 0, tiled=True)]
  transfers between devices with their start and end apart: 4 -> 8, of which waited for: 1 -> 5; matrix products, arithmetic and copies ran while one was open for 0% -> 1% of each run, Pallas kernels for 0% -> 13%
where the time goes in v1:
time: 150 us
  blocking collectives  39.1 us (26%)
  Pallas kernels  34.5 us (23%)
  waiting for transfers between devices  33.1 us (22%)
  starting transfers between devices  31.3 us (21%)
  local copies, waits for them, and re-layouts  6.15 us (4%)
  other arithmetic  4.05 us (3%)
  between operations  1.5 us (1%)
    all_to_all x1, blocking collectives, body(): plane = lax.all_to_all(plane, PLANE, 0, 0, tiled=True)  25.8 us
    all_to_all x1, starting transfers between devices, body(): table = lax.all_to_all(sent, SLABS, 0, 0, tiled=True)  15.4 us
    all_to_all x1, blocking collectives, body(): part = jnp.sum(lax.all_to_all(part, 'z', 0, 0, tiled=True), axis=0)  13.3 us
    pallas_call x1, Pallas kernels, body(): call(act_grad_kernel, [jax.ShapeDtypeStruct((voxels, slots, width), F32),...  12.9 us
    pallas_call x1, Pallas kernels, body(): call(weight_grad_kernel, [jax.ShapeDtypeStruct((3, 9, width, 2 * width),...  12.2 us
    all_to_all x1, waiting for transfers between devices, body(): line = lax.all_to_all(line, 'z', 0, 0, tiled=True).reshape(piece, 2 * width)  8.98 us
    all_to_all x1, waiting for transfers between devices, body(): lax.all_to_all(weight_term.reshape(n_plane, piece, 2 * width), PLANE, 0,...  8.84 us
    ppermute x1, waiting for transfers between devices, body(): before = lax.ppermute(high, SLABS, [(i, i + 1) for i in range(n_slab - 1)])  6.22 us
  transfers between devices with their start and end apart: 8, of which 5 were waited for; matrix products, arithmetic and copies ran while one was open for 1% of the time, Pallas kernels for 13%

profile of v1, /device:TPU:2, one launch (start us, length us, event | category | flops | bytes accessed | tf_op | source)
XLA Modules:
  0.0 149.7 jit_solution(3748714455856063158)
XLA Ops:
  0.6 0.0 copy-start
  0.6 1.1 copy-done
  1.8 1.0 shard_map.103
  2.7 0.1 collective-permute-start
  2.8 4.9 %collective-permute-start.3 = (bf16[16,48,128]{2,1,0:T(8,128)(2,1)S(1)}, bf16[16,48,128]{2,1,0:T(8,128)(2,1)S(1)}, u32[]{:S(2)}, u32[]{:S(2)}) collective-permute-start(bf16[16,48,128]{2,1,0:T(8,128)(2,1)S(1)} %get-tuple-element.17), channel_id=1, source_target_pairs={{2,0},{4,2},{6,4},{8,6},{10,8},{12,10},{14,12},{16,14},{18,16},{20... | collective-permute-start | bytes 589832 | tf_op jit(solution)/shard_map/ppermute | solution.py:321
  7.8 1.9 %collective-permute-start.1 = (bf16[16,48,128]{2,1,0:T(8,128)(2,1)S(1)}, bf16[16,48,128]{2,1,0:T(8,128)(2,1)S(1)}, u32[]{:S(2)}, u32[]{:S(2)}) collective-permute-start(bf16[16,48,128]{2,1,0:T(8,128)(2,1)S(1)} %get-tuple-element.16), channel_id=1, source_target_pairs={{0,2},{2,4},{4,6},{6,8},{8,10},{10,12},{12,14},{14,16},{16,18},{18... | collective-permute-start | bytes 589832 | tf_op jit(solution)/shard_map/ppermute | solution.py:320
  9.7 2.9 %collective-permute-done.3 = bf16[16,48,128]{2,1,0:T(8,128)(2,1)S(1)} collective-permute-done((bf16[16,48,128]{2,1,0:T(8,128)(2,1)S(1)}, bf16[16,48,128]{2,1,0:T(8,128)(2,1)S(1)}, u32[]{:S(2)}, u32[]{:S(2)}) %collective-permute-start.3) | collective-permute-done | bytes 196640 | tf_op jit(solution)/shard_map/ppermute | solution.py:321
  12.5 0.0 collective-permute-start.4
  12.5 6.2 %collective-permute-done.1 = bf16[16,48,128]{2,1,0:T(8,128)(2,1)S(1)} collective-permute-done((bf16[16,48,128]{2,1,0:T(8,128)(2,1)S(1)}, bf16[16,48,128]{2,1,0:T(8,128)(2,1)S(1)}, u32[]{:S(2)}, u32[]{:S(2)}) %collective-permute-start.1) | collective-permute-done | bytes 196640 | tf_op jit(solution)/shard_map/ppermute | solution.py:320
  18.8 0.0 collective-permute-start.2
  19.4 0.0 copy-start.2
  19.4 1.1 copy-done.2
  20.6 2.4 %shard_map.102 = (bf16[64,48,128]{2,1,0:T(8,128)(2,1)S(1)}, f32[128,1,128]{2,1,0:T(1,128)}) custom-call(s32[1]{0:T(128)S(6)} %copy.13.counts_ref, bf16[3072,128]{1,0:T(8,128)(2,1)S(1)} %bitcast.25), custom_call_target="tpu_custom_call" | custom-call | tf_op jit(solution)/shard_map/pallas_call | solution.py:323
  22.9 15.4 %all-to-all-start = ((f32[128,1,128]{2,1,0:T(1,128)}), f32[128,1,128]{2,1,0:T(1,128)S(1)}, u32[]{:S(2)}, u32[]{:S(2)}) async-start(f32[128,1,128]{2,1,0:T(1,128)} %get-tuple-element.13), calls=%async_computation | async-start | bytes 131072 | tf_op jit(solution)/shard_map/all_to_all | solution.py:329
  38.3 0.8 copy.12.near_ref
  39.1 0.0 collective-permute-done.4
  39.1 0.0 collective-permute-done.2
  39.2 0.0 collective-permute-done
  39.2 0.0 copy-start.4
  39.2 0.0 copy-start.6
  39.2 4.2 %shard_map.104.grid_hbm.grid_ref = bf16[6,6,6,48,256]{4,3,2,1,0:T(8,128)(2,1)} custom-call(s32[1]{0:T(128)} %bitcast.3.core_ref, s32[48,27]{1,0:T(8,128)S(1)} %copy.12.near_ref, bf16[4,4,4,48,128]{4,3,2,1,0:T(8,128)(2,1)S(1)} %bitcast.28, bf16[4,4,4,48,128]{4,3,2,1,0:T(8,128)(2,1)S(1)} %bitcast.29, bf16[4,4,48,128]{3,2,1,0:T(8,128)(2,1)S(1)} %bitcast.31, ...), custom_call_target="tpu_custom_call" | custom-call | flops 1000000000 | tf_op jit(solution)/shard_map/pallas_call | solution.py:336
  43.4 6.2 %all-to-all-done.table_ref = f32[128,1,128]{2,1,0:T(1,128)S(1)} async-done(((f32[128,1,128]{2,1,0:T(1,128)}), f32[128,1,128]{2,1,0:T(1,128)S(1)}, u32[]{:S(2)}, u32[]{:S(2)}) %all-to-all-start) | async-done | bytes 65568 | tf_op jit(solution)/shard_map/all_to_all | solution.py:329
  49.6 0.0 copy-done.4
  49.6 0.0 copy-done.6
  49.6 12.2 %shard_map.105 = (bf16[3,9,128,256]{3,2,1,0:T(8,128)(2,1)}, f32[8,128]{1,0:T(8,128)S(1)}) custom-call(s32[1]{0:T(128)S(6)} %copy.13.counts_ref, f32[128,1,128]{2,1,0:T(1,128)S(1)} %all-to-all-done.table_ref, f32[1,128]{1,0:T(1,128)S(1)} %bitcast.37, f32[1,128]{1,0:T(1,128)S(1)} %bitcast.41, bf16[64,48,128]{2,1,0:T(8,128)(2,1)S(1)} %get-tuple-element.14.values_ref, ...), custom_call_target="tpu_custom_call" | custom-call | flops 5435817984 | tf_op jit(solution)/shard_map/pallas_call | solution.py:358
  61.8 5.6 %all-to-all-start.1 = ((bf16[16,216,256]{2,1,0:T(8,128)(2,1)}), bf16[16,216,256]{2,1,0:T(8,128)(2,1)}, u32[]{:S(2)}, u32[]{:S(2)}) async-start(bf16[16,216,256]{2,1,0:T(8,128)(2,1)} %bitcast.11), calls=%async_computation.1 | async-start | bytes 3538944 | tf_op jit(solution)/shard_map/all_to_all | solution.py:374
  67.5 0.0 copy-start.5
  67.5 1.5 copy-done.5
  68.9 12.9 %shard_map.106 = (f32[64,48,128]{2,1,0:T(8,128)S(1)}, f32[1,256]{1,0:T(1,128)S(1)}) custom-call(s32[1]{0:T(128)S(6)} %copy.13.counts_ref, f32[8,128]{1,0:T(8,128)S(1)} %get-tuple-element.18.norm_ref, f32[1,128]{1,0:T(1,128)S(1)} %bitcast.38, f32[1,128]{1,0:T(1,128)S(1)} %bitcast.42, bf16[64,48,128]{2,1,0:T(8,128)(2,1)S(1)} %get-tuple-element.14.values_ref, ...), custom_call_target="tpu_custom_call" | custom-call | flops 5435817984 | tf_op jit(solution)/shard_map/pallas_call | solution.py:378
  81.8 8.8 %all-to-all-done.1 = bf16[16,216,256]{2,1,0:T(8,128)(2,1)} async-done(((bf16[16,216,256]{2,1,0:T(8,128)(2,1)}), bf16[16,216,256]{2,1,0:T(8,128)(2,1)}, u32[]{:S(2)}, u32[]{:S(2)}) %all-to-all-start.1) | async-done | bytes 1769504 | tf_op jit(solution)/shard_map/all_to_all | solution.py:374
  90.6 1.7 %convert_reduce_fusion = f32[216,256]{1,0:T(8,128)S(1)} fusion(bf16[16,216,256]{2,1,0:T(8,128)(2,1)} %all-to-all-done.1), kind=kLoop, calls=%fused_computation | loop fusion | flops 1714176 | bytes 1990656 | tf_op jit(solution)/shard_map/reduce_sum | solution.py:397
  92.5 13.3 %all_to_all.25 = f32[8,28,256]{2,1,0:T(8,128)S(1)} all-to-all(f32[8,28,256]{2,1,0:T(8,128)S(1)} %pad_maximum_fusion), channel_id=1, replica_groups=mesh['z'=8,'x'=4,'y'=4,'ch'=2] {'z'}, dimensions={0} | all-to-all | bytes 458752 | tf_op jit(solution)/shard_map/all_to_all | solution.py:401
  105.8 0.7 broadcast_in_dim.24
  106.5 3.4 %all-to-all-start.3 = ((bf16[8,27,256]{2,1,0:T(8,128)(2,1)}), bf16[8,27,256]{2,1,0:T(8,128)(2,1)S(1)}, u32[]{:S(2)}, u32[]{:S(2)}) async-start(bf16[8,27,256]{2,1,0:T(8,128)(2,1)} %broadcast_in_dim.24), calls=%async_computation.3 | async-start | bytes 262144 | tf_op jit(solution)/shard_map/all_to_all | solution.py:404
  109.9 9.0 %all-to-all-done.3 = bf16[8,27,256]{2,1,0:T(8,128)(2,1)S(1)} async-done(((bf16[8,27,256]{2,1,0:T(8,128)(2,1)}), bf16[8,27,256]{2,1,0:T(8,128)(2,1)S(1)}, u32[]{:S(2)}, u32[]{:S(2)}) %all-to-all-start.3) | async-done | bytes 110624 | tf_op jit(solution)/shard_map/all_to_all | solution.py:404
  118.8 0.1 reshape.90
  118.9 0.2 broadcast_in_dim.26
  119.1 25.8 %all_to_all.26 = bf16[16,224,256]{2,1,0:T(8,128)(2,1)S(1)} all-to-all(bf16[16,224,256]{2,1,0:T(8,128)(2,1)S(1)} %broadcast_in_dim.26), channel_id=1, replica_groups=mesh['z'=8,'x'=4,'y'=4,'ch'=2] {'x','y'}, dimensions={0} | all-to-all | bytes 3670016 | tf_op jit(solution)/shard_map/all_to_all | solution.py:413
  144.9 0.1 slice.28
  145.1 0.0 copy-start.1
  145.1 0.0 copy-start.3
  145.1 2.2 %convert.5 = f32[27,128,256]{2,1,0:T(8,128)} convert(bf16[27,128,256]{2,1,0:T(8,128)(2,1)S(1)} %bitcast.43) | non-fusion elementwise | flops 884736 | bytes 5308416 | tf_op jit(solution)/shard_map/reshape | solution.py:414
  147.4 0.5 slice_bitcast_fusion
  147.9 0.0 copy-done.1
  147.9 0.0 copy-done.3
  147.9 1.9 %shard_map.107 = bf16[3072,128]{1,0:T(8,128)(2,1)} custom-call(s32[1]{0:T(128)S(6)} %copy.13.counts_ref, f32[8,128]{1,0:T(8,128)S(1)} %get-tuple-element.18.norm_ref, f32[1,128]{1,0:T(1,128)S(1)} %bitcast.39, f32[1,256]{1,0:T(1,128)S(1)} %bitcast.35, bf16[3072,128]{1,0:T(8,128)(2,1)S(1)} %bitcast.26, bf16[3072,128]{1,0:T(8,128)(2,1)S(1)} %bitcast.24, ...), custom_call_target="tpu_custom_call" | custom-call | tf_op jit(solution)/shard_map/pallas_call | solution.py:417
  (9 shorter events, 0.2 us)
Async XLA Ops:
  0.6 1.1 copy-start
  2.7 36.4 %collective-permute-start = (bf16[64,48,128]{2,1,0:T(8,128)(2,1)S(1)}, bf16[64,48,128]{2,1,0:T(8,128)(2,1)S(1)}, u32[]{:S(2)}, u32[]{:S(2)}) collective-permute-start(bf16[64,48,128]{2,1,0:T(8,128)(2,1)S(1)} %get-tuple-element.15), channel_id=1, source_target_pairs={{0,1},{1,0},{2,3},{3,2},{4,5},{5,4},{6,7},{7,6},{8,9},{9,8},{10,11... | collective-permute-start | bytes 2359304 | tf_op jit(solution)/shard_map/ppermute | solution.py:322
  2.8 9.7 %collective-permute-start.3 = (bf16[16,48,128]{2,1,0:T(8,128)(2,1)S(1)}, bf16[16,48,128]{2,1,0:T(8,128)(2,1)S(1)}, u32[]{:S(2)}, u32[]{:S(2)}) collective-permute-start(bf16[16,48,128]{2,1,0:T(8,128)(2,1)S(1)} %get-tuple-element.17), channel_id=1, source_target_pairs={{2,0},{4,2},{6,4},{8,6},{10,8},{12,10},{14,12},{16,14},{18,16},{20... | collective-permute-start | bytes 589832 | tf_op jit(solution)/shard_map/ppermute | solution.py:321
  7.8 11.0 %collective-permute-start.1 = (bf16[16,48,128]{2,1,0:T(8,128)(2,1)S(1)}, bf16[16,48,128]{2,1,0:T(8,128)(2,1)S(1)}, u32[]{:S(2)}, u32[]{:S(2)}) collective-permute-start(bf16[16,48,128]{2,1,0:T(8,128)(2,1)S(1)} %get-tuple-element.16), channel_id=1, source_target_pairs={{0,2},{2,4},{4,6},{6,8},{8,10},{10,12},{12,14},{14,16},{16,18},{18... | collective-permute-start | bytes 589832 | tf_op jit(solution)/shard_map/ppermute | solution.py:320
  12.5 26.6 %collective-permute-start.4 = (bf16[16,48,128]{2,1,0:T(8,128)(2,1)S(1)}, bf16[16,48,128]{2,1,0:T(8,128)(2,1)S(1)}, u32[]{:S(2)}, u32[]{:S(2)}) collective-permute-start(bf16[16,48,128]{2,1,0:T(8,128)(2,1)S(1)} %collective-permute-done.3), channel_id=1, source_target_pairs={{0,1},{1,0},{2,3},{3,2},{4,5},{5,4},{6,7},{7,6},{8,9},{9,8},{10,11... | collective-permute-start | bytes 589832 | tf_op jit(solution)/shard_map/ppermute | solution.py:331
  18.8 20.4 %collective-permute-start.2 = (bf16[16,48,128]{2,1,0:T(8,128)(2,1)S(1)}, bf16[16,48,128]{2,1,0:T(8,128)(2,1)S(1)}, u32[]{:S(2)}, u32[]{:S(2)}) collective-permute-start(bf16[16,48,128]{2,1,0:T(8,128)(2,1)S(1)} %collective-permute-done.1), channel_id=1, source_target_pairs={{0,1},{1,0},{2,3},{3,2},{4,5},{5,4},{6,7},{7,6},{8,9},{9,8},{10,11... | collective-permute-start | bytes 589832 | tf_op jit(solution)/shard_map/ppermute | solution.py:330
  19.4 1.1 copy-start.2
  22.9 26.7 %all-to-all-start = ((f32[128,1,128]{2,1,0:T(1,128)}), f32[128,1,128]{2,1,0:T(1,128)S(1)}, u32[]{:S(2)}, u32[]{:S(2)}) async-start(f32[128,1,128]{2,1,0:T(1,128)} %get-tuple-element.13), calls=%async_computation | async-start | bytes 131072 | tf_op jit(solution)/shard_map/all_to_all | solution.py:329
  39.2 10.4 %copy-start.4 = (f32[128]{0:T(128)S(1)}, f32[128]{0:T(128)}, u32[]{:S(2)}) copy-start(f32[128]{0:T(128)} %param.10) | copy-start | bytes 1540
  39.2 10.4 %copy-start.6 = (f32[128]{0:T(128)S(1)}, f32[128]{0:T(128)}, u32[]{:S(2)}) copy-start(f32[128]{0:T(128)} %param.11) | copy-start | bytes 1540
  61.8 28.8 %all-to-all-start.1 = ((bf16[16,216,256]{2,1,0:T(8,128)(2,1)}), bf16[16,216,256]{2,1,0:T(8,128)(2,1)}, u32[]{:S(2)}, u32[]{:S(2)}) async-start(bf16[16,216,256]{2,1,0:T(8,128)(2,1)} %bitcast.11), calls=%async_computation.1 | async-start | bytes 3538944 | tf_op jit(solution)/shard_map/all_to_all | solution.py:374
  67.5 1.5 copy-start.5
  106.5 12.4 %all-to-all-start.3 = ((bf16[8,27,256]{2,1,0:T(8,128)(2,1)}), bf16[8,27,256]{2,1,0:T(8,128)(2,1)S(1)}, u32[]{:S(2)}, u32[]{:S(2)}) async-start(bf16[8,27,256]{2,1,0:T(8,128)(2,1)} %broadcast_in_dim.24), calls=%async_computation.3 | async-start | bytes 262144 | tf_op jit(solution)/shard_map/all_to_all | solution.py:404
  145.1 2.8 %copy-start.1 = (bf16[48,64,128]{2,1,0:T(8,128)(2,1)S(1)}, bf16[48,64,128]{2,1,0:T(8,128)(2,1)}, u32[]{:S(2)}) copy-start(bf16[48,64,128]{2,1,0:T(8,128)(2,1)} %param.8) | copy-start | bytes 2359300
  145.1 2.8 %copy-start.3 = (bf16[48,64,128]{2,1,0:T(8,128)(2,1)S(1)}, bf16[48,64,128]{2,1,0:T(8,128)(2,1)}, u32[]{:S(2)}) copy-start(bf16[48,64,128]{2,1,0:T(8,128)(2,1)} %param.7) | copy-start | bytes 2359300

commit v2 on v1

--- a/solution.py
+++ b/solution.py
@@ -17,20 +17,20 @@
 VMEM = pl.BlockSpec(memory_space=pltpu.VMEM)
 SMEM = pl.BlockSpec(memory_space=pltpu.SMEM)
 ANY = pl.BlockSpec(memory_space=pl.ANY)
-
-
-def call(kernel, out_shape, in_specs, scratch=(), flops=0, bytes_accessed=0):
-    several = isinstance(out_shape, (list, tuple))
+HBM = pl.BlockSpec(memory_space=pltpu.HBM)
+
+
+def call(kernel, out_shape, in_specs, scratch=(), out_specs=VMEM, flops=0, mib=20):
+    if isinstance(out_shape, (list, tuple)) and out_specs is VMEM:
+        out_specs = [VMEM] * len(out_shape)
     return pl.pallas_call(
         kernel,
         out_shape=out_shape,
         in_specs=in_specs,
-        out_specs=[VMEM] * len(out_shape) if several else VMEM,
+        out_specs=out_specs,
         scratch_shapes=list(scratch),
-        compiler_params=pltpu.CompilerParams(vmem_limit_bytes=48 * 1024 * 1024),
-        cost_estimate=pl.CostEstimate(
-            flops=flops, bytes_accessed=bytes_accessed, transcendentals=0
-        ),
+        compiler_params=pltpu.CompilerParams(vmem_limit_bytes=mib * 1024 * 1024),
+        cost_estimate=pl.CostEstimate(flops=flops, bytes_accessed=0, transcendentals=0),
     )
 
 
@@ -48,22 +48,63 @@
         out_ref[voxel] = rows_ref[pl.ds(voxel, slots, stride=64), :].astype(out_ref.dtype)
 
 
-def turn_kernel(in_ref, out_ref, low_ref, high_ref, rows_ref):
-    rows_ref[...] = in_ref[...].astype(F32)
-    turned(rows_ref, out_ref)
-    low_ref[...] = out_ref[0:16]
-    high_ref[...] = out_ref[48:64]
-
-
-def sums_kernel(counts_ref, in_ref, out_ref, sent_ref, rows_ref):
-    slots = out_ref.shape[1]
+def prepare_kernel(
+    counts_ref,
+    values_hbm,
+    cotangent_hbm,
+    values_hbm_out,
+    own_hbm,
+    low_hbm,
+    high_hbm,
+    sent_ref,
+    held_ref,
+    rows_ref,
+    values_out,
+    own_ref,
+    sems,
+    out_sems,
+):
+    slots = own_ref.shape[1]
     count = counts_ref[0]
-    rows_ref[...] = in_ref[...].astype(F32)
+    chunk = 64 * (slots // 4)
+    copies = [
+        pltpu.make_async_copy(
+            source.at[pl.ds(at * chunk, chunk)],
+            held_ref.at[which, pl.ds(at * chunk, chunk)],
+            sems.at[which, at],
+        )
+        for which, source in enumerate((cotangent_hbm, values_hbm))
+        for at in range(4)
+    ]
+    for copy in copies:
+        copy.start()
+    for at in range(4):
+        copies[at].wait()
+        rows_ref[0, at * chunk : at * chunk + chunk] = held_ref[
+            0, at * chunk : at * chunk + chunk
+        ].astype(F32)
+    turned(rows_ref.at[0], own_ref)
+    sends = [
+        pltpu.make_async_copy(own_ref.at[0:16], low_hbm, out_sems.at[0]),
+        pltpu.make_async_copy(own_ref.at[48:64], high_hbm, out_sems.at[1]),
+        pltpu.make_async_copy(own_ref, own_hbm, out_sems.at[2]),
+        pltpu.make_async_copy(values_out, values_hbm_out, out_sems.at[3]),
+    ]
+    for send in sends[:3]:
+        send.start()
+    for at in range(4):
+        copies[4 + at].wait()
+        rows_ref[1, at * chunk : at * chunk + chunk] = held_ref[
+            1, at * chunk : at * chunk + chunk
+        ].astype(F32)
+
+    turned(rows_ref.at[1], values_out)
+    sends[3].start()
 
     def over_slots(term):
         total = jnp.zeros((8, 128), F32)
         for slot in range(slots):
-            rows = term(rows_ref[slot * 64 : slot * 64 + 64, :]).reshape(8, 8, 128).sum(axis=0)
+            rows = term(rows_ref[1, slot * 64 : slot * 64 + 64, :]).reshape(8, 8, 128).sum(axis=0)
             total = total + jnp.where(slot < count, rows, 0.0)
         return jnp.broadcast_to(jnp.sum(total, axis=0, keepdims=True), (8, 128))
 
@@ -83,7 +124,8 @@
     row = exact_dot(total, to_sum) + exact_dot(squares, to_square)
     row = row + jnp.where(iota((8, 128), 1) == 32, count.astype(F32), 0.0)
     sent_ref[...] = jnp.broadcast_to(row[0:1].reshape(1, 1, 128), sent_ref.shape)
-    turned(rows_ref, out_ref)
+    for send in sends:
+        send.wait()
 
 
 def halo_kernel(
@@ -166,17 +208,13 @@
     gain_ref,
     shift_ref,
     values_ref,
-    grid_hbm,
+    grid_ref,
     out_ref,
     norm_ref,
-    grid_ref,
     act_ref,
     total_ref,
-    sem,
 ):
     slots = values_ref.shape[1]
-    copy = pltpu.make_async_copy(grid_hbm, grid_ref, sem)
-    copy.start()
     table = table_ref[...]
     held = jnp.sum(table, axis=0)
     voxels = held[:, 32:33] * (64.0 * GROUP_CH)
@@ -208,10 +246,7 @@
             pieces.append(jnp.where(live, pre / (1.0 + jnp.exp(-pre)), 0.0))
         rows = jnp.concatenate(pieces, axis=0)
         act_ref[plane * 128 : plane * 128 + 128, :] = rows.T.astype(BF16)
-    copy.wait()
-
-    @pl.loop(0, 9)
-    def _(turn):
+    for turn in range(9):
         for plane in range(6):
             first, last = planes_of(plane)
             part = jnp.dot(
@@ -279,9 +314,39 @@
 
 
 def last_kernel(
-    counts_ref, norm_ref, gain_ref, sums_ref, values_ref, cotangent_ref, grad_ref, out_ref
+    counts_ref,
+    norm_ref,
+    gain_ref,
+    plane_ref,
+    values_ref,
+    cotangent_ref,
+    grad_ref,
+    out_hbm,
+    weight_hbm,
+    sums_ref,
+    out_ref,
+    weight_ref,
+    out_sems,
+    weight_sems,
 ):
     slots = grad_ref.shape[0] // 64
+    pieces = plane_ref.shape[0]
+    piece = weight_ref.shape[0] // pieces
+    copies = []
+    totals = jnp.zeros((1, 256), F32)
+    for at in range(pieces):
+        block = plane_ref[at].astype(F32)
+        rows = pl.ds(at * piece, piece)
+        weight_ref[rows] = block[0:piece]
+        totals = totals + (block[piece : piece + 1] + block[piece + 1 : piece + 2])
+        totals = totals + block[piece + 2 : piece + 3]
+        copies.append(
+            pltpu.make_async_copy(weight_ref.at[rows], weight_hbm.at[rows], weight_sems.at[at])
+        )
+        copies[-1].start()
+    shift_sum, gain_sum = totals[:, 0:128], totals[:, 128:256]
+    sums_ref[0:1] = gain_sum
+    sums_ref[1:2] = shift_sum
     mean, rstd, voxels = norm_ref[0:1, :], norm_ref[1:2, :], norm_ref[2:3, :]
     gain = gain_ref[...]
     lane_in, lane_out = iota((128, 128), 0), iota((128, 128), 1)
@@ -290,8 +355,9 @@
     def grouped(row):
         return exact_dot(jnp.broadcast_to(row, (8, 128)), same)[0:1]
 
-    first = grouped(gain * sums_ref[:, 0:128]) / voxels
-    second = grouped(gain * sums_ref[:, 128:256]) / voxels
+    first = grouped(gain * shift_sum) / voxels
+    second = grouped(gain * gain_sum) / voxels
+    chunk = slots // 4
     for slot in range(slots):
         rows = slice(slot * 64, slot * 64 + 64)
         normed = (values_ref[rows, :].astype(F32) - mean) * rstd
@@ -299,6 +365,15 @@
         inner = gain * grad - first - normed * second
         result = cotangent_ref[rows, :].astype(F32) + rstd * inner
         out_ref[rows, :] = jnp.where(slot < counts_ref[0], result, 0.0).astype(BF16)
+        if slot % chunk == chunk - 1:
+            at = slot // chunk
+            rows = pl.ds(at * chunk * 64, chunk * 64)
+            copies.append(
+                pltpu.make_async_copy(out_ref.at[rows], out_hbm.at[rows], out_sems.at[at])
+            )
+            copies[-1].start()
+    for copy in copies:
+        copy.wait()
 
 
 def body(features, cotangent, weight, gain, shift, counts, neighbours):
@@ -308,27 +383,41 @@
     n_line = lax.axis_size("z")
     n_slab = n_plane * n_line
     core = lax.axis_index("ch").astype(jnp.int32).reshape(1)
-    swap = [(0, 1), (1, 0)]
     turned_shape = jax.ShapeDtypeStruct((voxels, slots, width), BF16)
     face_shape = jax.ShapeDtypeStruct((16, slots, width), BF16)
-    rows_scratch = pltpu.VMEM((rows, width), F32)
     gain_row, shift_row = gain.reshape(1, width), shift.reshape(1, width)
 
-    own, low, high = call(
-        turn_kernel, [turned_shape, face_shape, face_shape], [VMEM], [rows_scratch]
-    )(cotangent.reshape(rows, width))
-    before = lax.ppermute(high, SLABS, [(i, i + 1) for i in range(n_slab - 1)])
-    after = lax.ppermute(low, SLABS, [(i + 1, i) for i in range(n_slab - 1)])
-    own_other = lax.ppermute(own, "ch", swap)
-    values, sent = call(
-        sums_kernel,
-        [turned_shape, jax.ShapeDtypeStruct((n_slab, 1, 128), F32)],
-        [SMEM, VMEM],
-        [rows_scratch],
-    )(counts, features.reshape(rows, width))
+    values, own, low, high, sent = call(
+        prepare_kernel,
+        [
+            turned_shape,
+            turned_shape,
+            face_shape,
+            face_shape,
+            jax.ShapeDtypeStruct((n_slab, 1, 128), F32),
+        ],
+        [SMEM, HBM, HBM],
+        [
+            pltpu.VMEM((2, rows, width), BF16),
+            pltpu.VMEM((2, rows, width), F32),
+            pltpu.VMEM(turned_shape.shape, BF16),
+            pltpu.VMEM(turned_shape.shape, BF16),
+            pltpu.SemaphoreType.DMA((2, 4)),
+            pltpu.SemaphoreType.DMA((4,)),
+        ],
+        [HBM, HBM, HBM, HBM, VMEM],
+        mib=60,
+    )(counts, features.reshape(rows, width), cotangent.reshape(rows, width))
+    every = SLABS + ("ch",)
+    ups = [(i, i + 1) for i in range(n_slab - 1)]
+    straight = [(2 * i + c, 2 * j + c) for i, j in ups for c in range(2)]
+    across = [(2 * i + c, 2 * j + 1 - c) for i, j in ups for c in range(2)]
+    before = lax.ppermute(high, every, straight)
+    before_other = lax.ppermute(high, every, across)
+    after = lax.ppermute(low, every, [(j, i) for i, j in straight])
+    after_other = lax.ppermute(low, every, [(j, i) for i, j in across])
+    own_other = lax.ppermute(own, "ch", [(0, 1), (1, 0)])
     table = lax.all_to_all(sent, SLABS, 0, 0, tiled=True)
-    before_other = lax.ppermute(before, "ch", swap)
-    after_other = lax.ppermute(after, "ch", swap)
 
     cube = (4, 4, 4, slots, width)
     face = (4, 4, slots, width)
@@ -361,12 +450,10 @@
             jax.ShapeDtypeStruct((3, 9, width, 2 * width), BF16),
             jax.ShapeDtypeStruct((8, 128), F32),
         ],
-        [SMEM, VMEM, VMEM, VMEM, VMEM, ANY],
-        [
-            pltpu.VMEM(grid_shape, BF16),
+        [SMEM] + [VMEM] * 5,
+        [
             pltpu.VMEM((4 * width, 16 * slots), BF16),
             pltpu.VMEM((3, width, 2 * width), F32),
-            pltpu.SemaphoreType.DMA,
         ],
         flops=2 * rows * 27 * width * 2 * width,
     )(counts, table, gain_row, shift_row, values, grid)
@@ -411,27 +498,35 @@
     line = jnp.concatenate([line] + split + [jnp.zeros((5, 2 * width), BF16)], axis=0)
     plane = jnp.broadcast_to(line[None], (n_plane,) + line.shape)
     plane = lax.all_to_all(plane, PLANE, 0, 0, tiled=True)
-    grad_weight = plane[:, :piece].astype(F32).reshape(27, width, 2 * width)
-    totals = jnp.sum(plane[:, piece : piece + 3].astype(F32), axis=(0, 1)).reshape(1, 2 * width)
-
-    grad_features = call(
+    grad_features, grad_weight, totals = call(
         last_kernel,
-        jax.ShapeDtypeStruct((rows, width), BF16),
+        [
+            jax.ShapeDtypeStruct((rows, width), BF16),
+            jax.ShapeDtypeStruct((27 * width, 2 * width), F32),
+            jax.ShapeDtypeStruct((2, width), F32),
+        ],
         [SMEM] + [VMEM] * 6,
+        [
+            pltpu.VMEM((rows, width), BF16),
+            pltpu.VMEM((27 * width, 2 * width), F32),
+            pltpu.SemaphoreType.DMA((4,)),
+            pltpu.SemaphoreType.DMA((n_plane,)),
+        ],
+        [HBM, HBM, VMEM],
     )(
         counts,
         norm,
         gain_row,
-        totals,
+        plane,
         features.reshape(rows, width),
         cotangent.reshape(rows, width),
         grad_pre.reshape(rows, width),
     )
     return (
         grad_features.reshape(features.shape),
-        grad_weight,
-        totals[0, width:],
-        totals[0, :width],
+        grad_weight.reshape(27, width, 2 * width),
+        totals[0],
+        totals[1],
     )
 
 

time: 150 us -> 147 us (0.980)
  waiting for transfers between devices: 33.1 us -> 23.4 us
  starting transfers between devices: 31.3 us -> 39.5 us
  Pallas kernels: 34.5 us -> 27.9 us
  local copies, waits for them, and re-layouts: 6.15 us -> 11.9 us
  other arithmetic: 4.05 us -> 1.8 us
    ppermute x5, waiting for transfers between devices: 9.09 us -> 0.01 us  [the longest x1 0.01 us: body(): after_other = lax.ppermute(low, every, [(j, i) for i, j in across])]
    ppermute x5, starting transfers between devices: 6.91 us -> 14.9 us  [the longest x1 6.03 us: body(): after = lax.ppermute(low, every, [(j, i) for i, j in straight])]
    unnamed x15 -> x23, local copies, waits for them, and re-layouts: 4.55 us -> 10.4 us
    pallas_call x1, Pallas kernels: 12.2 us -> 8.03 us  [body(): call(weight_grad_kernel, [jax.ShapeDtypeStruct((3, 9, width, 2 * width),...]
    pallas_call x1, Pallas kernels: 12.9 us -> 10.2 us  [body(): call(act_grad_kernel, [jax.ShapeDtypeStruct((voxels, slots, width), F32),...]
    pallas_call x3 -> x2, Pallas kernels: 5.19 us -> 7.7 us  [the longest x1 5.4 us: body(): call(prepare_kernel, [turned_shape, turned_shape, face_shape, face_shape,...]
    pallas_call x1, Pallas kernels: 4.2 us -> 1.87 us  [body(): call(halo_kernel, jax.ShapeDtypeStruct(grid_shape, BF16), [SMEM, VMEM] +...]
    reshape x1 -> x0, other arithmetic: 2.23 us -> none  [body(): grad_weight = plane[:, :piece].astype(F32).reshape(27, width, 2 * width)]
  transfers between devices with their start and end apart: 8 -> 8, of which waited for: 5 -> 3; matrix products, arithmetic and copies ran while one was open for 1% -> 1% of each run, Pallas kernels for 13% -> 8%
where the time goes in v2:
time: 147 us; the launch traced here: 146 us
  blocking collectives  40.3 us (27%)
  starting transfers between devices  39.5 us (27%)
  Pallas kernels  27.9 us (19%)
  waiting for transfers between devices  23.4 us (16%)
  local copies, waits for them, and re-layouts  11.9 us (8%)
  other arithmetic  1.8 us (1%)
  between operations  1.52 us (1%)
    all_to_all x1, blocking collectives, body(): plane = lax.all_to_all(plane, PLANE, 0, 0, tiled=True)  25.9 us
    all_to_all x1, starting transfers between devices, body(): table = lax.all_to_all(sent, SLABS, 0, 0, tiled=True)  15.5 us
    all_to_all x1, blocking collectives, body(): part = jnp.sum(lax.all_to_all(part, 'z', 0, 0, tiled=True), axis=0)  14.3 us
    unnamed x23, local copies, waits for them, and re-layouts  10.4 us
    pallas_call x1, Pallas kernels, body(): call(act_grad_kernel, [jax.ShapeDtypeStruct((voxels, slots, width), F32),...  10.2 us
    all_to_all x1, waiting for transfers between devices, body(): lax.all_to_all(weight_term.reshape(n_plane, piece, 2 * width), PLANE, 0,...  9.34 us
    all_to_all x1, waiting for transfers between devices, body(): line = lax.all_to_all(line, 'z', 0, 0, tiled=True).reshape(piece, 2 * width)  8.98 us
    pallas_call x1, Pallas kernels, body(): call(weight_grad_kernel, [jax.ShapeDtypeStruct((3, 9, width, 2 * width),...  8.03 us
  transfers between devices with their start and end apart: 8, of which 3 were waited for; matrix products, arithmetic and copies ran while one was open for 1% of the time, Pallas kernels for 8%

profile of v2, /device:TPU:2, one launch (start us, length us, event | category | flops | bytes accessed | tf_op | source)
XLA Modules:
  0.0 146.3 jit_solution(8605499155404994147)
XLA Ops:
  1.3 5.4 %shard_map.102 = (bf16[64,48,128]{2,1,0:T(8,128)(2,1)}, bf16[64,48,128]{2,1,0:T(8,128)(2,1)}, bf16[16,48,128]{2,1,0:T(8,128)(2,1)}, bf16[16,48,128]{2,1,0:T(8,128)(2,1)}, f32[128,1,128]{2,1,0:T(1,128)}) custom-call(s32[1]{0:T(128)S(6)} %copy.13.counts_ref, bf16[3072,128]{1,0:T(8,128)(2,1)} %bitcast.21, bf16[3072,128]{1,0:T(8,128)(2,1)} %bitcast.23), custom_call_target="tpu_custom_call" | custom-call | tf_op jit(solution)/shard_map/pallas_call | solution.py:390
  6.7 0.1 collective-permute-start
  6.8 5.0 %collective-permute-start.4 = (bf16[16,48,128]{2,1,0:T(8,128)(2,1)}, bf16[16,48,128]{2,1,0:T(8,128)(2,1)S(1)}, u32[]{:S(2)}, u32[]{:S(2)}) collective-permute-start(bf16[16,48,128]{2,1,0:T(8,128)(2,1)} %get-tuple-element.20), channel_id=1, source_target_pairs={{3,0},{2,1},{5,2},{4,3},{7,4},{6,5},{9,6},{8,7},{11,8},{10,9},{13,... | collective-permute-start | bytes 589832 | tf_op jit(solution)/shard_map/ppermute | solution.py:418
  11.8 1.9 %collective-permute-start.1 = (bf16[16,48,128]{2,1,0:T(8,128)(2,1)}, bf16[16,48,128]{2,1,0:T(8,128)(2,1)S(1)}, u32[]{:S(2)}, u32[]{:S(2)}) collective-permute-start(bf16[16,48,128]{2,1,0:T(8,128)(2,1)} %get-tuple-element.19), channel_id=1, source_target_pairs={{0,2},{1,3},{2,4},{3,5},{4,6},{5,7},{6,8},{7,9},{8,10},{9,11},{10,... | collective-permute-start | bytes 589832 | tf_op jit(solution)/shard_map/ppermute | solution.py:415
  13.7 1.9 %collective-permute-start.2 = (bf16[16,48,128]{2,1,0:T(8,128)(2,1)}, bf16[16,48,128]{2,1,0:T(8,128)(2,1)S(1)}, u32[]{:S(2)}, u32[]{:S(2)}) collective-permute-start(bf16[16,48,128]{2,1,0:T(8,128)(2,1)} %get-tuple-element.19), channel_id=1, source_target_pairs={{0,3},{1,2},{2,5},{3,4},{4,7},{5,6},{6,9},{7,8},{8,11},{9,10},{10,... | collective-permute-start | bytes 589832 | tf_op jit(solution)/shard_map/ppermute | solution.py:416
  15.6 6.0 %collective-permute-start.3 = (bf16[16,48,128]{2,1,0:T(8,128)(2,1)}, bf16[16,48,128]{2,1,0:T(8,128)(2,1)S(1)}, u32[]{:S(2)}, u32[]{:S(2)}) collective-permute-start(bf16[16,48,128]{2,1,0:T(8,128)(2,1)} %get-tuple-element.20), channel_id=1, source_target_pairs={{2,0},{3,1},{4,2},{5,3},{6,4},{7,5},{8,6},{9,7},{10,8},{11,9},{12,... | collective-permute-start | bytes 589832 | tf_op jit(solution)/shard_map/ppermute | solution.py:417
  21.7 15.5 %all-to-all-start = ((f32[128,1,128]{2,1,0:T(1,128)}), f32[128,1,128]{2,1,0:T(1,128)S(1)}, u32[]{:S(2)}, u32[]{:S(2)}) async-start(f32[128,1,128]{2,1,0:T(1,128)} %get-tuple-element.16), calls=%async_computation | async-start | bytes 131072 | tf_op jit(solution)/shard_map/all_to_all | solution.py:420
  37.2 0.8 copy.12.near_ref
  38.0 0.0 collective-permute-done.4
  38.0 0.0 collective-permute-done.1
  38.0 0.0 collective-permute-done.2
  38.0 0.0 collective-permute-done.3
  38.0 0.0 collective-permute-done
  38.0 0.0 copy-start.5
  38.0 1.1 copy-done.5
  39.2 0.0 copy-start.6
  39.2 0.0 copy-start.8
  39.2 1.9 %shard_map.103.grid_ref = bf16[6,6,6,48,256]{4,3,2,1,0:T(8,128)(2,1)S(1)} custom-call(s32[1]{0:T(128)} %bitcast.4.core_ref, s32[48,27]{1,0:T(8,128)S(1)} %copy.12.near_ref, bf16[4,4,4,48,128]{4,3,2,1,0:T(8,128)(2,1)S(1)} %bitcast.26, bf16[4,4,4,48,128]{4,3,2,1,0:T(8,128)(2,1)S(1)} %bitcast.27, bf16[4,4,48,128]{3,2,1,0:T(8,128)(2,1)S(1)} %bitcast.29, ...), custom_call_target="tpu_custom_call" | custom-call | flops 1000000000 | tf_op jit(solution)/shard_map/pallas_call | solution.py:425
  41.0 0.0 copy-start
  41.1 2.4 %copy-done = bf16[6,6,6,48,256]{4,3,2,1,0:T(8,128)(2,1)} copy-done((bf16[6,6,6,48,256]{4,3,2,1,0:T(8,128)(2,1)}, bf16[6,6,6,48,256]{4,3,2,1,0:T(8,128)(2,1)S(1)}, u32[]{:S(2)}) %copy-start) | copy-done | bytes 5308440
  43.4 5.1 %all-to-all-done.table_ref = f32[128,1,128]{2,1,0:T(1,128)S(1)} async-done(((f32[128,1,128]{2,1,0:T(1,128)}), f32[128,1,128]{2,1,0:T(1,128)S(1)}, u32[]{:S(2)}, u32[]{:S(2)}) %all-to-all-start) | async-done | bytes 65568 | tf_op jit(solution)/shard_map/all_to_all | solution.py:420
  48.5 0.0 copy-done.6
  48.5 0.0 copy-done.8
  48.5 0.0 copy-done.10
  48.5 0.0 copy-start.1
  48.5 2.5 %copy-done.1 = bf16[6,6,6,48,256]{4,3,2,1,0:T(8,128)(2,1)S(1)} copy-done((bf16[6,6,6,48,256]{4,3,2,1,0:T(8,128)(2,1)S(1)}, bf16[6,6,6,48,256]{4,3,2,1,0:T(8,128)(2,1)}, u32[]{:S(2)}) %copy-start.1) | copy-done | bytes 5308440
  51.0 8.0 %shard_map.104 = (bf16[3,9,128,256]{3,2,1,0:T(8,128)(2,1)}, f32[8,128]{1,0:T(8,128)S(1)}) custom-call(s32[1]{0:T(128)S(6)} %copy.13.counts_ref, f32[128,1,128]{2,1,0:T(1,128)S(1)} %all-to-all-done.table_ref, f32[1,128]{1,0:T(1,128)S(1)} %bitcast.33, f32[1,128]{1,0:T(1,128)S(1)} %bitcast.37, bf16[64,48,128]{2,1,0:T(8,128)(2,1)S(1)} %copy-done.8, ...), custom_call_target="tpu_custom_call" | custom-call | flops 5435817984 | tf_op jit(solution)/shard_map/pallas_call | solution.py:447
  59.1 5.7 %all-to-all-start.1 = ((bf16[16,216,256]{2,1,0:T(8,128)(2,1)}), bf16[16,216,256]{2,1,0:T(8,128)(2,1)}, u32[]{:S(2)}, u32[]{:S(2)}) async-start(bf16[16,216,256]{2,1,0:T(8,128)(2,1)} %bitcast.11), calls=%async_computation.1 | async-start | bytes 3538944 | tf_op jit(solution)/shard_map/all_to_all | solution.py:461
  64.8 0.0 copy-done.7
  64.8 0.0 copy-start.2
  64.8 2.5 %copy-done.2 = bf16[6,6,6,48,256]{4,3,2,1,0:T(8,128)(2,1)S(1)} copy-done((bf16[6,6,6,48,256]{4,3,2,1,0:T(8,128)(2,1)S(1)}, bf16[6,6,6,48,256]{4,3,2,1,0:T(8,128)(2,1)}, u32[]{:S(2)}) %copy-start.2) | copy-done | bytes 5308440
  67.3 1.1 copy-done.9
  68.4 10.2 %shard_map.105 = (f32[64,48,128]{2,1,0:T(8,128)S(1)}, f32[1,256]{1,0:T(1,128)S(1)}) custom-call(s32[1]{0:T(128)S(6)} %copy.13.counts_ref, f32[8,128]{1,0:T(8,128)S(1)} %get-tuple-element.21.norm_ref, f32[1,128]{1,0:T(1,128)S(1)} %bitcast.34, f32[1,128]{1,0:T(1,128)S(1)} %bitcast.38, bf16[64,48,128]{2,1,0:T(8,128)(2,1)S(1)} %copy-done.9, ...), custom_call_target="tpu_custom_call" | custom-call | flops 5435817984 | tf_op jit(solution)/shard_map/pallas_call | solution.py:465
  78.7 9.3 %all-to-all-done.1 = bf16[16,216,256]{2,1,0:T(8,128)(2,1)} async-done(((bf16[16,216,256]{2,1,0:T(8,128)(2,1)}), bf16[16,216,256]{2,1,0:T(8,128)(2,1)}, u32[]{:S(2)}, u32[]{:S(2)}) %all-to-all-start.1) | async-done | bytes 1769504 | tf_op jit(solution)/shard_map/all_to_all | solution.py:461
  88.0 1.7 %convert_reduce_fusion = f32[216,256]{1,0:T(8,128)S(1)} fusion(bf16[16,216,256]{2,1,0:T(8,128)(2,1)} %all-to-all-done.1), kind=kLoop, calls=%fused_computation | loop fusion | flops 1714176 | bytes 1990656 | tf_op jit(solution)/shard_map/reduce_sum | solution.py:484
  89.9 14.3 %all_to_all.25 = f32[8,28,256]{2,1,0:T(8,128)S(1)} all-to-all(f32[8,28,256]{2,1,0:T(8,128)S(1)} %pad_maximum_fusion), channel_id=1, replica_groups=mesh['z'=8,'x'=4,'y'=4,'ch'=2] {'z'}, dimensions={0} | all-to-all | bytes 458752 | tf_op jit(solution)/shard_map/all_to_all | solution.py:488
  104.2 0.7 broadcast_in_dim.24
  104.9 3.4 %all-to-all-start.3 = ((bf16[8,27,256]{2,1,0:T(8,128)(2,1)}), bf16[8,27,256]{2,1,0:T(8,128)(2,1)S(1)}, u32[]{:S(2)}, u32[]{:S(2)}) async-start(bf16[8,27,256]{2,1,0:T(8,128)(2,1)} %broadcast_in_dim.24), calls=%async_computation.3 | async-start | bytes 262144 | tf_op jit(solution)/shard_map/all_to_all | solution.py:491
  108.3 9.0 %all-to-all-done.3 = bf16[8,27,256]{2,1,0:T(8,128)(2,1)S(1)} async-done(((bf16[8,27,256]{2,1,0:T(8,128)(2,1)}), bf16[8,27,256]{2,1,0:T(8,128)(2,1)S(1)}, u32[]{:S(2)}, u32[]{:S(2)}) %all-to-all-start.3) | async-done | bytes 110624 | tf_op jit(solution)/shard_map/all_to_all | solution.py:491
  117.3 0.1 reshape.84
  117.4 0.2 broadcast_in_dim.26
  117.5 0.0 copy-start.3
  117.6 0.0 copy-start.4
  117.6 25.9 %all_to_all.26.plane_ref = bf16[16,224,256]{2,1,0:T(8,128)(2,1)S(1)} all-to-all(bf16[16,224,256]{2,1,0:T(8,128)(2,1)S(1)} %broadcast_in_dim.26), channel_id=1, replica_groups=mesh['z'=8,'x'=4,'y'=4,'ch'=2] {'x','y'}, dimensions={0} | all-to-all | bytes 3670016 | tf_op jit(solution)/shard_map/all_to_all | solution.py:500
  143.5 0.0 copy-done.3
  143.5 0.0 copy-done.4
  143.5 2.3 %shard_map.106 = (bf16[3072,128]{1,0:T(8,128)(2,1)}, f32[3456,256]{1,0:T(8,128)}, f32[2,128]{1,0:T(2,128)S(1)}) custom-call(s32[1]{0:T(128)S(6)} %copy.13.counts_ref, f32[8,128]{1,0:T(8,128)S(1)} %get-tuple-element.21.norm_ref, f32[1,128]{1,0:T(1,128)S(1)} %bitcast.35, bf16[16,224,256]{2,1,0:T(8,128)(2,1)S(1)} %all_to_all.26.plane_ref, ...), custom_call_target="tpu_custom_call" | custom-call | tf_op jit(solution)/shard_map/pallas_call | solution.py:501
  145.8 0.5 slice_bitcast_fusion
  (11 shorter events, 0.1 us)
Async XLA Ops:
  6.7 31.3 %collective-permute-start = (bf16[64,48,128]{2,1,0:T(8,128)(2,1)}, bf16[64,48,128]{2,1,0:T(8,128)(2,1)S(1)}, u32[]{:S(2)}, u32[]{:S(2)}) collective-permute-start(bf16[64,48,128]{2,1,0:T(8,128)(2,1)} %get-tuple-element.18), channel_id=1, source_target_pairs={{0,1},{1,0},{2,3},{3,2},{4,5},{5,4},{6,7},{7,6},{8,9},{9,8},{10,11... | collective-permute-start | bytes 2359304 | tf_op jit(solution)/shard_map/ppermute | solution.py:419
  6.8 31.2 %collective-permute-start.4 = (bf16[16,48,128]{2,1,0:T(8,128)(2,1)}, bf16[16,48,128]{2,1,0:T(8,128)(2,1)S(1)}, u32[]{:S(2)}, u32[]{:S(2)}) collective-permute-start(bf16[16,48,128]{2,1,0:T(8,128)(2,1)} %get-tuple-element.20), channel_id=1, source_target_pairs={{3,0},{2,1},{5,2},{4,3},{7,4},{6,5},{9,6},{8,7},{11,8},{10,9},{13,... | collective-permute-start | bytes 589832 | tf_op jit(solution)/shard_map/ppermute | solution.py:418
  11.8 26.2 %collective-permute-start.1 = (bf16[16,48,128]{2,1,0:T(8,128)(2,1)}, bf16[16,48,128]{2,1,0:T(8,128)(2,1)S(1)}, u32[]{:S(2)}, u32[]{:S(2)}) collective-permute-start(bf16[16,48,128]{2,1,0:T(8,128)(2,1)} %get-tuple-element.19), channel_id=1, source_target_pairs={{0,2},{1,3},{2,4},{3,5},{4,6},{5,7},{6,8},{7,9},{8,10},{9,11},{10,... | collective-permute-start | bytes 589832 | tf_op jit(solution)/shard_map/ppermute | solution.py:415
  13.7 24.3 %collective-permute-start.2 = (bf16[16,48,128]{2,1,0:T(8,128)(2,1)}, bf16[16,48,128]{2,1,0:T(8,128)(2,1)S(1)}, u32[]{:S(2)}, u32[]{:S(2)}) collective-permute-start(bf16[16,48,128]{2,1,0:T(8,128)(2,1)} %get-tuple-element.19), channel_id=1, source_target_pairs={{0,3},{1,2},{2,5},{3,4},{4,7},{5,6},{6,9},{7,8},{8,11},{9,10},{10,... | collective-permute-start | bytes 589832 | tf_op jit(solution)/shard_map/ppermute | solution.py:416
  15.6 22.4 %collective-permute-start.3 = (bf16[16,48,128]{2,1,0:T(8,128)(2,1)}, bf16[16,48,128]{2,1,0:T(8,128)(2,1)S(1)}, u32[]{:S(2)}, u32[]{:S(2)}) collective-permute-start(bf16[16,48,128]{2,1,0:T(8,128)(2,1)} %get-tuple-element.20), channel_id=1, source_target_pairs={{2,0},{3,1},{4,2},{5,3},{6,4},{7,5},{8,6},{9,7},{10,8},{11,9},{12,... | collective-permute-start | bytes 589832 | tf_op jit(solution)/shard_map/ppermute | solution.py:417
  21.7 26.8 %all-to-all-start = ((f32[128,1,128]{2,1,0:T(1,128)}), f32[128,1,128]{2,1,0:T(1,128)S(1)}, u32[]{:S(2)}, u32[]{:S(2)}) async-start(f32[128,1,128]{2,1,0:T(1,128)} %get-tuple-element.16), calls=%async_computation | async-start | bytes 131072 | tf_op jit(solution)/shard_map/all_to_all | solution.py:420
  38.0 1.1 copy-start.5
  39.2 9.4 %copy-start.6 = (f32[128]{0:T(128)S(1)}, f32[128]{0:T(128)}, u32[]{:S(2)}) copy-start(f32[128]{0:T(128)} %param.10) | copy-start | bytes 1540
  39.2 9.4 %copy-start.8 = (bf16[64,48,128]{2,1,0:T(8,128)(2,1)S(1)}, bf16[64,48,128]{2,1,0:T(8,128)(2,1)}, u32[]{:S(2)}) copy-start(bf16[64,48,128]{2,1,0:T(8,128)(2,1)} %get-tuple-element.17.values_ref) | copy-start | bytes 2359300
  39.2 9.4 %copy-start.10 = (f32[128]{0:T(128)S(1)}, f32[128]{0:T(128)}, u32[]{:S(2)}) copy-start(f32[128]{0:T(128)} %param.11) | copy-start | bytes 1540
  41.0 2.4 %copy-start = (bf16[6,6,6,48,256]{4,3,2,1,0:T(8,128)(2,1)}, bf16[6,6,6,48,256]{4,3,2,1,0:T(8,128)(2,1)S(1)}, u32[]{:S(2)}) copy-start(bf16[6,6,6,48,256]{4,3,2,1,0:T(8,128)(2,1)S(1)} %shard_map.103.grid_ref) | copy-start | bytes 15925252
  48.5 2.5 %copy-start.1 = (bf16[6,6,6,48,256]{4,3,2,1,0:T(8,128)(2,1)S(1)}, bf16[6,6,6,48,256]{4,3,2,1,0:T(8,128)(2,1)}, u32[]{:S(2)}) copy-start(bf16[6,6,6,48,256]{4,3,2,1,0:T(8,128)(2,1)} %copy-done) | copy-start | bytes 15925252
  59.1 5.7 %copy-start.7 = (bf16[27,128,256]{2,1,0:T(8,128)(2,1)S(1)}, bf16[27,128,256]{2,1,0:T(8,128)(2,1)}, u32[]{:S(2)}) copy-start(bf16[27,128,256]{2,1,0:T(8,128)(2,1)} %param.9) | copy-start | bytes 5308420
  59.1 29.0 %all-to-all-start.1 = ((bf16[16,216,256]{2,1,0:T(8,128)(2,1)}), bf16[16,216,256]{2,1,0:T(8,128)(2,1)}, u32[]{:S(2)}, u32[]{:S(2)}) async-start(bf16[16,216,256]{2,1,0:T(8,128)(2,1)} %bitcast.11), calls=%async_computation.1 | async-start | bytes 3538944 | tf_op jit(solution)/shard_map/all_to_all | solution.py:461
  64.8 2.5 %copy-start.2 = (bf16[6,6,6,48,256]{4,3,2,1,0:T(8,128)(2,1)S(1)}, bf16[6,6,6,48,256]{4,3,2,1,0:T(8,128)(2,1)}, u32[]{:S(2)}) copy-start(bf16[6,6,6,48,256]{4,3,2,1,0:T(8,128)(2,1)} %copy-done) | copy-start | bytes 15925252
  67.3 1.1 copy-start.9
  104.9 12.4 %all-to-all-start.3 = ((bf16[8,27,256]{2,1,0:T(8,128)(2,1)}), bf16[8,27,256]{2,1,0:T(8,128)(2,1)S(1)}, u32[]{:S(2)}, u32[]{:S(2)}) async-start(bf16[8,27,256]{2,1,0:T(8,128)(2,1)} %broadcast_in_dim.24), calls=%async_computation.3 | async-start | bytes 262144 | tf_op jit(solution)/shard_map/all_to_all | solution.py:491
  117.5 26.0 %copy-start.3 = (bf16[48,64,128]{2,1,0:T(8,128)(2,1)S(1)}, bf16[48,64,128]{2,1,0:T(8,128)(2,1)}, u32[]{:S(2)}) copy-start(bf16[48,64,128]{2,1,0:T(8,128)(2,1)} %param.7) | copy-start | bytes 2359300
  117.6 25.9 %copy-start.4 = (bf16[48,64,128]{2,1,0:T(8,128)(2,1)S(1)}, bf16[48,64,128]{2,1,0:T(8,128)(2,1)}, u32[]{:S(2)}) copy-start(bf16[48,64,128]{2,1,0:T(8,128)(2,1)} %param.8) | copy-start | bytes 2359300

commit v3 on v2

--- a/solution.py
+++ b/solution.py
@@ -16,11 +16,11 @@
 BF16 = jnp.bfloat16
 VMEM = pl.BlockSpec(memory_space=pltpu.VMEM)
 SMEM = pl.BlockSpec(memory_space=pltpu.SMEM)
+HBM = pl.BlockSpec(memory_space=pltpu.HBM)
 ANY = pl.BlockSpec(memory_space=pl.ANY)
-HBM = pl.BlockSpec(memory_space=pltpu.HBM)
-
-
-def call(kernel, out_shape, in_specs, scratch=(), out_specs=VMEM, flops=0, mib=20):
+
+
+def call(kernel, out_shape, in_specs, scratch=(), out_specs=VMEM, flops=0, mib=52, aliases=None):
     if isinstance(out_shape, (list, tuple)) and out_specs is VMEM:
         out_specs = [VMEM] * len(out_shape)
     return pl.pallas_call(
@@ -29,6 +29,7 @@
         in_specs=in_specs,
         out_specs=out_specs,
         scratch_shapes=list(scratch),
+        input_output_aliases=aliases or {},
         compiler_params=pltpu.CompilerParams(vmem_limit_bytes=mib * 1024 * 1024),
         cost_estimate=pl.CostEstimate(flops=flops, bytes_accessed=0, transcendentals=0),
     )
@@ -48,63 +49,50 @@
         out_ref[voxel] = rows_ref[pl.ds(voxel, slots, stride=64), :].astype(out_ref.dtype)
 
 
-def prepare_kernel(
-    counts_ref,
-    values_hbm,
-    cotangent_hbm,
-    values_hbm_out,
-    own_hbm,
-    low_hbm,
-    high_hbm,
-    sent_ref,
-    held_ref,
-    rows_ref,
-    values_out,
-    own_ref,
-    sems,
-    out_sems,
-):
-    slots = own_ref.shape[1]
-    count = counts_ref[0]
-    chunk = 64 * (slots // 4)
+def fetch(source, target, sems, pieces):
+    step = source.shape[0] // pieces
     copies = [
         pltpu.make_async_copy(
-            source.at[pl.ds(at * chunk, chunk)],
-            held_ref.at[which, pl.ds(at * chunk, chunk)],
-            sems.at[which, at],
+            source.at[pl.ds(at * step, step)], target.at[pl.ds(at * step, step)], sems.at[at]
         )
-        for which, source in enumerate((cotangent_hbm, values_hbm))
-        for at in range(4)
+        for at in range(pieces)
     ]
     for copy in copies:
         copy.start()
-    for at in range(4):
-        copies[at].wait()
-        rows_ref[0, at * chunk : at * chunk + chunk] = held_ref[
-            0, at * chunk : at * chunk + chunk
-        ].astype(F32)
-    turned(rows_ref.at[0], own_ref)
+    return copies
+
+
+def widen(copies, held_ref, rows_ref):
+    step = held_ref.shape[0] // len(copies)
+    for at, copy in enumerate(copies):
+        copy.wait()
+        rows = slice(at * step, at * step + step)
+        rows_ref[rows, :] = held_ref[rows, :].astype(F32)
+
+
+def turn_kernel(in_hbm, own_hbm, low_hbm, high_hbm, held_ref, rows_ref, own_ref, sems, out_sems):
+    widen(fetch(in_hbm, held_ref, sems, 4), held_ref, rows_ref)
+    turned(rows_ref, own_ref)
     sends = [
-        pltpu.make_async_copy(own_ref.at[0:16], low_hbm, out_sems.at[0]),
-        pltpu.make_async_copy(own_ref.at[48:64], high_hbm, out_sems.at[1]),
-        pltpu.make_async_copy(own_ref, own_hbm, out_sems.at[2]),
-        pltpu.make_async_copy(values_out, values_hbm_out, out_sems.at[3]),
+        pltpu.make_async_copy(own_ref, own_hbm, out_sems.at[0]),
+        pltpu.make_async_copy(own_ref.at[0:16], low_hbm, out_sems.at[1]),
+        pltpu.make_async_copy(own_ref.at[48:64], high_hbm, out_sems.at[2]),
     ]
-    for send in sends[:3]:
+    for send in sends:
         send.start()
-    for at in range(4):
-        copies[4 + at].wait()
-        rows_ref[1, at * chunk : at * chunk + chunk] = held_ref[
-            1, at * chunk : at * chunk + chunk
-        ].astype(F32)
-
-    turned(rows_ref.at[1], values_out)
-    sends[3].start()
+    for send in sends:
+        send.wait()
+
+
+def sums_kernel(counts_ref, values_hbm, sent_ref, held_ref, rows_ref, sems):
+    slots = held_ref.shape[0] // 64
+    count = counts_ref[0]
+    widen(fetch(values_hbm, held_ref, sems, 4), held_ref, rows_ref)
 
     def over_slots(term):
         total = jnp.zeros((8, 128), F32)
         for slot in range(slots):
-            rows = term(rows_ref[1, slot * 64 : slot * 64 + 64, :]).reshape(8, 8, 128).sum(axis=0)
+            rows = term(rows_ref[slot * 64 : slot * 64 + 64, :]).reshape(8, 8, 128).sum(axis=0)
             total = total + jnp.where(slot < count, rows, 0.0)
         return jnp.broadcast_to(jnp.sum(total, axis=0, keepdims=True), (8, 128))
 
@@ -124,77 +112,68 @@
     row = exact_dot(total, to_sum) + exact_dot(squares, to_square)
     row = row + jnp.where(iota((8, 128), 1) == 32, count.astype(F32), 0.0)
     sent_ref[...] = jnp.broadcast_to(row[0:1].reshape(1, 1, 128), sent_ref.shape)
-    for send in sends:
-        send.wait()
-
-
-def halo_kernel(
-    core_ref,
-    near_ref,
-    own_ref,
-    own_other_ref,
-    before_ref,
-    before_other_ref,
-    after_ref,
-    after_other_ref,
-    grid_ref,
-    low_ref,
-    high_ref,
-    pick_ref,
-    sems,
-):
-    slots = near_ref.shape[0]
-    core = core_ref[0]
+
+
+def lanes_of(core):
     mine = pl.ds(pl.multiple_of(core * 128, 128), 128)
     other = pl.ds(pl.multiple_of((1 - core) * 128, 128), 128)
-    centre = grid_ref.at[1:5, 1:5, 1:5]
+    return mine, other
+
+
+def side(at):
+    return -1 if at == 0 else (1 if at == 5 else 0)
+
+
+def source(at):
+    return {0: 4, 5: 1}.get(at, at)
+
+
+def offset_of(dx, b, c):
+    return 9 * (dx + 1) + 3 * (side(b) + 1) + side(c) + 1
+
+
+def choose(near, offset, first, last):
+    columns = iota((near.shape[0], last - first), 1) + first
+    return (near[:, offset : offset + 1] == columns).astype(F32).astype(BF16)
+
+
+def halo_kernel(core_ref, near_ref, own_ref, own_other_ref, middle_hbm, middle_ref, sems, out_sems):
+    slots = near_ref.shape[0]
+    mine, other = lanes_of(core_ref[0])
+    centre = middle_ref.at[:, 1:5, 1:5]
     copies = [
         pltpu.make_async_copy(own_ref, centre.at[:, :, :, :, mine], sems.at[0]),
         pltpu.make_async_copy(own_other_ref, centre.at[:, :, :, :, other], sems.at[1]),
-        pltpu.make_async_copy(before_ref, low_ref.at[:, :, :, mine], sems.at[2]),
-        pltpu.make_async_copy(before_other_ref, low_ref.at[:, :, :, other], sems.at[3]),
-        pltpu.make_async_copy(after_ref, high_ref.at[:, :, :, mine], sems.at[4]),
-        pltpu.make_async_copy(after_other_ref, high_ref.at[:, :, :, other], sems.at[5]),
     ]
     for copy in copies:
         copy.start()
     near = near_ref[...]
-    columns = iota((slots, 3 * slots), 1)
-    for offset in range(27):
-        pick_ref[offset] = (near[:, offset : offset + 1] == columns).astype(F32)
+    places = [(b, c) for b in range(6) for c in range(6) if side(b) or side(c)]
+    picks = {
+        offset: choose(near, offset, slots, 2 * slots)
+        for offset in sorted({offset_of(0, b, c) for b, c in places})
+    }
     for copy in copies:
         copy.wait()
-
-    def side(at):
-        return -1 if at == 0 else (1 if at == 5 else 0)
-
-    def source(at):
-        return {0: 4, 5: 1}.get(at, at)
-
-    places = [(a, b, c) for a in range(6) for b in range(6) for c in range(6)]
-    for a, b, c in places:
-        dx, dy, dz = side(a), side(b), side(c)
-        if (dx, dy, dz) == (0, 0, 0):
-            continue
-        offset = 9 * (dx + 1) + 3 * (dy + 1) + dz + 1
-        inside = grid_ref[source(a), source(b), source(c)]
-        if dx == 0:
-            pick = pick_ref[offset, :, slots : 2 * slots]
-            table = inside
-        elif dx < 0:
-            pick = pick_ref[offset, :, 0 : 2 * slots]
-            table = jnp.concatenate([low_ref[source(b) - 1, source(c) - 1], inside], axis=0)
-        else:
-            pick = pick_ref[offset, :, slots : 3 * slots]
-            table = jnp.concatenate([inside, high_ref[source(b) - 1, source(c) - 1]], axis=0)
-        grid_ref[a, b, c] = jnp.dot(pick.astype(BF16), table, preferred_element_type=F32).astype(
-            BF16
+    sends = []
+    for plane in range(4):
+        for b, c in places:
+            middle_ref[plane, b, c] = jnp.dot(
+                picks[offset_of(0, b, c)],
+                middle_ref[plane, source(b), source(c)],
+                preferred_element_type=F32,
+            ).astype(BF16)
+        sends.append(
+            pltpu.make_async_copy(middle_ref.at[plane], middle_hbm.at[plane], out_sems.at[plane])
         )
-
-
-def window(grid_ref, plane, turn):
-    slots = grid_ref.shape[3]
-    block = grid_ref[plane, pl.ds(2 - turn // 3, 4), pl.ds(2 - turn % 3, 4)]
+        sends[-1].start()
+    for send in sends:
+        send.wait()
+
+
+def window(plane_ref, turn):
+    slots = plane_ref.shape[2]
+    block = plane_ref[pl.ds(2 - turn // 3, 4), pl.ds(2 - turn % 3, 4)]
     return block.reshape(16 * slots, 256)
 
 
@@ -207,14 +186,26 @@
     table_ref,
     gain_ref,
     shift_ref,
-    values_ref,
-    grid_ref,
-    out_ref,
+    values_hbm,
+    middle_hbm,
+    out_hbm,
+    part_hbm,
+    edge_ref,
     norm_ref,
+    held_ref,
+    rows_ref,
+    middle_ref,
     act_ref,
     total_ref,
+    out_ref,
+    part_ref,
+    sems,
+    plane_sems,
+    out_sems,
 ):
-    slots = values_ref.shape[1]
+    slots = middle_ref.shape[3]
+    copies = fetch(values_hbm, held_ref, sems, 4)
+    planes = fetch(middle_hbm, middle_ref, plane_sems, 4)
     table = table_ref[...]
     held = jnp.sum(table, axis=0)
     voxels = held[:, 32:33] * (64.0 * GROUP_CH)
@@ -238,31 +229,134 @@
     norm_ref[3:8, :] = jnp.zeros((5, 128), F32)
     gain, shift = gain_ref[...], shift_ref[...]
     live = iota((slots, 128), 0) < counts_ref[0]
+    widen(copies, held_ref, rows_ref)
     for plane in range(4):
         pieces = []
         for voxel in range(plane * 16, plane * 16 + 16):
-            normed = (values_ref[voxel].astype(F32) - mean) * rstd
+            normed = (rows_ref[pl.ds(voxel, slots, stride=64), :] - mean) * rstd
             pre = normed * gain + shift
             pieces.append(jnp.where(live, pre / (1.0 + jnp.exp(-pre)), 0.0))
         rows = jnp.concatenate(pieces, axis=0)
         act_ref[plane * 128 : plane * 128 + 128, :] = rows.T.astype(BF16)
+    edge_ref[0] = act_ref[0:128, :]
+    edge_ref[1] = act_ref[384:512, :]
+    sends = []
     for turn in range(9):
-        for plane in range(6):
+        seen = set()
+        for plane in range(1, 5):
+            if turn == 0:
+                planes[plane - 1].wait()
             first, last = planes_of(plane)
             part = jnp.dot(
                 act_ref[first * 128 : last * 128, :],
-                window(grid_ref, plane, turn),
+                window(middle_ref.at[plane - 1], turn),
                 preferred_element_type=F32,
             )
             for at in range(first, last):
                 step = at - plane + 2
                 term = part[(at - first) * 128 : (at - first) * 128 + 128]
-                if at == 0:
+                if step in seen:
+                    total_ref[step] += term
+                else:
                     total_ref[step] = term
-                else:
-                    total_ref[step] += term
-        for step in range(3):
-            out_ref[step, turn] = total_ref[step].astype(BF16)
+                    seen.add(step)
+        out_ref[turn] = total_ref[1].astype(BF16)
+        part_ref[0, turn] = total_ref[0]
+        part_ref[1, turn] = total_ref[2]
+        sends += [
+            pltpu.make_async_copy(out_ref.at[turn], out_hbm.at[1, turn], out_sems.at[0, turn]),
+            pltpu.make_async_copy(part_ref.at[0, turn], part_hbm.at[0, turn], out_sems.at[1, turn]),
+            pltpu.make_async_copy(part_ref.at[1, turn], part_hbm.at[1, turn], out_sems.at[2, turn]),
+        ]
+        for send in sends[-3:]:
+            send.start()
+    for send in sends:
+        send.wait()
+
+
+def edge_kernel(
+    core_ref,
+    near_ref,
+    edge_ref,
+    before_ref,
+    before_other_ref,
+    after_ref,
+    after_other_ref,
+    middle_hbm,
+    part_hbm,
+    in_hbm,
+    out_hbm,
+    sides_hbm,
+    face_ref,
+    inner_ref,
+    sides_ref,
+    part_ref,
+    out_ref,
+    sems,
+    part_sems,
+    out_sems,
+    side_sems,
+):
+    slots = near_ref.shape[0]
+    mine, other = lanes_of(core_ref[0])
+    copies = [
+        pltpu.make_async_copy(before_ref, face_ref.at[0, :, :, :, mine], sems.at[0]),
+        pltpu.make_async_copy(before_other_ref, face_ref.at[0, :, :, :, other], sems.at[1]),
+        pltpu.make_async_copy(after_ref, face_ref.at[1, :, :, :, mine], sems.at[2]),
+        pltpu.make_async_copy(after_other_ref, face_ref.at[1, :, :, :, other], sems.at[3]),
+        pltpu.make_async_copy(middle_hbm.at[3, 1:5, 1:5], inner_ref.at[0], sems.at[4]),
+        pltpu.make_async_copy(middle_hbm.at[0, 1:5, 1:5], inner_ref.at[1], sems.at[5]),
+    ]
+    for copy in copies:
+        copy.start()
+    parts = [
+        pltpu.make_async_copy(part_hbm.at[which], part_ref.at[which], part_sems.at[which])
+        for which in range(2)
+    ]
+    for part in parts:
+        part.start()
+    near = near_ref[...]
+    places = [(b, c) for b in range(6) for c in range(6)]
+    sends = []
+    for which, dx in enumerate((-1, 1)):
+        lowest = which * slots
+        picks = {
+            offset: choose(near, offset, lowest, lowest + 2 * slots)
+            for offset in sorted({offset_of(dx, b, c) for b, c in places})
+        }
+        if which == 0:
+            for copy in copies:
+                copy.wait()
+        for b, c in places:
+            outer = face_ref[which, source(b) - 1, source(c) - 1]
+            inner = inner_ref[which, source(b) - 1, source(c) - 1]
+            table = [outer, inner] if which == 0 else [inner, outer]
+            sides_ref[which, b, c] = jnp.dot(
+                picks[offset_of(dx, b, c)],
+                jnp.concatenate(table, axis=0),
+                preferred_element_type=F32,
+            ).astype(BF16)
+        sends.append(
+            pltpu.make_async_copy(sides_ref.at[which], sides_hbm.at[which], side_sems.at[which])
+        )
+        sends[-1].start()
+        parts[which].wait()
+    for turn in range(9):
+        for which in range(2):
+            term = jnp.dot(
+                edge_ref[which], window(sides_ref.at[which], turn), preferred_element_type=F32
+            )
+            out_ref[1 - which, turn] = (part_ref[1 - which, turn] + term).astype(BF16)
+            sends.append(
+                pltpu.make_async_copy(
+                    out_ref.at[1 - which, turn],
+                    out_hbm.at[2 - 2 * which, turn],
+                    out_sems.at[which, turn],
+                )
+            )
+            sends[-1].start()
+    for send in sends:
+        send.wait()
 
 
 def act_grad_kernel(
@@ -272,21 +366,25 @@
     shift_ref,
     values_ref,
     weight_ref,
-    grid_ref,
+    middle_ref,
+    sides_ref,
     out_ref,
     sums_ref,
     total_ref,
+    rows_ref,
 ):
-    slots = values_ref.shape[1]
+    slots = middle_ref.shape[3]
     total_ref[...] = jnp.zeros_like(total_ref)
+    rows_ref[...] = values_ref[...].astype(F32)
 
     @pl.loop(0, 9)
     def _(turn):
         for plane in range(6):
             first, last = planes_of(plane)
             low, high = first - plane + 2, last - plane + 2
+            rows = sides_ref.at[plane // 5] if plane in (0, 5) else middle_ref.at[plane - 1]
             part = lax.dot_general(
-                window(grid_ref, plane, turn),
+                window(rows, turn),
                 weight_ref[low:high, turn].reshape((high - low) * 128, 256),
                 (((1,), (1,)), ((), ())),
                 preferred_element_type=F32,
@@ -301,7 +399,7 @@
     shift_sum = jnp.zeros((8, 128), F32)
     gain_sum = jnp.zeros((8, 128), F32)
     for voxel in range(64):
-        normed = (values_ref[voxel].astype(F32) - mean) * rstd
+        normed = (rows_ref[pl.ds(voxel, slots, stride=64), :] - mean) * rstd
         pre = normed * gain + shift
         sig = 1.0 / (1.0 + jnp.exp(-pre))
         grad = total_ref[voxel // 16, voxel % 16] * sig * (1.0 + pre * (1.0 - sig))
@@ -386,28 +484,55 @@
     turned_shape = jax.ShapeDtypeStruct((voxels, slots, width), BF16)
     face_shape = jax.ShapeDtypeStruct((16, slots, width), BF16)
     gain_row, shift_row = gain.reshape(1, width), shift.reshape(1, width)
-
-    values, own, low, high, sent = call(
-        prepare_kernel,
-        [
-            turned_shape,
-            turned_shape,
-            face_shape,
-            face_shape,
-            jax.ShapeDtypeStruct((n_slab, 1, 128), F32),
-        ],
-        [SMEM, HBM, HBM],
-        [
-            pltpu.VMEM((2, rows, width), BF16),
-            pltpu.VMEM((2, rows, width), F32),
+    value_rows = features.reshape(rows, width)
+    cotangent_rows = cotangent.reshape(rows, width)
+    work = 2 * rows * 27 * width * 2 * width
+
+    sent = call(
+        sums_kernel,
+        jax.ShapeDtypeStruct((n_slab, 1, 128), F32),
+        [SMEM, HBM],
+        [
+            pltpu.VMEM((rows, width), BF16),
+            pltpu.VMEM((rows, width), F32),
+            pltpu.SemaphoreType.DMA((4,)),
+        ],
+        mib=60,
+    )(counts, value_rows)
+    table = lax.all_to_all(sent, SLABS, 0, 0, tiled=True)
+    own, low, high = call(
+        turn_kernel,
+        [turned_shape, face_shape, face_shape],
+        [HBM],
+        [
+            pltpu.VMEM((rows, width), BF16),
+            pltpu.VMEM((rows, width), F32),
             pltpu.VMEM(turned_shape.shape, BF16),
-            pltpu.VMEM(turned_shape.shape, BF16),
-            pltpu.SemaphoreType.DMA((2, 4)),
             pltpu.SemaphoreType.DMA((4,)),
-        ],
-        [HBM, HBM, HBM, HBM, VMEM],
+            pltpu.SemaphoreType.DMA((3,)),
+        ],
+        [HBM] * 3,
         mib=60,
-    )(counts, features.reshape(rows, width), cotangent.reshape(rows, width))
+    )(cotangent_rows)
+    own_other = lax.ppermute(own, "ch", [(0, 1), (1, 0)])
+
+    cube = (4, 4, 4, slots, width)
+    face = (4, 4, slots, width)
+    middle_shape = (4, 6, 6, slots, 2 * width)
+    middle = call(
+        halo_kernel,
+        jax.ShapeDtypeStruct(middle_shape, BF16),
+        [SMEM, VMEM, ANY, ANY],
+        [
+            pltpu.VMEM(middle_shape, BF16),
+            pltpu.SemaphoreType.DMA((2,)),
+            pltpu.SemaphoreType.DMA((4,)),
+        ],
+        HBM,
+        flops=10**9,
+    )(core, neighbours, own.reshape(cube), own_other.reshape(cube))
+
+    table, middle, low, high = lax.optimization_barrier((table, middle, low, high))
     every = SLABS + ("ch",)
     ups = [(i, i + 1) for i in range(n_slab - 1)]
     straight = [(2 * i + c, 2 * j + c) for i, j in ups for c in range(2)]
@@ -416,47 +541,64 @@
     before_other = lax.ppermute(high, every, across)
     after = lax.ppermute(low, every, [(j, i) for i, j in straight])
     after_other = lax.ppermute(low, every, [(j, i) for i, j in across])
-    own_other = lax.ppermute(own, "ch", [(0, 1), (1, 0)])
-    table = lax.all_to_all(sent, SLABS, 0, 0, tiled=True)
-
-    cube = (4, 4, 4, slots, width)
-    face = (4, 4, slots, width)
-    grid_shape = (6, 6, 6, slots, 2 * width)
-    grid = call(
-        halo_kernel,
-        jax.ShapeDtypeStruct(grid_shape, BF16),
-        [SMEM, VMEM] + [ANY] * 6,
-        [
-            pltpu.VMEM((4, 4, slots, 2 * width), BF16),
-            pltpu.VMEM((4, 4, slots, 2 * width), BF16),
-            pltpu.VMEM((27, slots, 3 * slots), F32),
+
+    term_shape = jax.ShapeDtypeStruct((3, 9, width, 2 * width), BF16)
+    part_shape = jax.ShapeDtypeStruct((2, 9, width, 2 * width), F32)
+    weight_term, part_term, edge, norm = call(
+        weight_grad_kernel,
+        [
+            term_shape,
+            part_shape,
+            jax.ShapeDtypeStruct((2, width, 16 * slots), BF16),
+            jax.ShapeDtypeStruct((8, 128), F32),
+        ],
+        [SMEM, VMEM, VMEM, VMEM, HBM, HBM],
+        [
+            pltpu.VMEM((rows, width), BF16),
+            pltpu.VMEM((rows, width), F32),
+            pltpu.VMEM(middle_shape, BF16),
+            pltpu.VMEM((4 * width, 16 * slots), BF16),
+            pltpu.VMEM((3, width, 2 * width), F32),
+            pltpu.VMEM((9, width, 2 * width), BF16),
+            pltpu.VMEM(part_shape.shape, F32),
+            pltpu.SemaphoreType.DMA((4,)),
+            pltpu.SemaphoreType.DMA((4,)),
+            pltpu.SemaphoreType.DMA((3, 9)),
+        ],
+        [HBM, HBM, VMEM, VMEM],
+        flops=work,
+    )(counts, table, gain_row, shift_row, value_rows, middle)
+    sides_shape = jax.ShapeDtypeStruct((2, 6, 6, slots, 2 * width), BF16)
+    weight_term, sides = call(
+        edge_kernel,
+        [term_shape, sides_shape],
+        [SMEM, VMEM, VMEM] + [ANY] * 4 + [HBM] * 3,
+        [
+            pltpu.VMEM((2, 4, 4, slots, 2 * width), BF16),
+            pltpu.VMEM((2, 4, 4, slots, 2 * width), BF16),
+            pltpu.VMEM(sides_shape.shape, BF16),
+            pltpu.VMEM(part_shape.shape, F32),
+            pltpu.VMEM((2, 9, width, 2 * width), BF16),
             pltpu.SemaphoreType.DMA((6,)),
-        ],
-        flops=10**9,
+            pltpu.SemaphoreType.DMA((2,)),
+            pltpu.SemaphoreType.DMA((2, 9)),
+            pltpu.SemaphoreType.DMA((2,)),
+        ],
+        [HBM, HBM],
+        aliases={9: 0},
+        flops=work // 6,
     )(
         core,
         neighbours,
-        own.reshape(cube),
-        own_other.reshape(cube),
+        edge,
         before.reshape(face),
         before_other.reshape(face),
         after.reshape(face),
         after_other.reshape(face),
-    )
-
-    weight_term, norm = call(
-        weight_grad_kernel,
-        [
-            jax.ShapeDtypeStruct((3, 9, width, 2 * width), BF16),
-            jax.ShapeDtypeStruct((8, 128), F32),
-        ],
-        [SMEM] + [VMEM] * 5,
-        [
-            pltpu.VMEM((4 * width, 16 * slots), BF16),
-            pltpu.VMEM((3, width, 2 * width), F32),
-        ],
-        flops=2 * rows * 27 * width * 2 * width,
-    )(counts, table, gain_row, shift_row, values, grid)
+        middle,
+        part_term,
+        weight_term,
+    )
     piece = 27 * width // n_plane
     parts = lax.all_to_all(
         weight_term.reshape(n_plane, piece, 2 * width), PLANE, 0, 0, tiled=True
@@ -468,17 +610,18 @@
             jax.ShapeDtypeStruct((voxels, slots, width), F32),
             jax.ShapeDtypeStruct((1, 2 * width), F32),
         ],
-        [SMEM] + [VMEM] * 6,
-        [pltpu.VMEM((4, 16, slots, width), F32)],
-        flops=2 * rows * 27 * width * 2 * width,
+        [SMEM] + [VMEM] * 7,
+        [pltpu.VMEM((4, 16, slots, width), F32), pltpu.VMEM((rows, width), F32)],
+        flops=work,
     )(
         counts,
         norm,
         gain_row,
         shift_row,
-        values,
+        value_rows,
         weight.reshape(3, 9, width, 2 * width),
-        grid,
+        middle,
+        sides,
     )
 
     part = jnp.sum(parts.astype(F32), axis=0).reshape(n_line, piece // n_line, 2 * width)
@@ -513,13 +656,14 @@
             pltpu.SemaphoreType.DMA((n_plane,)),
         ],
         [HBM, HBM, VMEM],
+        mib=20,
     )(
         counts,
         norm,
         gain_row,
         plane,
-        features.reshape(rows, width),
-        cotangent.reshape(rows, width),
+        value_rows,
+        cotangent_rows,
         grad_pre.reshape(rows, width),
     )
     return (

time: 147 us -> 148 us (level)
  Pallas kernels: 27.9 us -> 39.7 us
  local copies, waits for them, and re-layouts: 11.9 us -> 2.74 us
  waiting for transfers between devices: 23.4 us -> 25.4 us
  other arithmetic: 1.8 us -> 0.31 us
    unnamed x23 -> x19, local copies, waits for them, and re-layouts: 10.4 us -> 1.26 us
    pallas_call x3 -> x5, Pallas kernels: 15.3 us -> 22.4 us  [the longest x1 9.55 us: body(): call(weight_grad_kernel, [term_shape, part_shape, jax.ShapeDtypeStruct((2...]
    pallas_call x1, Pallas kernels: 10.2 us -> 15.1 us  [body(): call(act_grad_kernel, [jax.ShapeDtypeStruct((voxels, slots, width), F32),...]
    all_to_all x1, waiting for transfers between devices: 5.11 us -> 7.57 us  [body(): table = lax.all_to_all(sent, SLABS, 0, 0, tiled=True)]
    reduce_sum x1, other arithmetic: 1.74 us -> 0.25 us  [body(): jnp.sum(parts.astype(F32), axis=0)]
  transfers between devices with their start and end apart: 8 -> 8, of which waited for: 3 -> 3; matrix products, arithmetic and copies ran while one was open for 1% -> 0% of each run, Pallas kernels for 8% -> 20%
where the time goes in v3:
time: 148 us
  Pallas kernels  39.7 us (27%)
  blocking collectives  39.4 us (27%)
  starting transfers between devices  38.8 us (26%)
  waiting for transfers between devices  25.4 us (17%)
  local copies, waits for them, and re-layouts  2.74 us (2%)
  between operations  1.56 us (1%)
    all_to_all x1, blocking collectives, body(): plane = lax.all_to_all(plane, PLANE, 0, 0, tiled=True)  26.1 us
    all_to_all x1, starting transfers between devices, body(): table = lax.all_to_all(sent, SLABS, 0, 0, tiled=True)  15.4 us
    pallas_call x1, Pallas kernels, body(): call(act_grad_kernel, [jax.ShapeDtypeStruct((voxels, slots, width), F32),...  15.1 us
    all_to_all x1, blocking collectives, body(): part = jnp.sum(lax.all_to_all(part, 'z', 0, 0, tiled=True), axis=0)  13.3 us
    pallas_call x1, Pallas kernels, body(): call(weight_grad_kernel, [term_shape, part_shape, jax.ShapeDtypeStruct((2...  9.55 us
    all_to_all x1, waiting for transfers between devices, body(): line = lax.all_to_all(line, 'z', 0, 0, tiled=True).reshape(piece, 2 * width)  8.98 us
    all_to_all x1, waiting for transfers between devices, body(): lax.all_to_all(weight_term.reshape(n_plane, piece, 2 * width), PLANE, 0,...  8.8 us
    all_to_all x1, waiting for transfers between devices, body(): table = lax.all_to_all(sent, SLABS, 0, 0, tiled=True)  7.57 us
  transfers between devices with their start and end apart: 8, of which 3 were waited for; matrix products, arithmetic and copies ran while one was open for 0% of the time, Pallas kernels for 20%

profile of v3, /device:TPU:2, one launch (start us, length us, event | category | flops | bytes accessed | tf_op | source)
XLA Modules:
  0.0 147.8 jit_solution(1413202820612292957)
XLA Ops:
  0.6 0.0 copy-start.6
  0.6 3.2 %shard_map.103 = (bf16[64,48,128]{2,1,0:T(8,128)(2,1)}, bf16[16,48,128]{2,1,0:T(8,128)(2,1)}, bf16[16,48,128]{2,1,0:T(8,128)(2,1)}) custom-call(bf16[3072,128]{1,0:T(8,128)(2,1)} %bitcast.25), custom_call_target="tpu_custom_call" | custom-call | tf_op jit(solution)/shard_map/pallas_call | solution.py:503
  3.8 0.1 collective-permute-start
  4.6 2.7 %shard_map.102 = f32[128,1,128]{2,1,0:T(1,128)} custom-call(s32[1]{0:T(128)S(6)} %copy.17.counts_ref, bf16[3072,128]{1,0:T(8,128)(2,1)} %bitcast.21), custom_call_target="tpu_custom_call" | custom-call | tf_op jit(solution)/shard_map/pallas_call | solution.py:491
  7.2 15.4 %all-to-all-start = ((f32[128,1,128]{2,1,0:T(1,128)}), f32[128,1,128]{2,1,0:T(1,128)S(1)}, u32[]{:S(2)}, u32[]{:S(2)}) async-start(f32[128,1,128]{2,1,0:T(1,128)} %shard_map.102), calls=%async_computation | async-start | bytes 131072 | tf_op jit(solution)/shard_map/all_to_all | solution.py:502
  22.7 0.0 copy-done.6
  22.7 0.1 copy.14.near_ref
  22.8 0.0 collective-permute-done
  22.8 0.0 copy-start.3
  22.8 1.1 copy-done.3
  23.9 0.0 copy-start.8
  23.9 0.0 copy-start.7
  23.9 0.0 copy-start
  23.9 0.0 copy-start.5
  24.0 2.5 %shard_map.104.middle_hbm.middle_ref = bf16[4,6,6,48,256]{4,3,2,1,0:T(8,128)(2,1)} custom-call(s32[1]{0:T(128)} %bitcast.1.core_ref, s32[48,27]{1,0:T(8,128)S(1)} %copy.14.near_ref, bf16[4,4,4,48,128]{4,3,2,1,0:T(8,128)(2,1)S(1)} %bitcast.28, bf16[4,4,4,48,128]{4,3,2,1,0:T(8,128)(2,1)S(1)} %bitcast.29), custom_call_target="tpu_custom_call" | custom-call | flops 1000000000 | tf_op jit(solution)/shard_map/pallas_call | solution.py:522
  26.5 7.6 %all-to-all-done.table_ref = f32[128,1,128]{2,1,0:T(1,128)S(1)} async-done(((f32[128,1,128]{2,1,0:T(1,128)}), f32[128,1,128]{2,1,0:T(1,128)S(1)}, u32[]{:S(2)}, u32[]{:S(2)}) %all-to-all-start) | async-done | bytes 65568 | tf_op jit(solution)/shard_map/all_to_all | solution.py:502
  34.0 0.0 copy-done.8
  34.0 2.5 %collective-permute-start.1 = (bf16[16,48,128]{2,1,0:T(8,128)(2,1)S(1)}, bf16[16,48,128]{2,1,0:T(8,128)(2,1)S(1)}, u32[]{:S(2)}, u32[]{:S(2)}) collective-permute-start(bf16[16,48,128]{2,1,0:T(8,128)(2,1)S(1)} %copy-done.8), channel_id=1, source_target_pairs={{0,2},{1,3},{2,4},{3,5},{4,6},{5,7},{6,8},{7,9},{8,10},{9,11},{10,... | collective-permute-start | bytes 589832 | tf_op jit(solution)/shard_map/ppermute | solution.py:540
  36.5 1.9 %collective-permute-start.2 = (bf16[16,48,128]{2,1,0:T(8,128)(2,1)S(1)}, bf16[16,48,128]{2,1,0:T(8,128)(2,1)S(1)}, u32[]{:S(2)}, u32[]{:S(2)}) collective-permute-start(bf16[16,48,128]{2,1,0:T(8,128)(2,1)S(1)} %copy-done.8), channel_id=1, source_target_pairs={{0,3},{1,2},{2,5},{3,4},{4,7},{5,6},{6,9},{7,8},{8,11},{9,10},{10,... | collective-permute-start | bytes 589832 | tf_op jit(solution)/shard_map/ppermute | solution.py:541
  38.4 0.0 copy-done.7
  38.5 5.5 %collective-permute-start.3 = (bf16[16,48,128]{2,1,0:T(8,128)(2,1)S(1)}, bf16[16,48,128]{2,1,0:T(8,128)(2,1)S(1)}, u32[]{:S(2)}, u32[]{:S(2)}) collective-permute-start(bf16[16,48,128]{2,1,0:T(8,128)(2,1)S(1)} %copy-done.7), channel_id=1, source_target_pairs={{2,0},{3,1},{4,2},{5,3},{6,4},{7,5},{8,6},{9,7},{10,8},{11,9},{12,... | collective-permute-start | bytes 589832 | tf_op jit(solution)/shard_map/ppermute | solution.py:542
  43.9 3.5 %collective-permute-start.4 = (bf16[16,48,128]{2,1,0:T(8,128)(2,1)S(1)}, bf16[16,48,128]{2,1,0:T(8,128)(2,1)S(1)}, u32[]{:S(2)}, u32[]{:S(2)}) collective-permute-start(bf16[16,48,128]{2,1,0:T(8,128)(2,1)S(1)} %copy-done.7), channel_id=1, source_target_pairs={{3,0},{2,1},{5,2},{4,3},{7,4},{6,5},{9,6},{8,7},{11,8},{10,9},{13,... | collective-permute-start | bytes 589832 | tf_op jit(solution)/shard_map/ppermute | solution.py:543
  47.5 0.0 copy-done
  47.5 0.0 copy-done.4
  47.5 0.0 copy-done.5
  47.5 9.6 %shard_map.105 = (bf16[3,9,128,256]{3,2,1,0:T(8,128)(2,1)}, f32[2,9,128,256]{3,2,1,0:T(8,128)}, bf16[2,128,768]{2,1,0:T(8,128)(2,1)S(1)}, f32[8,128]{1,0:T(8,128)S(1)}) custom-call(s32[1]{0:T(128)S(6)} %copy.17.counts_ref, f32[128,1,128]{2,1,0:T(1,128)S(1)} %all-to-all-done.table_ref, f32[1,128]{1,0:T(1,128)S(1)} %bitcast.35, f32[1,128]{1,0:T(1,128)S(1)} %bitcast.38, ...), custom_call_target="tpu_custom_call" | custom-call | flops 5435817984 | tf_op jit(solution)/shard_map/pallas_call | solution.py:547
  57.1 0.0 collective-permute-done.1
  57.1 0.0 collective-permute-done.2
  57.1 0.0 collective-permute-done.3
  57.1 0.0 collective-permute-done.4
  57.1 4.5 %shard_map.106 = (bf16[3,9,128,256]{3,2,1,0:T(8,128)(2,1)}, bf16[2,6,6,48,256]{4,3,2,1,0:T(8,128)(2,1)}) custom-call(s32[1]{0:T(128)} %bitcast.1.core_ref, s32[48,27]{1,0:T(8,128)S(1)} %copy.14.near_ref, bf16[2,128,768]{2,1,0:T(8,128)(2,1)S(1)} %get-tuple-element.28.edge_ref, bf16[4,4,48,128]{3,2,1,0:T(8,128)(2,1)S(1)} %bitcast.30, ...), custom_call_target="tpu_custom_call", output_to_operand_aliasing={{0}: (9, {})} | custom-call | flops 905969664 | tf_op jit(solution)/shard_map/pallas_call | solution.py:572
  61.6 6.5 %all-to-all-start.1 = ((bf16[16,216,256]{2,1,0:T(8,128)(2,1)}), bf16[16,216,256]{2,1,0:T(8,128)(2,1)S(1)}, u32[]{:S(2)}, u32[]{:S(2)}) async-start(bf16[16,216,256]{2,1,0:T(8,128)(2,1)} %bitcast.40), calls=%async_computation.1 | async-start | bytes 3538944 | tf_op jit(solution)/shard_map/all_to_all | solution.py:603
  68.0 15.1 %shard_map.107 = (f32[64,48,128]{2,1,0:T(8,128)}, f32[1,256]{1,0:T(1,128)S(1)}) custom-call(s32[1]{0:T(128)S(6)} %copy.17.counts_ref, f32[8,128]{1,0:T(8,128)S(1)} %get-tuple-element.27.norm_ref, f32[1,128]{1,0:T(1,128)S(1)} %bitcast.36, f32[1,128]{1,0:T(1,128)S(1)} %bitcast.39, bf16[3072,128]{1,0:T(8,128)(2,1)S(1)} %bitcast.23, ...), custom_call_target="tpu_custom_call" | custom-call | flops 5435817984 | tf_op jit(solution)/shard_map/pallas_call | solution.py:607
  83.1 8.8 %all-to-all-done.1 = bf16[16,216,256]{2,1,0:T(8,128)(2,1)S(1)} async-done(((bf16[16,216,256]{2,1,0:T(8,128)(2,1)}), bf16[16,216,256]{2,1,0:T(8,128)(2,1)S(1)}, u32[]{:S(2)}, u32[]{:S(2)}) %all-to-all-start.1) | async-done | bytes 1769504 | tf_op jit(solution)/shard_map/all_to_all | solution.py:603
  91.9 0.3 convert_reduce_fusion
  92.2 13.3 %all_to_all.25 = f32[8,28,256]{2,1,0:T(8,128)S(1)} all-to-all(f32[8,28,256]{2,1,0:T(8,128)S(1)} %pad_maximum_fusion), channel_id=1, replica_groups=mesh['z'=8,'x'=4,'y'=4,'ch'=2] {'z'}, dimensions={0} | all-to-all | bytes 458752 | tf_op jit(solution)/shard_map/all_to_all | solution.py:631
  105.5 0.7 broadcast_in_dim.24
  106.2 3.4 %all-to-all-start.3 = ((bf16[8,27,256]{2,1,0:T(8,128)(2,1)}), bf16[8,27,256]{2,1,0:T(8,128)(2,1)S(1)}, u32[]{:S(2)}, u32[]{:S(2)}) async-start(bf16[8,27,256]{2,1,0:T(8,128)(2,1)} %broadcast_in_dim.24), calls=%async_computation.3 | async-start | bytes 262144 | tf_op jit(solution)/shard_map/all_to_all | solution.py:634
  109.6 9.0 %all-to-all-done.3 = bf16[8,27,256]{2,1,0:T(8,128)(2,1)S(1)} async-done(((bf16[8,27,256]{2,1,0:T(8,128)(2,1)}), bf16[8,27,256]{2,1,0:T(8,128)(2,1)S(1)}, u32[]{:S(2)}, u32[]{:S(2)}) %all-to-all-start.3) | async-done | bytes 110624 | tf_op jit(solution)/shard_map/all_to_all | solution.py:634
  118.6 0.1 reshape.82
  118.7 0.2 broadcast_in_dim.26
  118.9 0.0 copy-start.1
  118.9 0.0 copy-start.2
  118.9 26.1 %all_to_all.26.plane_ref = bf16[16,224,256]{2,1,0:T(8,128)(2,1)S(1)} all-to-all(bf16[16,224,256]{2,1,0:T(8,128)(2,1)S(1)} %broadcast_in_dim.26), channel_id=1, replica_groups=mesh['z'=8,'x'=4,'y'=4,'ch'=2] {'x','y'}, dimensions={0} | all-to-all | bytes 3670016 | tf_op jit(solution)/shard_map/all_to_all | solution.py:643
  145.0 0.0 copy-done.1
  145.0 0.0 copy-done.2
  145.0 2.3 %shard_map.108 = (bf16[3072,128]{1,0:T(8,128)(2,1)}, f32[3456,256]{1,0:T(8,128)}, f32[2,128]{1,0:T(2,128)S(1)}) custom-call(s32[1]{0:T(128)S(6)} %copy.17.counts_ref, f32[8,128]{1,0:T(8,128)S(1)} %get-tuple-element.27.norm_ref, f32[1,128]{1,0:T(1,128)S(1)} %bitcast.37, bf16[16,224,256]{2,1,0:T(8,128)(2,1)S(1)} %all_to_all.26.plane_ref, ...), custom_call_target="tpu_custom_call" | custom-call | tf_op jit(solution)/shard_map/pallas_call | solution.py:644
  147.3 0.5 slice_bitcast_fusion
  (9 shorter events, 0.1 us)
Async XLA Ops:
  0.6 22.1 %copy-start.6 = (s32[48,27]{0,1:T(8,128)S(1)}, s32[48,27]{0,1:T(8,128)}, u32[]{:S(2)}) copy-start(s32[48,27]{0,1:T(8,128)} %param.13) | copy-start | bytes 15556
  3.8 19.0 %collective-permute-start = (bf16[64,48,128]{2,1,0:T(8,128)(2,1)}, bf16[64,48,128]{2,1,0:T(8,128)(2,1)S(1)}, u32[]{:S(2)}, u32[]{:S(2)}) collective-permute-start(bf16[64,48,128]{2,1,0:T(8,128)(2,1)} %get-tuple-element.22), channel_id=1, source_target_pairs={{0,1},{1,0},{2,3},{3,2},{4,5},{5,4},{6,7},{7,6},{8,9},{9,8},{10,11... | collective-permute-start | bytes 2359304 | tf_op jit(solution)/shard_map/ppermute | solution.py:517
  7.2 26.8 %all-to-all-start = ((f32[128,1,128]{2,1,0:T(1,128)}), f32[128,1,128]{2,1,0:T(1,128)S(1)}, u32[]{:S(2)}, u32[]{:S(2)}) async-start(f32[128,1,128]{2,1,0:T(1,128)} %shard_map.102), calls=%async_computation | async-start | bytes 131072 | tf_op jit(solution)/shard_map/all_to_all | solution.py:502
  22.8 1.1 copy-start.3
  23.9 10.1 %copy-start.8 = (bf16[16,48,128]{2,1,0:T(8,128)(2,1)S(1)}, bf16[16,48,128]{2,1,0:T(8,128)(2,1)}, u32[]{:S(2)}) copy-start(bf16[16,48,128]{2,1,0:T(8,128)(2,1)} %get-tuple-element.29) | copy-start | bytes 589828
  23.9 14.5 %copy-start.7 = (bf16[16,48,128]{2,1,0:T(8,128)(2,1)S(1)}, bf16[16,48,128]{2,1,0:T(8,128)(2,1)}, u32[]{:S(2)}) copy-start(bf16[16,48,128]{2,1,0:T(8,128)(2,1)} %get-tuple-element.30) | copy-start | bytes 589828
  23.9 23.6 %copy-start = (bf16[48,64,128]{2,1,0:T(8,128)(2,1)S(1)}, bf16[48,64,128]{2,1,0:T(8,128)(2,1)}, u32[]{:S(2)}) copy-start(bf16[48,64,128]{2,1,0:T(8,128)(2,1)} %param.7) | copy-start | bytes 2359300
  23.9 23.6 %copy-start.4 = (f32[128]{0:T(128)S(1)}, f32[128]{0:T(128)}, u32[]{:S(2)}) copy-start(f32[128]{0:T(128)} %param.10) | copy-start | bytes 1540
  23.9 23.6 %copy-start.5 = (f32[128]{0:T(128)S(1)}, f32[128]{0:T(128)}, u32[]{:S(2)}) copy-start(f32[128]{0:T(128)} %param.11) | copy-start | bytes 1540
  34.0 23.0 %collective-permute-start.1 = (bf16[16,48,128]{2,1,0:T(8,128)(2,1)S(1)}, bf16[16,48,128]{2,1,0:T(8,128)(2,1)S(1)}, u32[]{:S(2)}, u32[]{:S(2)}) collective-permute-start(bf16[16,48,128]{2,1,0:T(8,128)(2,1)S(1)} %copy-done.8), channel_id=1, source_target_pairs={{0,2},{1,3},{2,4},{3,5},{4,6},{5,7},{6,8},{7,9},{8,10},{9,11},{10,... | collective-permute-start | bytes 589832 | tf_op jit(solution)/shard_map/ppermute | solution.py:540
  36.5 20.6 %collective-permute-start.2 = (bf16[16,48,128]{2,1,0:T(8,128)(2,1)S(1)}, bf16[16,48,128]{2,1,0:T(8,128)(2,1)S(1)}, u32[]{:S(2)}, u32[]{:S(2)}) collective-permute-start(bf16[16,48,128]{2,1,0:T(8,128)(2,1)S(1)} %copy-done.8), channel_id=1, source_target_pairs={{0,3},{1,2},{2,5},{3,4},{4,7},{5,6},{6,9},{7,8},{8,11},{9,10},{10,... | collective-permute-start | bytes 589832 | tf_op jit(solution)/shard_map/ppermute | solution.py:541
  38.5 18.6 %collective-permute-start.3 = (bf16[16,48,128]{2,1,0:T(8,128)(2,1)S(1)}, bf16[16,48,128]{2,1,0:T(8,128)(2,1)S(1)}, u32[]{:S(2)}, u32[]{:S(2)}) collective-permute-start(bf16[16,48,128]{2,1,0:T(8,128)(2,1)S(1)} %copy-done.7), channel_id=1, source_target_pairs={{2,0},{3,1},{4,2},{5,3},{6,4},{7,5},{8,6},{9,7},{10,8},{11,9},{12,... | collective-permute-start | bytes 589832 | tf_op jit(solution)/shard_map/ppermute | solution.py:542
  43.9 13.2 %collective-permute-start.4 = (bf16[16,48,128]{2,1,0:T(8,128)(2,1)S(1)}, bf16[16,48,128]{2,1,0:T(8,128)(2,1)S(1)}, u32[]{:S(2)}, u32[]{:S(2)}) collective-permute-start(bf16[16,48,128]{2,1,0:T(8,128)(2,1)S(1)} %copy-done.7), channel_id=1, source_target_pairs={{3,0},{2,1},{5,2},{4,3},{7,4},{6,5},{9,6},{8,7},{11,8},{10,9},{13,... | collective-permute-start | bytes 589832 | tf_op jit(solution)/shard_map/ppermute | solution.py:543
  61.6 30.3 %all-to-all-start.1 = ((bf16[16,216,256]{2,1,0:T(8,128)(2,1)}), bf16[16,216,256]{2,1,0:T(8,128)(2,1)S(1)}, u32[]{:S(2)}, u32[]{:S(2)}) async-start(bf16[16,216,256]{2,1,0:T(8,128)(2,1)} %bitcast.40), calls=%async_computation.1 | async-start | bytes 3538944 | tf_op jit(solution)/shard_map/all_to_all | solution.py:603
  106.2 12.4 %all-to-all-start.3 = ((bf16[8,27,256]{2,1,0:T(8,128)(2,1)}), bf16[8,27,256]{2,1,0:T(8,128)(2,1)S(1)}, u32[]{:S(2)}, u32[]{:S(2)}) async-start(bf16[8,27,256]{2,1,0:T(8,128)(2,1)} %broadcast_in_dim.24), calls=%async_computation.3 | async-start | bytes 262144 | tf_op jit(solution)/shard_map/all_to_all | solution.py:634
  118.9 26.1 %copy-start.1 = (bf16[48,64,128]{2,1,0:T(8,128)(2,1)S(1)}, bf16[48,64,128]{2,1,0:T(8,128)(2,1)}, u32[]{:S(2)}) copy-start(bf16[48,64,128]{2,1,0:T(8,128)(2,1)} %param.8) | copy-start | bytes 2359300
  118.9 26.1 %copy-start.2 = (f32[64,48,128]{2,1,0:T(8,128)S(1)}, f32[64,48,128]{2,1,0:T(8,128)}, u32[]{:S(2)}) copy-start(f32[64,48,128]{2,1,0:T(8,128)} %get-tuple-element.36) | copy-start | bytes 4718596

commit v4 on v3

--- a/solution.py
+++ b/solution.py
@@ -70,13 +70,17 @@
         rows_ref[rows, :] = held_ref[rows, :].astype(F32)
 
 
-def turn_kernel(in_hbm, own_hbm, low_hbm, high_hbm, held_ref, rows_ref, own_ref, sems, out_sems):
-    widen(fetch(in_hbm, held_ref, sems, 4), held_ref, rows_ref)
+def turn_kernel(
+    core_ref, in_hbm, own_hbm, give_hbm, keep_hbm, held_ref, rows_ref, own_ref, sems, out_sems
+):
+    copies = fetch(in_hbm, held_ref, sems, 4)
+    core = core_ref[0]
+    widen(copies, held_ref, rows_ref)
     turned(rows_ref, own_ref)
     sends = [
-        pltpu.make_async_copy(own_ref, own_hbm, out_sems.at[0]),
-        pltpu.make_async_copy(own_ref.at[0:16], low_hbm, out_sems.at[1]),
-        pltpu.make_async_copy(own_ref.at[48:64], high_hbm, out_sems.at[2]),
+        pltpu.make_async_copy(own_ref.at[pl.ds(48 * core, 16)], give_hbm, out_sems.at[0]),
+        pltpu.make_async_copy(own_ref.at[pl.ds(48 - 48 * core, 16)], keep_hbm, out_sems.at[1]),
+        pltpu.make_async_copy(own_ref, own_hbm, out_sems.at[2]),
     ]
     for send in sends:
         send.start()
@@ -188,24 +192,28 @@
     shift_ref,
     values_hbm,
     middle_hbm,
+    sides_hbm,
     out_hbm,
-    part_hbm,
-    edge_ref,
     norm_ref,
     held_ref,
     rows_ref,
-    middle_ref,
+    grid_ref,
     act_ref,
     total_ref,
     out_ref,
-    part_ref,
     sems,
     plane_sems,
     out_sems,
 ):
-    slots = middle_ref.shape[3]
+    slots = grid_ref.shape[3]
     copies = fetch(values_hbm, held_ref, sems, 4)
-    planes = fetch(middle_hbm, middle_ref, plane_sems, 4)
+    sources = [sides_hbm.at[0]] + [middle_hbm.at[at] for at in range(4)] + [sides_hbm.at[1]]
+    planes = [
+        pltpu.make_async_copy(place, grid_ref.at[at], plane_sems.at[at])
+        for at, place in enumerate(sources)
+    ]
+    for plane in planes:
+        plane.start()
     table = table_ref[...]
     held = jnp.sum(table, axis=0)
     voxels = held[:, 32:33] * (64.0 * GROUP_CH)
@@ -238,18 +246,16 @@
             pieces.append(jnp.where(live, pre / (1.0 + jnp.exp(-pre)), 0.0))
         rows = jnp.concatenate(pieces, axis=0)
         act_ref[plane * 128 : plane * 128 + 128, :] = rows.T.astype(BF16)
-    edge_ref[0] = act_ref[0:128, :]
-    edge_ref[1] = act_ref[384:512, :]
     sends = []
     for turn in range(9):
         seen = set()
-        for plane in range(1, 5):
+        for plane in range(6):
             if turn == 0:
-                planes[plane - 1].wait()
+                planes[plane].wait()
             first, last = planes_of(plane)
             part = jnp.dot(
                 act_ref[first * 128 : last * 128, :],
-                window(middle_ref.at[plane - 1], turn),
+                window(grid_ref.at[plane], turn),
                 preferred_element_type=F32,
             )
             for at in range(first, last):
@@ -260,16 +266,14 @@
                 else:
                     total_ref[step] = term
                     seen.add(step)
-        out_ref[turn] = total_ref[1].astype(BF16)
-        part_ref[0, turn] = total_ref[0]
-        part_ref[1, turn] = total_ref[2]
-        sends += [
-            pltpu.make_async_copy(out_ref.at[turn], out_hbm.at[1, turn], out_sems.at[0, turn]),
-            pltpu.make_async_copy(part_ref.at[0, turn], part_hbm.at[0, turn], out_sems.at[1, turn]),
-            pltpu.make_async_copy(part_ref.at[1, turn], part_hbm.at[1, turn], out_sems.at[2, turn]),
-        ]
-        for send in sends[-3:]:
-            send.start()
+        for step in range(3):
+            out_ref[step, turn] = total_ref[step].astype(BF16)
+            sends.append(
+                pltpu.make_async_copy(
+                    out_ref.at[step, turn], out_hbm.at[step, turn], out_sems.at[step, turn]
+                )
+            )
+            sends[-1].start()
     for send in sends:
         send.wait()
 
@@ -277,44 +281,30 @@
 def edge_kernel(
     core_ref,
     near_ref,
-    edge_ref,
-    before_ref,
-    before_other_ref,
-    after_ref,
-    after_other_ref,
+    received_ref,
+    theirs_ref,
     middle_hbm,
-    part_hbm,
-    in_hbm,
-    out_hbm,
     sides_hbm,
     face_ref,
     inner_ref,
     sides_ref,
-    part_ref,
-    out_ref,
     sems,
-    part_sems,
-    out_sems,
     side_sems,
 ):
     slots = near_ref.shape[0]
-    mine, other = lanes_of(core_ref[0])
+    core = core_ref[0]
+    mine, other = lanes_of(core)
+    near_face, far_face = face_ref.at[core], face_ref.at[1 - core]
     copies = [
-        pltpu.make_async_copy(before_ref, face_ref.at[0, :, :, :, mine], sems.at[0]),
-        pltpu.make_async_copy(before_other_ref, face_ref.at[0, :, :, :, other], sems.at[1]),
-        pltpu.make_async_copy(after_ref, face_ref.at[1, :, :, :, mine], sems.at[2]),
-        pltpu.make_async_copy(after_other_ref, face_ref.at[1, :, :, :, other], sems.at[3]),
+        pltpu.make_async_copy(received_ref.at[0], near_face.at[:, :, :, mine], sems.at[0]),
+        pltpu.make_async_copy(received_ref.at[1], near_face.at[:, :, :, other], sems.at[1]),
+        pltpu.make_async_copy(theirs_ref.at[0], far_face.at[:, :, :, other], sems.at[2]),
+        pltpu.make_async_copy(theirs_ref.at[1], far_face.at[:, :, :, mine], sems.at[3]),
         pltpu.make_async_copy(middle_hbm.at[3, 1:5, 1:5], inner_ref.at[0], sems.at[4]),
         pltpu.make_async_copy(middle_hbm.at[0, 1:5, 1:5], inner_ref.at[1], sems.at[5]),
     ]
     for copy in copies:
         copy.start()
-    parts = [
-        pltpu.make_async_copy(part_hbm.at[which], part_ref.at[which], part_sems.at[which])
-        for which in range(2)
-    ]
-    for part in parts:
-        part.start()
     near = near_ref[...]
     places = [(b, c) for b in range(6) for c in range(6)]
     sends = []
@@ -340,21 +330,6 @@
             pltpu.make_async_copy(sides_ref.at[which], sides_hbm.at[which], side_sems.at[which])
         )
         sends[-1].start()
-        parts[which].wait()
-    for turn in range(9):
-        for which in range(2):
-            term = jnp.dot(
-                edge_ref[which], window(sides_ref.at[which], turn), preferred_element_type=F32
-            )
-            out_ref[1 - which, turn] = (part_ref[1 - which, turn] + term).astype(BF16)
-            sends.append(
-                pltpu.make_async_copy(
-                    out_ref.at[1 - which, turn],
-                    out_hbm.at[2 - 2 * which, turn],
-                    out_sems.at[which, turn],
-                )
-            )
-            sends[-1].start()
     for send in sends:
         send.wait()
 
@@ -500,10 +475,10 @@
         mib=60,
     )(counts, value_rows)
     table = lax.all_to_all(sent, SLABS, 0, 0, tiled=True)
-    own, low, high = call(
+    own, give, keep = call(
         turn_kernel,
         [turned_shape, face_shape, face_shape],
-        [HBM],
+        [SMEM, HBM],
         [
             pltpu.VMEM((rows, width), BF16),
             pltpu.VMEM((rows, width), F32),
@@ -513,8 +488,13 @@
         ],
         [HBM] * 3,
         mib=60,
-    )(cotangent_rows)
-    own_other = lax.ppermute(own, "ch", [(0, 1), (1, 0)])
+    )(core, cotangent_rows)
+    cores = [(0, 1), (1, 0)]
+    ups = [(i, i + 1) for i in range(n_slab - 1)]
+    outward = [(2 * i, 2 * j) for i, j in ups] + [(2 * j + 1, 2 * i + 1) for i, j in ups]
+    sent_planes = jnp.stack([keep, lax.ppermute(give, "ch", cores)])
+    own_other = lax.ppermute(own, "ch", cores)
+    received = lax.ppermute(sent_planes, SLABS + ("ch",), outward)
 
     cube = (4, 4, 4, slots, width)
     face = (4, 4, slots, width)
@@ -532,73 +512,42 @@
         flops=10**9,
     )(core, neighbours, own.reshape(cube), own_other.reshape(cube))
 
-    table, middle, low, high = lax.optimization_barrier((table, middle, low, high))
-    every = SLABS + ("ch",)
-    ups = [(i, i + 1) for i in range(n_slab - 1)]
-    straight = [(2 * i + c, 2 * j + c) for i, j in ups for c in range(2)]
-    across = [(2 * i + c, 2 * j + 1 - c) for i, j in ups for c in range(2)]
-    before = lax.ppermute(high, every, straight)
-    before_other = lax.ppermute(high, every, across)
-    after = lax.ppermute(low, every, [(j, i) for i, j in straight])
-    after_other = lax.ppermute(low, every, [(j, i) for i, j in across])
-
-    term_shape = jax.ShapeDtypeStruct((3, 9, width, 2 * width), BF16)
-    part_shape = jax.ShapeDtypeStruct((2, 9, width, 2 * width), F32)
-    weight_term, part_term, edge, norm = call(
-        weight_grad_kernel,
-        [
-            term_shape,
-            part_shape,
-            jax.ShapeDtypeStruct((2, width, 16 * slots), BF16),
-            jax.ShapeDtypeStruct((8, 128), F32),
-        ],
-        [SMEM, VMEM, VMEM, VMEM, HBM, HBM],
-        [
-            pltpu.VMEM((rows, width), BF16),
-            pltpu.VMEM((rows, width), F32),
-            pltpu.VMEM(middle_shape, BF16),
-            pltpu.VMEM((4 * width, 16 * slots), BF16),
-            pltpu.VMEM((3, width, 2 * width), F32),
-            pltpu.VMEM((9, width, 2 * width), BF16),
-            pltpu.VMEM(part_shape.shape, F32),
-            pltpu.SemaphoreType.DMA((4,)),
-            pltpu.SemaphoreType.DMA((4,)),
-            pltpu.SemaphoreType.DMA((3, 9)),
-        ],
-        [HBM, HBM, VMEM, VMEM],
-        flops=work,
-    )(counts, table, gain_row, shift_row, value_rows, middle)
+    middle, received = lax.optimization_barrier((middle, received))
+    theirs = lax.ppermute(received, "ch", cores)
     sides_shape = jax.ShapeDtypeStruct((2, 6, 6, slots, 2 * width), BF16)
-    weight_term, sides = call(
+    sides = call(
         edge_kernel,
-        [term_shape, sides_shape],
-        [SMEM, VMEM, VMEM] + [ANY] * 4 + [HBM] * 3,
+        sides_shape,
+        [SMEM, VMEM, ANY, ANY, HBM],
         [
             pltpu.VMEM((2, 4, 4, slots, 2 * width), BF16),
             pltpu.VMEM((2, 4, 4, slots, 2 * width), BF16),
             pltpu.VMEM(sides_shape.shape, BF16),
-            pltpu.VMEM(part_shape.shape, F32),
-            pltpu.VMEM((2, 9, width, 2 * width), BF16),
             pltpu.SemaphoreType.DMA((6,)),
             pltpu.SemaphoreType.DMA((2,)),
-            pltpu.SemaphoreType.DMA((2, 9)),
-            pltpu.SemaphoreType.DMA((2,)),
-        ],
-        [HBM, HBM],
-        aliases={9: 0},
-        flops=work // 6,
-    )(
-        core,
-        neighbours,
-        edge,
-        before.reshape(face),
-        before_other.reshape(face),
-        after.reshape(face),
-        after_other.reshape(face),
-        middle,
-        part_term,
-        weight_term,
-    )
+        ],
+        HBM,
+    )(core, neighbours, received.reshape((2,) + face), theirs.reshape((2,) + face), middle)
+
+    term_shape = jax.ShapeDtypeStruct((3, 9, width, 2 * width), BF16)
+    weight_term, norm = call(
+        weight_grad_kernel,
+        [term_shape, jax.ShapeDtypeStruct((8, 128), F32)],
+        [SMEM, VMEM, VMEM, VMEM, HBM, HBM, HBM],
+        [
+            pltpu.VMEM((rows, width), BF16),
+            pltpu.VMEM((rows, width), F32),
+            pltpu.VMEM((6, 6, 6, slots, 2 * width), BF16),
+            pltpu.VMEM((4 * width, 16 * slots), BF16),
+            pltpu.VMEM((3, width, 2 * width), F32),
+            pltpu.VMEM(term_shape.shape, BF16),
+            pltpu.SemaphoreType.DMA((4,)),
+            pltpu.SemaphoreType.DMA((6,)),
+            pltpu.SemaphoreType.DMA((3, 9)),
+        ],
+        [HBM, VMEM],
+        flops=work,
+    )(counts, table, gain_row, shift_row, value_rows, middle, sides)
     piece = 27 * width // n_plane
     parts = lax.all_to_all(
         weight_term.reshape(n_plane, piece, 2 * width), PLANE, 0, 0, tiled=True

time: 148 us -> 144 us (0.973)
  starting transfers between devices: 38.8 us -> 28.5 us
  waiting for transfers between devices: 25.4 us -> 30.4 us
    ppermute x5 -> x4, starting transfers between devices: 13.5 us -> 4.08 us  [the longest x1 3.48 us: body(): received = lax.ppermute(sent_planes, SLABS + ('ch',), outward)]
    ppermute x5 -> x4, waiting for transfers between devices: 0.01 us -> 6.11 us  [the longest x1 3.84 us: body(): received = lax.ppermute(sent_planes, SLABS + ('ch',), outward)]
    all_to_all x1, waiting for transfers between devices: 8.8 us -> 7.12 us  [body(): lax.all_to_all(weight_term.reshape(n_plane, piece, 2 * width), PLANE, 0,...]
    all_to_all x1, starting transfers between devices: 6.45 us -> 4.97 us  [body(): lax.all_to_all(weight_term.reshape(n_plane, piece, 2 * width), PLANE, 0,...]
  transfers between devices with their start and end apart: 8 -> 7, of which waited for: 3 -> 5; matrix products, arithmetic and copies ran while one was open for 0% -> 1% of each run, Pallas kernels for 20% -> 16%
where the time goes in v4:
time: 144 us; the launch traced here: 143 us
  Pallas kernels  39.9 us (28%)
  blocking collectives  38.5 us (27%)
  waiting for transfers between devices  30.4 us (21%)
  starting transfers between devices  28.5 us (20%)
  local copies, waits for them, and re-layouts  3.44 us (2%)
  between operations  1.49 us (1%)
    all_to_all x1, blocking collectives, body(): plane = lax.all_to_all(plane, PLANE, 0, 0, tiled=True)  25.6 us
    all_to_all x1, starting transfers between devices, body(): table = lax.all_to_all(sent, SLABS, 0, 0, tiled=True)  16.1 us
    pallas_call x1, Pallas kernels, body(): call(act_grad_kernel, [jax.ShapeDtypeStruct((voxels, slots, width), F32),...  15.3 us
    all_to_all x1, blocking collectives, body(): part = jnp.sum(lax.all_to_all(part, 'z', 0, 0, tiled=True), axis=0)  12.9 us
    pallas_call x1, Pallas kernels, body(): call(weight_grad_kernel, [term_shape, jax.ShapeDtypeStruct((8, 128), F32)...  10.9 us
    all_to_all x1, waiting for transfers between devices, body(): line = lax.all_to_all(line, 'z', 0, 0, tiled=True).reshape(piece, 2 * width)  8.98 us
    all_to_all x1, waiting for transfers between devices, body(): table = lax.all_to_all(sent, SLABS, 0, 0, tiled=True)  8.18 us
    all_to_all x1, waiting for transfers between devices, body(): lax.all_to_all(weight_term.reshape(n_plane, piece, 2 * width), PLANE, 0,...  7.12 us
  transfers between devices with their start and end apart: 7, of which 5 were waited for; matrix products, arithmetic and copies ran while one was open for 1% of the time, Pallas kernels for 16%

profile of v4, /device:TPU:2, one launch (start us, length us, event | category | flops | bytes accessed | tf_op | source)
XLA Modules:
  0.0 143.5 jit_solution(1178188499321338809)
XLA Ops:
  0.6 3.2 %shard_map.103 = (bf16[64,48,128]{2,1,0:T(8,128)(2,1)}, bf16[16,48,128]{2,1,0:T(8,128)(2,1)}, bf16[16,48,128]{2,1,0:T(8,128)(2,1)}) custom-call(s32[1]{0:T(128)} %bitcast.3.core_ref, bf16[3072,128]{1,0:T(8,128)(2,1)} %bitcast.25), custom_call_target="tpu_custom_call" | custom-call | tf_op jit(solution)/shard_map/pallas_call | solution.py:478
  3.8 0.1 collective-permute-start
  3.9 0.5 collective-permute-start.1
  4.4 2.3 %collective-permute-done.1 = bf16[16,48,128]{2,1,0:T(8,128)(2,1)S(1)} collective-permute-done((bf16[16,48,128]{2,1,0:T(8,128)(2,1)}, bf16[16,48,128]{2,1,0:T(8,128)(2,1)S(1)}, u32[]{:S(2)}, u32[]{:S(2)}) %collective-permute-start.1) | collective-permute-done | bytes 196640 | tf_op jit(solution)/shard_map/ppermute | solution.py:495
  6.7 1.0 pad_maximum_fusion
  7.7 3.5 %collective-permute-start.2 = (bf16[2,16,48,128]{3,2,1,0:T(8,128)(2,1)S(1)}, bf16[2,16,48,128]{3,2,1,0:T(8,128)(2,1)S(1)}, u32[]{:S(2)}, u32[]{:S(2)}) collective-permute-start(bf16[2,16,48,128]{3,2,1,0:T(8,128)(2,1)S(1)} %pad_maximum_fusion), channel_id=1, source_target_pairs={{0,2},{2,4},{4,6},{6,8},{8,10},{10,12},{12,14},{14,16},{16,18},{18... | collective-permute-start | bytes 1179656 | tf_op jit(solution)/shard_map/ppermute | solution.py:497
  11.2 0.8 copy.13.near_ref
  11.9 0.0 collective-permute-done
  12.0 0.0 copy-start.3
  12.0 1.1 copy-done.3
  13.1 2.5 %shard_map.104.middle_hbm.middle_ref = bf16[4,6,6,48,256]{4,3,2,1,0:T(8,128)(2,1)} custom-call(s32[1]{0:T(128)} %bitcast.3.core_ref, s32[48,27]{1,0:T(8,128)S(1)} %copy.13.near_ref, bf16[4,4,4,48,128]{4,3,2,1,0:T(8,128)(2,1)S(1)} %bitcast.28, bf16[4,4,4,48,128]{4,3,2,1,0:T(8,128)(2,1)S(1)} %bitcast.29), custom_call_target="tpu_custom_call" | custom-call | flops 1000000000 | tf_op jit(solution)/shard_map/pallas_call | solution.py:502
  15.6 3.8 %collective-permute-done.2 = bf16[2,16,48,128]{3,2,1,0:T(8,128)(2,1)S(1)} collective-permute-done((bf16[2,16,48,128]{3,2,1,0:T(8,128)(2,1)S(1)}, bf16[2,16,48,128]{3,2,1,0:T(8,128)(2,1)S(1)}, u32[]{:S(2)}, u32[]{:S(2)}) %collective-permute-start.2) | collective-permute-done | bytes 393248 | tf_op jit(solution)/shard_map/ppermute | solution.py:497
  19.4 0.0 collective-permute-start.3
  20.1 2.7 %shard_map.102 = f32[128,1,128]{2,1,0:T(1,128)} custom-call(s32[1]{0:T(128)S(6)} %copy.15.counts_ref, bf16[3072,128]{1,0:T(8,128)(2,1)} %bitcast.21), custom_call_target="tpu_custom_call" | custom-call | tf_op jit(solution)/shard_map/pallas_call | solution.py:466
  22.8 16.1 %all-to-all-start = ((f32[128,1,128]{2,1,0:T(1,128)}), f32[128,1,128]{2,1,0:T(1,128)S(1)}, u32[]{:S(2)}, u32[]{:S(2)}) async-start(f32[128,1,128]{2,1,0:T(1,128)} %shard_map.102), calls=%async_computation | async-start | bytes 131072 | tf_op jit(solution)/shard_map/all_to_all | solution.py:477
  38.9 0.0 collective-permute-done.3
  38.9 0.0 copy-start
  38.9 0.0 copy-start.4
  38.9 0.0 copy-start.5
  38.9 3.0 %shard_map.105.sides_hbm.sides_ref = bf16[2,6,6,48,256]{4,3,2,1,0:T(8,128)(2,1)} custom-call(s32[1]{0:T(128)} %bitcast.3.core_ref, s32[48,27]{1,0:T(8,128)S(1)} %copy.13.near_ref, bf16[2,4,4,48,128]{4,3,2,1,0:T(8,128)(2,1)S(1)} %bitcast.30, bf16[2,4,4,48,128]{4,3,2,1,0:T(8,128)(2,1)S(1)} %bitcast.31, bf16[4,6,6,48,256]{4,3,2,1,0:T(8,128)(2,1)} %shard_map.104.middle_hbm.middle_ref), custom_call_target="tpu_custom_call" | custom-call | tf_op jit(solution)/shard_map/pallas_call | solution.py:518
  42.0 8.2 %all-to-all-done.table_ref = f32[128,1,128]{2,1,0:T(1,128)S(1)} async-done(((f32[128,1,128]{2,1,0:T(1,128)}), f32[128,1,128]{2,1,0:T(1,128)S(1)}, u32[]{:S(2)}, u32[]{:S(2)}) %all-to-all-start) | async-done | bytes 65568 | tf_op jit(solution)/shard_map/all_to_all | solution.py:477
  50.2 0.0 copy-done
  50.2 0.0 copy-done.4
  50.2 0.0 copy-done.5
  50.2 10.9 %shard_map.106 = (bf16[3,9,128,256]{3,2,1,0:T(8,128)(2,1)}, f32[8,128]{1,0:T(8,128)S(1)}) custom-call(s32[1]{0:T(128)S(6)} %copy.15.counts_ref, f32[128,1,128]{2,1,0:T(1,128)S(1)} %all-to-all-done.table_ref, f32[1,128]{1,0:T(1,128)S(1)} %bitcast.33, f32[1,128]{1,0:T(1,128)S(1)} %bitcast.36, bf16[3072,128]{1,0:T(8,128)(2,1)S(1)} %bitcast.22, ...), custom_call_target="tpu_custom_call" | custom-call | flops 5435817984 | tf_op jit(solution)/shard_map/pallas_call | solution.py:533
  61.1 5.0 %all-to-all-start.1 = ((bf16[16,216,256]{2,1,0:T(8,128)(2,1)}), bf16[16,216,256]{2,1,0:T(8,128)(2,1)S(1)}, u32[]{:S(2)}, u32[]{:S(2)}) async-start(bf16[16,216,256]{2,1,0:T(8,128)(2,1)} %bitcast.38), calls=%async_computation.1 | async-start | bytes 3538944 | tf_op jit(solution)/shard_map/all_to_all | solution.py:552
  66.1 15.3 %shard_map.107 = (f32[64,48,128]{2,1,0:T(8,128)}, f32[1,256]{1,0:T(1,128)S(1)}) custom-call(s32[1]{0:T(128)S(6)} %copy.15.counts_ref, f32[8,128]{1,0:T(8,128)S(1)} %get-tuple-element.21.norm_ref, f32[1,128]{1,0:T(1,128)S(1)} %bitcast.34, f32[1,128]{1,0:T(1,128)S(1)} %bitcast.37, bf16[3072,128]{1,0:T(8,128)(2,1)S(1)} %bitcast.23, ...), custom_call_target="tpu_custom_call" | custom-call | flops 5435817984 | tf_op jit(solution)/shard_map/pallas_call | solution.py:556
  81.4 7.1 %all-to-all-done.1 = bf16[16,216,256]{2,1,0:T(8,128)(2,1)S(1)} async-done(((bf16[16,216,256]{2,1,0:T(8,128)(2,1)}), bf16[16,216,256]{2,1,0:T(8,128)(2,1)S(1)}, u32[]{:S(2)}, u32[]{:S(2)}) %all-to-all-start.1) | async-done | bytes 1769504 | tf_op jit(solution)/shard_map/all_to_all | solution.py:552
  88.5 0.3 convert_reduce_fusion
  88.8 12.9 %all_to_all.25 = f32[8,28,256]{2,1,0:T(8,128)S(1)} all-to-all(f32[8,28,256]{2,1,0:T(8,128)S(1)} %pad_maximum_fusion.1), channel_id=1, replica_groups=mesh['z'=8,'x'=4,'y'=4,'ch'=2] {'z'}, dimensions={0} | all-to-all | bytes 458752 | tf_op jit(solution)/shard_map/all_to_all | solution.py:580
  101.7 0.7 broadcast_in_dim.24
  102.4 3.4 %all-to-all-start.3 = ((bf16[8,27,256]{2,1,0:T(8,128)(2,1)}), bf16[8,27,256]{2,1,0:T(8,128)(2,1)S(1)}, u32[]{:S(2)}, u32[]{:S(2)}) async-start(bf16[8,27,256]{2,1,0:T(8,128)(2,1)} %broadcast_in_dim.24), calls=%async_computation.3 | async-start | bytes 262144 | tf_op jit(solution)/shard_map/all_to_all | solution.py:583
  105.8 9.0 %all-to-all-done.3 = bf16[8,27,256]{2,1,0:T(8,128)(2,1)S(1)} async-done(((bf16[8,27,256]{2,1,0:T(8,128)(2,1)}), bf16[8,27,256]{2,1,0:T(8,128)(2,1)S(1)}, u32[]{:S(2)}, u32[]{:S(2)}) %all-to-all-start.3) | async-done | bytes 110624 | tf_op jit(solution)/shard_map/all_to_all | solution.py:583
  114.8 0.1 reshape.74
  114.9 0.2 broadcast_in_dim.26
  115.1 0.0 copy-start.1
  115.1 0.0 copy-start.2
  115.1 25.6 %all_to_all.26.plane_ref = bf16[16,224,256]{2,1,0:T(8,128)(2,1)S(1)} all-to-all(bf16[16,224,256]{2,1,0:T(8,128)(2,1)S(1)} %broadcast_in_dim.26), channel_id=1, replica_groups=mesh['z'=8,'x'=4,'y'=4,'ch'=2] {'x','y'}, dimensions={0} | all-to-all | bytes 3670016 | tf_op jit(solution)/shard_map/all_to_all | solution.py:592
  140.7 0.0 copy-done.1
  140.7 0.0 copy-done.2
  140.7 2.3 %shard_map.108 = (bf16[3072,128]{1,0:T(8,128)(2,1)}, f32[3456,256]{1,0:T(8,128)}, f32[2,128]{1,0:T(2,128)S(1)}) custom-call(s32[1]{0:T(128)S(6)} %copy.15.counts_ref, f32[8,128]{1,0:T(8,128)S(1)} %get-tuple-element.21.norm_ref, f32[1,128]{1,0:T(1,128)S(1)} %bitcast.35, bf16[16,224,256]{2,1,0:T(8,128)(2,1)S(1)} %all_to_all.26.plane_ref, ...), custom_call_target="tpu_custom_call" | custom-call | tf_op jit(solution)/shard_map/pallas_call | solution.py:593
  143.0 0.5 slice_bitcast_fusion
  (8 shorter events, 0.1 us)
Async XLA Ops:
  3.8 8.1 %collective-permute-start = (bf16[64,48,128]{2,1,0:T(8,128)(2,1)}, bf16[64,48,128]{2,1,0:T(8,128)(2,1)S(1)}, u32[]{:S(2)}, u32[]{:S(2)}) collective-permute-start(bf16[64,48,128]{2,1,0:T(8,128)(2,1)} %get-tuple-element.16), channel_id=1, source_target_pairs={{0,1},{1,0},{2,3},{3,2},{4,5},{5,4},{6,7},{7,6},{8,9},{9,8},{10,11... | collective-permute-start | bytes 2359304 | tf_op jit(solution)/shard_map/ppermute | solution.py:496
  3.9 2.8 %collective-permute-start.1 = (bf16[16,48,128]{2,1,0:T(8,128)(2,1)}, bf16[16,48,128]{2,1,0:T(8,128)(2,1)S(1)}, u32[]{:S(2)}, u32[]{:S(2)}) collective-permute-start(bf16[16,48,128]{2,1,0:T(8,128)(2,1)} %get-tuple-element.18), channel_id=1, source_target_pairs={{0,1},{1,0},{2,3},{3,2},{4,5},{5,4},{6,7},{7,6},{8,9},{9,8},{10,11... | collective-permute-start | bytes 589832 | tf_op jit(solution)/shard_map/ppermute | solution.py:495
  7.7 11.8 %collective-permute-start.2 = (bf16[2,16,48,128]{3,2,1,0:T(8,128)(2,1)S(1)}, bf16[2,16,48,128]{3,2,1,0:T(8,128)(2,1)S(1)}, u32[]{:S(2)}, u32[]{:S(2)}) collective-permute-start(bf16[2,16,48,128]{3,2,1,0:T(8,128)(2,1)S(1)} %pad_maximum_fusion), channel_id=1, source_target_pairs={{0,2},{2,4},{4,6},{6,8},{8,10},{10,12},{12,14},{14,16},{16,18},{18... | collective-permute-start | bytes 1179656 | tf_op jit(solution)/shard_map/ppermute | solution.py:497
  12.0 1.1 copy-start.3
  19.4 19.5 %collective-permute-start.3 = (bf16[2,16,48,128]{3,2,1,0:T(8,128)(2,1)S(1)}, bf16[2,16,48,128]{3,2,1,0:T(8,128)(2,1)S(1)}, u32[]{:S(2)}, u32[]{:S(2)}) collective-permute-start(bf16[2,16,48,128]{3,2,1,0:T(8,128)(2,1)S(1)} %collective-permute-done.2), channel_id=1, source_target_pairs={{0,1},{1,0},{2,3},{3,2},{4,5},{5,4},{6,7},{7,6},{8,9},{9,8},{10,11... | collective-permute-start | bytes 1179656 | tf_op jit(solution)/shard_map/ppermute | solution.py:516
  22.8 27.4 %all-to-all-start = ((f32[128,1,128]{2,1,0:T(1,128)}), f32[128,1,128]{2,1,0:T(1,128)S(1)}, u32[]{:S(2)}, u32[]{:S(2)}) async-start(f32[128,1,128]{2,1,0:T(1,128)} %shard_map.102), calls=%async_computation | async-start | bytes 131072 | tf_op jit(solution)/shard_map/all_to_all | solution.py:477
  38.9 11.3 %copy-start = (bf16[48,64,128]{2,1,0:T(8,128)(2,1)S(1)}, bf16[48,64,128]{2,1,0:T(8,128)(2,1)}, u32[]{:S(2)}) copy-start(bf16[48,64,128]{2,1,0:T(8,128)(2,1)} %param.7) | copy-start | bytes 2359300
  38.9 11.3 %copy-start.4 = (f32[128]{0:T(128)S(1)}, f32[128]{0:T(128)}, u32[]{:S(2)}) copy-start(f32[128]{0:T(128)} %param.10) | copy-start | bytes 1540
  38.9 11.2 %copy-start.5 = (f32[128]{0:T(128)S(1)}, f32[128]{0:T(128)}, u32[]{:S(2)}) copy-start(f32[128]{0:T(128)} %param.11) | copy-start | bytes 1540
  61.1 27.4 %all-to-all-start.1 = ((bf16[16,216,256]{2,1,0:T(8,128)(2,1)}), bf16[16,216,256]{2,1,0:T(8,128)(2,1)S(1)}, u32[]{:S(2)}, u32[]{:S(2)}) async-start(bf16[16,216,256]{2,1,0:T(8,128)(2,1)} %bitcast.38), calls=%async_computation.1 | async-start | bytes 3538944 | tf_op jit(solution)/shard_map/all_to_all | solution.py:552
  102.4 12.4 %all-to-all-start.3 = ((bf16[8,27,256]{2,1,0:T(8,128)(2,1)}), bf16[8,27,256]{2,1,0:T(8,128)(2,1)S(1)}, u32[]{:S(2)}, u32[]{:S(2)}) async-start(bf16[8,27,256]{2,1,0:T(8,128)(2,1)} %broadcast_in_dim.24), calls=%async_computation.3 | async-start | bytes 262144 | tf_op jit(solution)/shard_map/all_to_all | solution.py:583
  115.1 25.6 %copy-start.1 = (bf16[48,64,128]{2,1,0:T(8,128)(2,1)S(1)}, bf16[48,64,128]{2,1,0:T(8,128)(2,1)}, u32[]{:S(2)}) copy-start(bf16[48,64,128]{2,1,0:T(8,128)(2,1)} %param.8) | copy-start | bytes 2359300
  115.1 25.6 %copy-start.2 = (f32[64,48,128]{2,1,0:T(8,128)S(1)}, f32[64,48,128]{2,1,0:T(8,128)}, u32[]{:S(2)}) copy-start(f32[64,48,128]{2,1,0:T(8,128)} %get-tuple-element.24) | copy-start | bytes 4718596

commit v5 on v4

--- a/solution.py
+++ b/solution.py
@@ -141,7 +141,7 @@
     return (near[:, offset : offset + 1] == columns).astype(F32).astype(BF16)
 
 
-def halo_kernel(core_ref, near_ref, own_ref, own_other_ref, middle_hbm, middle_ref, sems, out_sems):
+def halo_kernel(core_ref, near_ref, own_ref, own_other_ref, middle_ref, sems):
     slots = near_ref.shape[0]
     mine, other = lanes_of(core_ref[0])
     centre = middle_ref.at[:, 1:5, 1:5]
@@ -159,7 +159,6 @@
     }
     for copy in copies:
         copy.wait()
-    sends = []
     for plane in range(4):
         for b, c in places:
             middle_ref[plane, b, c] = jnp.dot(
@@ -167,12 +166,6 @@
                 middle_ref[plane, source(b), source(c)],
                 preferred_element_type=F32,
             ).astype(BF16)
-        sends.append(
-            pltpu.make_async_copy(middle_ref.at[plane], middle_hbm.at[plane], out_sems.at[plane])
-        )
-        sends[-1].start()
-    for send in sends:
-        send.wait()
 
 
 def window(plane_ref, turn):
@@ -187,33 +180,43 @@
 
 def weight_grad_kernel(
     counts_ref,
+    core_ref,
+    near_ref,
     table_ref,
     gain_ref,
     shift_ref,
+    received_ref,
+    theirs_ref,
     values_hbm,
-    middle_hbm,
-    sides_hbm,
+    middle_ref,
     out_hbm,
+    grid_hbm,
     norm_ref,
     held_ref,
     rows_ref,
-    grid_ref,
+    sides_ref,
+    face_ref,
     act_ref,
     total_ref,
     out_ref,
     sems,
+    face_sems,
     plane_sems,
     out_sems,
 ):
-    slots = grid_ref.shape[3]
+    slots = middle_ref.shape[3]
+    core = core_ref[0]
+    mine, other = lanes_of(core)
+    near_face, far_face = face_ref.at[core], face_ref.at[1 - core]
     copies = fetch(values_hbm, held_ref, sems, 4)
-    sources = [sides_hbm.at[0]] + [middle_hbm.at[at] for at in range(4)] + [sides_hbm.at[1]]
-    planes = [
-        pltpu.make_async_copy(place, grid_ref.at[at], plane_sems.at[at])
-        for at, place in enumerate(sources)
+    faces = [
+        pltpu.make_async_copy(received_ref.at[0], near_face.at[:, :, :, mine], face_sems.at[0]),
+        pltpu.make_async_copy(received_ref.at[1], near_face.at[:, :, :, other], face_sems.at[1]),
+        pltpu.make_async_copy(theirs_ref.at[0], far_face.at[:, :, :, other], face_sems.at[2]),
+        pltpu.make_async_copy(theirs_ref.at[1], far_face.at[:, :, :, mine], face_sems.at[3]),
     ]
-    for plane in planes:
-        plane.start()
+    for copy in faces:
+        copy.start()
     table = table_ref[...]
     held = jnp.sum(table, axis=0)
     voxels = held[:, 32:33] * (64.0 * GROUP_CH)
@@ -225,11 +228,10 @@
     from_sum = (lane_in == lane_out // GROUP_CH).astype(F32)
     from_square = (lane_in == lane_out // GROUP_CH + 16).astype(F32)
 
-    def spread(row, matrix):
-        return exact_dot(jnp.broadcast_to(row, (8, 128)), matrix)[0:1]
-
-    mean = spread(mean, from_sum)
-    variance = (spread(between, from_sum) + spread(held, from_square)) / voxels
+    stacked = jnp.concatenate([mean, between, held, jnp.zeros((5, 128), F32)], axis=0)
+    spread = exact_dot(stacked, jnp.concatenate([from_sum, from_square], axis=1))
+    mean = spread[0:1, 0:128]
+    variance = (spread[1:2, 0:128] + spread[2:3, 128:256]) / voxels
     rstd = lax.rsqrt(variance + 1e-05)
     norm_ref[0:1, :] = mean
     norm_ref[1:2, :] = rstd
@@ -246,16 +248,37 @@
             pieces.append(jnp.where(live, pre / (1.0 + jnp.exp(-pre)), 0.0))
         rows = jnp.concatenate(pieces, axis=0)
         act_ref[plane * 128 : plane * 128 + 128, :] = rows.T.astype(BF16)
+    for copy in faces:
+        copy.wait()
+    near = near_ref[...]
+    places = [(b, c) for b in range(6) for c in range(6)]
     sends = []
+    for which, dx in enumerate((-1, 1)):
+        lowest = which * slots
+        picks = {
+            offset: choose(near, offset, lowest, lowest + 2 * slots)
+            for offset in sorted({offset_of(dx, b, c) for b, c in places})
+        }
+        for b, c in places:
+            outer = face_ref[which, source(b) - 1, source(c) - 1]
+            inner = middle_ref[3 - 3 * which, source(b), source(c)]
+            table = [outer, inner] if which == 0 else [inner, outer]
+            sides_ref[which, b, c] = jnp.dot(
+                picks[offset_of(dx, b, c)],
+                jnp.concatenate(table, axis=0),
+                preferred_element_type=F32,
+            ).astype(BF16)
+    planes = [sides_ref.at[0]] + [middle_ref.at[at] for at in range(4)] + [sides_ref.at[1]]
+    for at, plane in enumerate(planes):
+        sends.append(pltpu.make_async_copy(plane, grid_hbm.at[at], plane_sems.at[at]))
+        sends[-1].start()
     for turn in range(9):
         seen = set()
         for plane in range(6):
-            if turn == 0:
-                planes[plane].wait()
             first, last = planes_of(plane)
             part = jnp.dot(
                 act_ref[first * 128 : last * 128, :],
-                window(grid_ref.at[plane], turn),
+                window(planes[plane], turn),
                 preferred_element_type=F32,
             )
             for at in range(first, last):
@@ -278,62 +301,6 @@
         send.wait()
 
 
-def edge_kernel(
-    core_ref,
-    near_ref,
-    received_ref,
-    theirs_ref,
-    middle_hbm,
-    sides_hbm,
-    face_ref,
-    inner_ref,
-    sides_ref,
-    sems,
-    side_sems,
-):
-    slots = near_ref.shape[0]
-    core = core_ref[0]
-    mine, other = lanes_of(core)
-    near_face, far_face = face_ref.at[core], face_ref.at[1 - core]
-    copies = [
-        pltpu.make_async_copy(received_ref.at[0], near_face.at[:, :, :, mine], sems.at[0]),
-        pltpu.make_async_copy(received_ref.at[1], near_face.at[:, :, :, other], sems.at[1]),
-        pltpu.make_async_copy(theirs_ref.at[0], far_face.at[:, :, :, other], sems.at[2]),
-        pltpu.make_async_copy(theirs_ref.at[1], far_face.at[:, :, :, mine], sems.at[3]),
-        pltpu.make_async_copy(middle_hbm.at[3, 1:5, 1:5], inner_ref.at[0], sems.at[4]),
-        pltpu.make_async_copy(middle_hbm.at[0, 1:5, 1:5], inner_ref.at[1], sems.at[5]),
-    ]
-    for copy in copies:
-        copy.start()
-    near = near_ref[...]
-    places = [(b, c) for b in range(6) for c in range(6)]
-    sends = []
-    for which, dx in enumerate((-1, 1)):
-        lowest = which * slots
-        picks = {
-            offset: choose(near, offset, lowest, lowest + 2 * slots)
-            for offset in sorted({offset_of(dx, b, c) for b, c in places})
-        }
-        if which == 0:
-            for copy in copies:
-                copy.wait()
-        for b, c in places:
-            outer = face_ref[which, source(b) - 1, source(c) - 1]
-            inner = inner_ref[which, source(b) - 1, source(c) - 1]
-            table = [outer, inner] if which == 0 else [inner, outer]
-            sides_ref[which, b, c] = jnp.dot(
-                picks[offset_of(dx, b, c)],
-                jnp.concatenate(table, axis=0),
-                preferred_element_type=F32,
-            ).astype(BF16)
-        sends.append(
-            pltpu.make_async_copy(sides_ref.at[which], sides_hbm.at[which], side_sems.at[which])
-        )
-        sends[-1].start()
-    for send in sends:
-        send.wait()
-
-
 def act_grad_kernel(
     counts_ref,
     norm_ref,
@@ -341,14 +308,13 @@
     shift_ref,
     values_ref,
     weight_ref,
-    middle_ref,
-    sides_ref,
+    grid_ref,
     out_ref,
     sums_ref,
     total_ref,
     rows_ref,
 ):
-    slots = middle_ref.shape[3]
+    slots = grid_ref.shape[3]
     total_ref[...] = jnp.zeros_like(total_ref)
     rows_ref[...] = values_ref[...].astype(F32)
 
@@ -357,9 +323,8 @@
         for plane in range(6):
             first, last = planes_of(plane)
             low, high = first - plane + 2, last - plane + 2
-            rows = sides_ref.at[plane // 5] if plane in (0, 5) else middle_ref.at[plane - 1]
             part = lax.dot_general(
-                window(rows, turn),
+                window(grid_ref.at[plane], turn),
                 weight_ref[low:high, turn].reshape((high - low) * 128, 256),
                 (((1,), (1,)), ((), ())),
                 preferred_element_type=F32,
@@ -425,11 +390,11 @@
     lane_in, lane_out = iota((128, 128), 0), iota((128, 128), 1)
     same = (lane_in // GROUP_CH == lane_out // GROUP_CH).astype(F32)
 
-    def grouped(row):
-        return exact_dot(jnp.broadcast_to(row, (8, 128)), same)[0:1]
-
-    first = grouped(gain * shift_sum) / voxels
-    second = grouped(gain * gain_sum) / voxels
+    stacked = jnp.concatenate(
+        [gain * shift_sum, gain * gain_sum, jnp.zeros((6, 128), F32)], axis=0
+    )
+    grouped = exact_dot(stacked, same) / voxels
+    first, second = grouped[0:1], grouped[1:2]
     chunk = slots // 4
     for slot in range(slots):
         rows = slice(slot * 64, slot * 64 + 64)
@@ -503,51 +468,48 @@
         halo_kernel,
         jax.ShapeDtypeStruct(middle_shape, BF16),
         [SMEM, VMEM, ANY, ANY],
-        [
-            pltpu.VMEM(middle_shape, BF16),
-            pltpu.SemaphoreType.DMA((2,)),
-            pltpu.SemaphoreType.DMA((4,)),
-        ],
-        HBM,
+        [pltpu.SemaphoreType.DMA((2,))],
         flops=10**9,
+        mib=24,
     )(core, neighbours, own.reshape(cube), own_other.reshape(cube))
 
-    middle, received = lax.optimization_barrier((middle, received))
+    table, received = lax.optimization_barrier((table, received))
     theirs = lax.ppermute(received, "ch", cores)
-    sides_shape = jax.ShapeDtypeStruct((2, 6, 6, slots, 2 * width), BF16)
-    sides = call(
-        edge_kernel,
-        sides_shape,
-        [SMEM, VMEM, ANY, ANY, HBM],
-        [
-            pltpu.VMEM((2, 4, 4, slots, 2 * width), BF16),
-            pltpu.VMEM((2, 4, 4, slots, 2 * width), BF16),
-            pltpu.VMEM(sides_shape.shape, BF16),
-            pltpu.SemaphoreType.DMA((6,)),
-            pltpu.SemaphoreType.DMA((2,)),
-        ],
-        HBM,
-    )(core, neighbours, received.reshape((2,) + face), theirs.reshape((2,) + face), middle)
+    grid_shape = pltpu.HBM((6, 6, 6, slots, 2 * width), BF16)
 
     term_shape = jax.ShapeDtypeStruct((3, 9, width, 2 * width), BF16)
-    weight_term, norm = call(
+    weight_term, grid, norm = call(
         weight_grad_kernel,
-        [term_shape, jax.ShapeDtypeStruct((8, 128), F32)],
-        [SMEM, VMEM, VMEM, VMEM, HBM, HBM, HBM],
+        [term_shape, grid_shape, jax.ShapeDtypeStruct((8, 128), F32)],
+        [SMEM, SMEM, VMEM, VMEM, VMEM, VMEM, ANY, ANY, HBM, VMEM],
         [
             pltpu.VMEM((rows, width), BF16),
             pltpu.VMEM((rows, width), F32),
-            pltpu.VMEM((6, 6, 6, slots, 2 * width), BF16),
+            pltpu.VMEM((2, 6, 6, slots, 2 * width), BF16),
+            pltpu.VMEM((2, 4, 4, slots, 2 * width), BF16),
             pltpu.VMEM((4 * width, 16 * slots), BF16),
             pltpu.VMEM((3, width, 2 * width), F32),
             pltpu.VMEM(term_shape.shape, BF16),
             pltpu.SemaphoreType.DMA((4,)),
+            pltpu.SemaphoreType.DMA((4,)),
             pltpu.SemaphoreType.DMA((6,)),
             pltpu.SemaphoreType.DMA((3, 9)),
         ],
-        [HBM, VMEM],
+        [HBM, HBM, VMEM],
         flops=work,
-    )(counts, table, gain_row, shift_row, value_rows, middle, sides)
+        mib=24,
+    )(
+        counts,
+        core,
+        neighbours,
+        table,
+        gain_row,
+        shift_row,
+        received.reshape((2,) + face),
+        theirs.reshape((2,) + face),
+        value_rows,
+        middle,
+    )
     piece = 27 * width // n_plane
     parts = lax.all_to_all(
         weight_term.reshape(n_plane, piece, 2 * width), PLANE, 0, 0, tiled=True
@@ -559,9 +521,10 @@
             jax.ShapeDtypeStruct((voxels, slots, width), F32),
             jax.ShapeDtypeStruct((1, 2 * width), F32),
         ],
-        [SMEM] + [VMEM] * 7,
+        [SMEM] + [VMEM] * 6,
         [pltpu.VMEM((4, 16, slots, width), F32), pltpu.VMEM((rows, width), F32)],
         flops=work,
+        mib=24,
     )(
         counts,
         norm,
@@ -569,8 +532,7 @@
         shift_row,
         value_rows,
         weight.reshape(3, 9, width, 2 * width),
-        middle,
-        sides,
+        grid,
     )
 
     part = jnp.sum(parts.astype(F32), axis=0).reshape(n_line, piece // n_line, 2 * width)

time: 144 us -> 142 us (0.986)
  blocking collectives: 38.5 us -> 67.4 us
  starting transfers between devices: 28.5 us -> 13.1 us
  waiting for transfers between devices: 30.4 us -> 19.7 us
  Pallas kernels: 39.9 us -> 31.8 us
  local copies, waits for them, and re-layouts: 3.44 us -> 5.58 us
  other arithmetic: 1.27 us -> 2.76 us
    all_to_all x0 -> x1, blocking collectives: none -> 26.4 us  [body(): table = lax.all_to_all(sent, SLABS, 0, 0, tiled=True)]
    all_to_all x1 -> x0, starting transfers between devices: 16.1 us -> none  [body(): table = lax.all_to_all(sent, SLABS, 0, 0, tiled=True)]
    all_to_all x1 -> x0, waiting for transfers between devices: 8.18 us -> none  [body(): table = lax.all_to_all(sent, SLABS, 0, 0, tiled=True)]
    pallas_call x1, Pallas kernels: 15.3 us -> 11.3 us  [body(): call(act_grad_kernel, [jax.ShapeDtypeStruct((voxels, slots, width), F32),...]
    ppermute x1, waiting for transfers between devices: 3.84 us -> 0.01 us  [body(): received = lax.ppermute(sent_planes, SLABS + ('ch',), outward)]
    pallas_call x2 -> x1, Pallas kernels: 14 us -> 11.2 us  [body(): call(weight_grad_kernel, [term_shape, grid_shape, jax.ShapeDtypeStruct((8...]
    all_to_all x1, blocking collectives: 25.6 us -> 28.1 us  [body(): plane = lax.all_to_all(plane, PLANE, 0, 0, tiled=True)]
    unnamed x13 -> x17, local copies, waits for them, and re-layouts: 1.96 us -> 4.1 us
  transfers between devices with their start and end apart: 7 -> 6, of which waited for: 5 -> 4; matrix products, arithmetic and copies ran while one was open for 1% -> 1% of each run, Pallas kernels for 16% -> 11%
where the time goes in v5:
time: 142 us
  blocking collectives  67.4 us (47%)
  Pallas kernels  31.8 us (22%)
  waiting for transfers between devices  19.7 us (14%)
  starting transfers between devices  13.1 us (9%)
  local copies, waits for them, and re-layouts  5.58 us (4%)
  other arithmetic  2.76 us (2%)
  between operations  1.48 us (1%)
    all_to_all x1, blocking collectives, body(): plane = lax.all_to_all(plane, PLANE, 0, 0, tiled=True)  28.1 us
    all_to_all x1, blocking collectives, body(): table = lax.all_to_all(sent, SLABS, 0, 0, tiled=True)  26.4 us
    all_to_all x1, blocking collectives, body(): part = jnp.sum(lax.all_to_all(part, 'z', 0, 0, tiled=True), axis=0)  12.9 us
    pallas_call x1, Pallas kernels, body(): call(act_grad_kernel, [jax.ShapeDtypeStruct((voxels, slots, width), F32),...  11.3 us
    pallas_call x1, Pallas kernels, body(): call(weight_grad_kernel, [term_shape, grid_shape, jax.ShapeDtypeStruct((8...  11.2 us
    all_to_all x1, waiting for transfers between devices, body(): lax.all_to_all(weight_term.reshape(n_plane, piece, 2 * width), PLANE, 0,...  9.07 us
    all_to_all x1, waiting for transfers between devices, body(): line = lax.all_to_all(line, 'z', 0, 0, tiled=True).reshape(piece, 2 * width)  8.97 us
    all_to_all x1, starting transfers between devices, body(): lax.all_to_all(weight_term.reshape(n_plane, piece, 2 * width), PLANE, 0,...  5.61 us
  transfers between devices with their start and end apart: 6, of which 4 were waited for; matrix products, arithmetic and copies ran while one was open for 1% of the time, Pallas kernels for 11%

profile of v5, /device:TPU:2, one launch (start us, length us, event | category | flops | bytes accessed | tf_op | source)
XLA Modules:
  0.0 141.7 jit_solution(13756621670804202175)
XLA Ops:
  0.6 0.0 copy-start.7
  0.6 3.2 %shard_map.103 = (bf16[64,48,128]{2,1,0:T(8,128)(2,1)}, bf16[16,48,128]{2,1,0:T(8,128)(2,1)}, bf16[16,48,128]{2,1,0:T(8,128)(2,1)}) custom-call(s32[1]{0:T(128)} %bitcast.core_ref, bf16[3072,128]{1,0:T(8,128)(2,1)} %bitcast.25), custom_call_target="tpu_custom_call" | custom-call | tf_op jit(solution)/shard_map/pallas_call | solution.py:443
  3.8 0.0 copy-start.2
  3.8 0.1 collective-permute-start
  3.9 0.5 collective-permute-start.3
  4.4 1.1 collective-permute-done
  5.6 1.0 pad_maximum_fusion
  6.6 3.5 %collective-permute-start.1 = (bf16[2,16,48,128]{3,2,1,0:T(8,128)(2,1)S(1)}, bf16[2,16,48,128]{3,2,1,0:T(8,128)(2,1)S(1)}, u32[]{:S(2)}, u32[]{:S(2)}) collective-permute-start(bf16[2,16,48,128]{3,2,1,0:T(8,128)(2,1)S(1)} %pad_maximum_fusion), channel_id=1, source_target_pairs={{0,2},{2,4},{4,6},{6,8},{8,10},{10,12},{12,14},{14,16},{16,18},{18... | collective-permute-start | bytes 1179656 | tf_op jit(solution)/shard_map/ppermute | solution.py:462
  10.7 2.7 %shard_map.102 = f32[128,1,128]{2,1,0:T(1,128)} custom-call(s32[1]{0:T(128)S(6)} %copy.15.counts_ref, bf16[3072,128]{1,0:T(8,128)(2,1)} %bitcast.21), custom_call_target="tpu_custom_call" | custom-call | tf_op jit(solution)/shard_map/pallas_call | solution.py:431
  13.4 26.4 %all_to_all.25.table_ref = f32[128,1,128]{2,1,0:T(1,128)S(1)} all-to-all(f32[128,1,128]{2,1,0:T(1,128)} %shard_map.102), channel_id=1, replica_groups=mesh['z'=8,'x'=4,'y'=4,'ch'=2] {'z','x','y'}, dimensions={0} | all-to-all | bytes 131072 | tf_op jit(solution)/shard_map/all_to_all | solution.py:442
  39.8 0.0 collective-permute-done.1
  39.8 0.0 collective-permute-start.2
  39.8 0.0 copy-done.7
  39.8 0.1 copy.14.near_ref
  39.9 0.0 collective-permute-done.3
  39.9 0.0 copy-done.2
  39.9 0.0 copy-start
  39.9 0.0 copy-start.3
  39.9 0.0 copy-start.5
  39.9 1.1 shard_map.104.middle_ref
  41.0 0.5 collective-permute-done.2
  41.5 0.0 copy-done
  41.5 0.0 copy-done.3
  41.5 0.0 copy-done.5
  41.5 11.2 %shard_map.105 = (bf16[3,9,128,256]{3,2,1,0:T(8,128)(2,1)}, bf16[6,6,6,48,256]{4,3,2,1,0:T(8,128)(2,1)}, f32[8,128]{1,0:T(8,128)S(1)}) custom-call(s32[1]{0:T(128)S(6)} %copy.15.counts_ref, s32[1]{0:T(128)} %bitcast.core_ref, s32[48,27]{1,0:T(8,128)S(1)} %copy.14.near_ref, f32[128,1,128]{2,1,0:T(1,128)S(1)} %all_to_all.25.table_ref, f32[1,128]{1,0:T(1,128)S(1)} %bitcast.31, ...), custom_call_target="tpu_custom_call" | custom-call | flops 5435817984 | tf_op jit(solution)/shard_map/pallas_call | solution.py:481
  52.8 5.6 %all-to-all-start.1 = ((bf16[16,216,256]{2,1,0:T(8,128)(2,1)}), bf16[16,216,256]{2,1,0:T(8,128)(2,1)}, u32[]{:S(2)}, u32[]{:S(2)}) async-start(bf16[16,216,256]{2,1,0:T(8,128)(2,1)} %bitcast.11), calls=%async_computation.1 | async-start | bytes 3538944 | tf_op jit(solution)/shard_map/all_to_all | solution.py:514
  58.4 0.0 copy-start.4
  58.4 1.5 %copy-done.4 = bf16[27,128,256]{2,1,0:T(8,128)(2,1)S(1)} copy-done((bf16[27,128,256]{2,1,0:T(8,128)(2,1)S(1)}, bf16[27,128,256]{2,1,0:T(8,128)(2,1)}, u32[]{:S(2)}) %copy-start.4) | copy-done | bytes 1769496
  59.9 0.0 copy-start.6
  59.9 2.5 %copy-done.6 = bf16[6,6,6,48,256]{4,3,2,1,0:T(8,128)(2,1)S(1)} copy-done((bf16[6,6,6,48,256]{4,3,2,1,0:T(8,128)(2,1)S(1)}, bf16[6,6,6,48,256]{4,3,2,1,0:T(8,128)(2,1)}, u32[]{:S(2)}) %copy-start.6) | copy-done | bytes 5308440
  62.4 11.3 %shard_map.106 = (f32[64,48,128]{2,1,0:T(8,128)S(1)}, f32[1,256]{1,0:T(1,128)S(1)}) custom-call(s32[1]{0:T(128)S(6)} %copy.15.counts_ref, f32[8,128]{1,0:T(8,128)S(1)} %get-tuple-element.22.norm_ref, f32[1,128]{1,0:T(1,128)S(1)} %bitcast.32, f32[1,128]{1,0:T(1,128)S(1)} %bitcast.38, bf16[3072,128]{1,0:T(8,128)(2,1)S(1)} %bitcast.23, ...), custom_call_target="tpu_custom_call" | custom-call | flops 5435817984 | tf_op jit(solution)/shard_map/pallas_call | solution.py:518
  73.7 9.1 %all-to-all-done.1 = bf16[16,216,256]{2,1,0:T(8,128)(2,1)} async-done(((bf16[16,216,256]{2,1,0:T(8,128)(2,1)}), bf16[16,216,256]{2,1,0:T(8,128)(2,1)}, u32[]{:S(2)}, u32[]{:S(2)}) %all-to-all-start.1) | async-done | bytes 1769504 | tf_op jit(solution)/shard_map/all_to_all | solution.py:514
  82.8 1.7 %convert_reduce_fusion = f32[216,256]{1,0:T(8,128)S(1)} fusion(bf16[16,216,256]{2,1,0:T(8,128)(2,1)} %all-to-all-done.1), kind=kLoop, calls=%fused_computation | loop fusion | flops 1714176 | bytes 1990656 | tf_op jit(solution)/shard_map/reduce_sum | solution.py:538
  84.6 12.9 %all_to_all.26 = f32[8,28,256]{2,1,0:T(8,128)S(1)} all-to-all(f32[8,28,256]{2,1,0:T(8,128)S(1)} %pad_maximum_fusion.1), channel_id=1, replica_groups=mesh['z'=8,'x'=4,'y'=4,'ch'=2] {'z'}, dimensions={0} | all-to-all | bytes 458752 | tf_op jit(solution)/shard_map/all_to_all | solution.py:542
  97.5 0.7 broadcast_in_dim.24
  98.2 3.4 %all-to-all-start.3 = ((bf16[8,27,256]{2,1,0:T(8,128)(2,1)}), bf16[8,27,256]{2,1,0:T(8,128)(2,1)S(1)}, u32[]{:S(2)}, u32[]{:S(2)}) async-start(bf16[8,27,256]{2,1,0:T(8,128)(2,1)} %broadcast_in_dim.24), calls=%async_computation.3 | async-start | bytes 262144 | tf_op jit(solution)/shard_map/all_to_all | solution.py:545
  101.6 9.0 %all-to-all-done.3 = bf16[8,27,256]{2,1,0:T(8,128)(2,1)S(1)} async-done(((bf16[8,27,256]{2,1,0:T(8,128)(2,1)}), bf16[8,27,256]{2,1,0:T(8,128)(2,1)S(1)}, u32[]{:S(2)}, u32[]{:S(2)}) %all-to-all-start.3) | async-done | bytes 110624 | tf_op jit(solution)/shard_map/all_to_all | solution.py:545
  110.5 0.1 reshape.74
  110.6 0.2 broadcast_in_dim.26
  110.8 0.0 copy-start.1
  110.8 28.1 %all_to_all.27.plane_ref = bf16[16,224,256]{2,1,0:T(8,128)(2,1)S(1)} all-to-all(bf16[16,224,256]{2,1,0:T(8,128)(2,1)S(1)} %broadcast_in_dim.26), channel_id=1, replica_groups=mesh['z'=8,'x'=4,'y'=4,'ch'=2] {'x','y'}, dimensions={0} | all-to-all | bytes 3670016 | tf_op jit(solution)/shard_map/all_to_all | solution.py:554
  138.9 0.0 copy-done.1
  138.9 2.3 %shard_map.107 = (bf16[3072,128]{1,0:T(8,128)(2,1)}, f32[3456,256]{1,0:T(8,128)}, f32[2,128]{1,0:T(2,128)S(1)}) custom-call(s32[1]{0:T(128)S(6)} %copy.15.counts_ref, f32[8,128]{1,0:T(8,128)S(1)} %get-tuple-element.22.norm_ref, f32[1,128]{1,0:T(1,128)S(1)} %bitcast.33, bf16[16,224,256]{2,1,0:T(8,128)(2,1)S(1)} %all_to_all.27.plane_ref, ...), custom_call_target="tpu_custom_call" | custom-call | tf_op jit(solution)/shard_map/pallas_call | solution.py:555
  141.2 0.5 slice_bitcast_fusion
  (8 shorter events, 0.1 us)
Async XLA Ops:
  0.6 39.2 %copy-start.7 = (s32[48,27]{0,1:T(8,128)S(1)}, s32[48,27]{0,1:T(8,128)}, u32[]{:S(2)}) copy-start(s32[48,27]{0,1:T(8,128)} %param.13) | copy-start | bytes 15556
  3.8 36.1 %copy-start.2 = (bf16[64,48,128]{2,1,0:T(8,128)(2,1)S(1)}, bf16[64,48,128]{2,1,0:T(8,128)(2,1)}, u32[]{:S(2)}) copy-start(bf16[64,48,128]{2,1,0:T(8,128)(2,1)} %get-tuple-element.21) | copy-start | bytes 2359300
  3.8 1.7 %collective-permute-start = (bf16[16,48,128]{2,1,0:T(8,128)(2,1)}, bf16[16,48,128]{2,1,0:T(8,128)(2,1)S(1)}, u32[]{:S(2)}, u32[]{:S(2)}) collective-permute-start(bf16[16,48,128]{2,1,0:T(8,128)(2,1)} %get-tuple-element.18), channel_id=1, source_target_pairs={{0,1},{1,0},{2,3},{3,2},{4,5},{5,4},{6,7},{7,6},{8,9},{9,8},{10,11... | collective-permute-start | bytes 589832 | tf_op jit(solution)/shard_map/ppermute | solution.py:460
  3.9 36.0 %collective-permute-start.3 = (bf16[64,48,128]{2,1,0:T(8,128)(2,1)}, bf16[64,48,128]{2,1,0:T(8,128)(2,1)S(1)}, u32[]{:S(2)}, u32[]{:S(2)}) collective-permute-start(bf16[64,48,128]{2,1,0:T(8,128)(2,1)} %get-tuple-element.21), channel_id=1, source_target_pairs={{0,1},{1,0},{2,3},{3,2},{4,5},{5,4},{6,7},{7,6},{8,9},{9,8},{10,11... | collective-permute-start | bytes 2359304 | tf_op jit(solution)/shard_map/ppermute | solution.py:461
  6.6 33.3 %collective-permute-start.1 = (bf16[2,16,48,128]{3,2,1,0:T(8,128)(2,1)S(1)}, bf16[2,16,48,128]{3,2,1,0:T(8,128)(2,1)S(1)}, u32[]{:S(2)}, u32[]{:S(2)}) collective-permute-start(bf16[2,16,48,128]{3,2,1,0:T(8,128)(2,1)S(1)} %pad_maximum_fusion), channel_id=1, source_target_pairs={{0,2},{2,4},{4,6},{6,8},{8,10},{10,12},{12,14},{14,16},{16,18},{18... | collective-permute-start | bytes 1179656 | tf_op jit(solution)/shard_map/ppermute | solution.py:462
  39.8 1.7 %collective-permute-start.2 = (bf16[2,16,48,128]{3,2,1,0:T(8,128)(2,1)S(1)}, bf16[2,16,48,128]{3,2,1,0:T(8,128)(2,1)S(1)}, u32[]{:S(2)}, u32[]{:S(2)}) collective-permute-start(bf16[2,16,48,128]{3,2,1,0:T(8,128)(2,1)S(1)} %collective-permute-done.1), channel_id=1, source_target_pairs={{0,1},{1,0},{2,3},{3,2},{4,5},{5,4},{6,7},{7,6},{8,9},{9,8},{10,11... | collective-permute-start | bytes 1179656 | tf_op jit(solution)/shard_map/ppermute | solution.py:477
  39.9 1.6 %copy-start = (bf16[48,64,128]{2,1,0:T(8,128)(2,1)S(1)}, bf16[48,64,128]{2,1,0:T(8,128)(2,1)}, u32[]{:S(2)}) copy-start(bf16[48,64,128]{2,1,0:T(8,128)(2,1)} %param.7) | copy-start | bytes 2359300
  39.9 1.6 %copy-start.3 = (f32[128]{0:T(128)S(1)}, f32[128]{0:T(128)}, u32[]{:S(2)}) copy-start(f32[128]{0:T(128)} %param.10) | copy-start | bytes 1540
  39.9 1.6 %copy-start.5 = (f32[128]{0:T(128)S(1)}, f32[128]{0:T(128)}, u32[]{:S(2)}) copy-start(f32[128]{0:T(128)} %param.11) | copy-start | bytes 1540
  52.8 30.0 %all-to-all-start.1 = ((bf16[16,216,256]{2,1,0:T(8,128)(2,1)}), bf16[16,216,256]{2,1,0:T(8,128)(2,1)}, u32[]{:S(2)}, u32[]{:S(2)}) async-start(bf16[16,216,256]{2,1,0:T(8,128)(2,1)} %bitcast.11), calls=%async_computation.1 | async-start | bytes 3538944 | tf_op jit(solution)/shard_map/all_to_all | solution.py:514
  58.4 1.5 %copy-start.4 = (bf16[27,128,256]{2,1,0:T(8,128)(2,1)S(1)}, bf16[27,128,256]{2,1,0:T(8,128)(2,1)}, u32[]{:S(2)}) copy-start(bf16[27,128,256]{2,1,0:T(8,128)(2,1)} %param.9) | copy-start | bytes 5308420
  59.9 2.5 %copy-start.6 = (bf16[6,6,6,48,256]{4,3,2,1,0:T(8,128)(2,1)S(1)}, bf16[6,6,6,48,256]{4,3,2,1,0:T(8,128)(2,1)}, u32[]{:S(2)}) copy-start(bf16[6,6,6,48,256]{4,3,2,1,0:T(8,128)(2,1)} %get-tuple-element.24.grid_ref) | copy-start | bytes 15925252
  98.2 12.4 %all-to-all-start.3 = ((bf16[8,27,256]{2,1,0:T(8,128)(2,1)}), bf16[8,27,256]{2,1,0:T(8,128)(2,1)S(1)}, u32[]{:S(2)}, u32[]{:S(2)}) async-start(bf16[8,27,256]{2,1,0:T(8,128)(2,1)} %broadcast_in_dim.24), calls=%async_computation.3 | async-start | bytes 262144 | tf_op jit(solution)/shard_map/all_to_all | solution.py:545
  110.8 28.1 %copy-start.1 = (bf16[48,64,128]{2,1,0:T(8,128)(2,1)S(1)}, bf16[48,64,128]{2,1,0:T(8,128)(2,1)}, u32[]{:S(2)}) copy-start(bf16[48,64,128]{2,1,0:T(8,128)(2,1)} %param.8) | copy-start | bytes 2359300

commit v6 on v5

--- a/solution.py
+++ b/solution.py
@@ -70,12 +70,27 @@
         rows_ref[rows, :] = held_ref[rows, :].astype(F32)
 
 
-def turn_kernel(
-    core_ref, in_hbm, own_hbm, give_hbm, keep_hbm, held_ref, rows_ref, own_ref, sems, out_sems
+def prepare_kernel(
+    counts_ref,
+    core_ref,
+    cotangent_hbm,
+    values_hbm,
+    own_hbm,
+    give_hbm,
+    keep_hbm,
+    sent_ref,
+    held_ref,
+    rows_ref,
+    own_ref,
+    sems,
+    out_sems,
 ):
-    copies = fetch(in_hbm, held_ref, sems, 4)
+    slots = own_ref.shape[1]
+    turns = fetch(cotangent_hbm, held_ref.at[0], sems.at[0], 4)
+    copies = fetch(values_hbm, held_ref.at[1], sems.at[1], 4)
     core = core_ref[0]
-    widen(copies, held_ref, rows_ref)
+    count = counts_ref[0]
+    widen(turns, held_ref.at[0], rows_ref)
     turned(rows_ref, own_ref)
     sends = [
         pltpu.make_async_copy(own_ref.at[pl.ds(48 * core, 16)], give_hbm, out_sems.at[0]),
@@ -84,14 +99,7 @@
     ]
     for send in sends:
         send.start()
-    for send in sends:
-        send.wait()
-
-
-def sums_kernel(counts_ref, values_hbm, sent_ref, held_ref, rows_ref, sems):
-    slots = held_ref.shape[0] // 64
-    count = counts_ref[0]
-    widen(fetch(values_hbm, held_ref, sems, 4), held_ref, rows_ref)
+    widen(copies, held_ref.at[1], rows_ref)
 
     def over_slots(term):
         total = jnp.zeros((8, 128), F32)
@@ -116,6 +124,8 @@
     row = exact_dot(total, to_sum) + exact_dot(squares, to_square)
     row = row + jnp.where(iota((8, 128), 1) == 32, count.astype(F32), 0.0)
     sent_ref[...] = jnp.broadcast_to(row[0:1].reshape(1, 1, 128), sent_ref.shape)
+    for send in sends:
+        send.wait()
 
 
 def lanes_of(core):
@@ -187,19 +197,17 @@
     shift_ref,
     received_ref,
     theirs_ref,
-    values_hbm,
+    values_ref,
     middle_ref,
     out_hbm,
     grid_hbm,
     norm_ref,
-    held_ref,
     rows_ref,
     sides_ref,
     face_ref,
     act_ref,
     total_ref,
     out_ref,
-    sems,
     face_sems,
     plane_sems,
     out_sems,
@@ -208,7 +216,6 @@
     core = core_ref[0]
     mine, other = lanes_of(core)
     near_face, far_face = face_ref.at[core], face_ref.at[1 - core]
-    copies = fetch(values_hbm, held_ref, sems, 4)
     faces = [
         pltpu.make_async_copy(received_ref.at[0], near_face.at[:, :, :, mine], face_sems.at[0]),
         pltpu.make_async_copy(received_ref.at[1], near_face.at[:, :, :, other], face_sems.at[1]),
@@ -239,7 +246,7 @@
     norm_ref[3:8, :] = jnp.zeros((5, 128), F32)
     gain, shift = gain_ref[...], shift_ref[...]
     live = iota((slots, 128), 0) < counts_ref[0]
-    widen(copies, held_ref, rows_ref)
+    rows_ref[...] = values_ref[...].astype(F32)
     for plane in range(4):
         pieces = []
         for voxel in range(plane * 16, plane * 16 + 16):
@@ -291,12 +298,15 @@
                     seen.add(step)
         for step in range(3):
             out_ref[step, turn] = total_ref[step].astype(BF16)
-            sends.append(
-                pltpu.make_async_copy(
-                    out_ref.at[step, turn], out_hbm.at[step, turn], out_sems.at[step, turn]
+        if turn in (5, 8):
+            part = pl.ds(0, 6) if turn == 5 else pl.ds(6, 3)
+            for step in range(3):
+                sends.append(
+                    pltpu.make_async_copy(
+                        out_ref.at[step, part], out_hbm.at[step, part], out_sems.at[step, turn // 8]
+                    )
                 )
-            )
-            sends[-1].start()
+                sends[-1].start()
     for send in sends:
         send.wait()
 
@@ -361,7 +371,8 @@
     grad_ref,
     out_hbm,
     weight_hbm,
-    sums_ref,
+    gain_out,
+    shift_out,
     out_ref,
     weight_ref,
     out_sems,
@@ -383,8 +394,8 @@
         )
         copies[-1].start()
     shift_sum, gain_sum = totals[:, 0:128], totals[:, 128:256]
-    sums_ref[0:1] = gain_sum
-    sums_ref[1:2] = shift_sum
+    gain_out[...] = gain_sum
+    shift_out[...] = shift_sum
     mean, rstd, voxels = norm_ref[0:1, :], norm_ref[1:2, :], norm_ref[2:3, :]
     gain = gain_ref[...]
     lane_in, lane_out = iota((128, 128), 0), iota((128, 128), 1)
@@ -428,32 +439,26 @@
     cotangent_rows = cotangent.reshape(rows, width)
     work = 2 * rows * 27 * width * 2 * width
 
-    sent = call(
-        sums_kernel,
-        jax.ShapeDtypeStruct((n_slab, 1, 128), F32),
-        [SMEM, HBM],
+    own, give, keep, sent = call(
+        prepare_kernel,
         [
-            pltpu.VMEM((rows, width), BF16),
-            pltpu.VMEM((rows, width), F32),
-            pltpu.SemaphoreType.DMA((4,)),
+            turned_shape,
+            face_shape,
+            face_shape,
+            jax.ShapeDtypeStruct((n_slab, 1, 128), F32),
         ],
-        mib=60,
-    )(counts, value_rows)
-    table = lax.all_to_all(sent, SLABS, 0, 0, tiled=True)
-    own, give, keep = call(
-        turn_kernel,
-        [turned_shape, face_shape, face_shape],
-        [SMEM, HBM],
+        [SMEM, SMEM, HBM, HBM],
         [
-            pltpu.VMEM((rows, width), BF16),
+            pltpu.VMEM((2, rows, width), BF16),
             pltpu.VMEM((rows, width), F32),
             pltpu.VMEM(turned_shape.shape, BF16),
-            pltpu.SemaphoreType.DMA((4,)),
+            pltpu.SemaphoreType.DMA((2, 4)),
             pltpu.SemaphoreType.DMA((3,)),
         ],
-        [HBM] * 3,
+        [HBM, HBM, HBM, VMEM],
         mib=60,
-    )(core, cotangent_rows)
+    )(counts, core, cotangent_rows, value_rows)
+    table = lax.all_to_all(sent, SLABS, 0, 0, tiled=True)
     cores = [(0, 1), (1, 0)]
     ups = [(i, i + 1) for i in range(n_slab - 1)]
     outward = [(2 * i, 2 * j) for i, j in ups] + [(2 * j + 1, 2 * i + 1) for i, j in ups]
@@ -471,7 +476,12 @@
         [pltpu.SemaphoreType.DMA((2,))],
         flops=10**9,
         mib=24,
-    )(core, neighbours, own.reshape(cube), own_other.reshape(cube))
+    )(
+        core,
+        neighbours,
+        pltpu.with_memory_space_constraint(own.reshape(cube), pltpu.HBM),
+        own_other.reshape(cube),
+    )
 
     table, received = lax.optimization_barrier((table, received))
     theirs = lax.ppermute(received, "ch", cores)
@@ -481,9 +491,8 @@
     weight_term, grid, norm = call(
         weight_grad_kernel,
         [term_shape, grid_shape, jax.ShapeDtypeStruct((8, 128), F32)],
-        [SMEM, SMEM, VMEM, VMEM, VMEM, VMEM, ANY, ANY, HBM, VMEM],
+        [SMEM, SMEM, VMEM, VMEM, VMEM, VMEM, ANY, ANY, VMEM, VMEM],
         [
-            pltpu.VMEM((rows, width), BF16),
             pltpu.VMEM((rows, width), F32),
             pltpu.VMEM((2, 6, 6, slots, 2 * width), BF16),
             pltpu.VMEM((2, 4, 4, slots, 2 * width), BF16),
@@ -491,9 +500,8 @@
             pltpu.VMEM((3, width, 2 * width), F32),
             pltpu.VMEM(term_shape.shape, BF16),
             pltpu.SemaphoreType.DMA((4,)),
-            pltpu.SemaphoreType.DMA((4,)),
             pltpu.SemaphoreType.DMA((6,)),
-            pltpu.SemaphoreType.DMA((3, 9)),
+            pltpu.SemaphoreType.DMA((3, 2)),
         ],
         [HBM, HBM, VMEM],
         flops=work,
@@ -524,7 +532,7 @@
         [SMEM] + [VMEM] * 6,
         [pltpu.VMEM((4, 16, slots, width), F32), pltpu.VMEM((rows, width), F32)],
         flops=work,
-        mib=24,
+        mib=58,
     )(
         counts,
         norm,
@@ -552,12 +560,13 @@
     line = jnp.concatenate([line] + split + [jnp.zeros((5, 2 * width), BF16)], axis=0)
     plane = jnp.broadcast_to(line[None], (n_plane,) + line.shape)
     plane = lax.all_to_all(plane, PLANE, 0, 0, tiled=True)
-    grad_features, grad_weight, totals = call(
+    grad_features, grad_weight, grad_gain, grad_shift = call(
         last_kernel,
         [
             jax.ShapeDtypeStruct((rows, width), BF16),
             jax.ShapeDtypeStruct((27 * width, 2 * width), F32),
-            jax.ShapeDtypeStruct((2, width), F32),
+            jax.ShapeDtypeStruct((1, width), F32),
+            jax.ShapeDtypeStruct((1, width), F32),
         ],
         [SMEM] + [VMEM] * 6,
         [
@@ -566,7 +575,7 @@
             pltpu.SemaphoreType.DMA((4,)),
             pltpu.SemaphoreType.DMA((n_plane,)),
         ],
-        [HBM, HBM, VMEM],
+        [HBM, HBM, VMEM, VMEM],
         mib=20,
     )(
         counts,
@@ -580,8 +589,8 @@
     return (
         grad_features.reshape(features.shape),
         grad_weight.reshape(27, width, 2 * width),
-        totals[0],
-        totals[1],
+        grad_gain.reshape(width),
+        grad_shift.reshape(width),
     )
 
 

time: 142 us -> 140 us (0.986)
  local copies, waits for them, and re-layouts: 5.58 us -> 1.69 us
  Pallas kernels: 31.8 us -> 33.9 us
  other arithmetic: 2.76 us -> 1.27 us
    pallas_call x1, Pallas kernels: 11.3 us -> 15.6 us  [body(): call(act_grad_kernel, [jax.ShapeDtypeStruct((voxels, slots, width), F32),...]
    unnamed x17 -> x23, local copies, waits for them, and re-layouts: 4.1 us -> 0.72 us
    pallas_call x2 -> x1, Pallas kernels: 5.87 us -> 3.84 us  [body(): call(prepare_kernel, [turned_shape, face_shape, face_shape, jax.ShapeDtyp...]
    reduce_sum x1, other arithmetic: 1.74 us -> 0.25 us  [body(): jnp.sum(parts.astype(F32), axis=0)]
    pallas_call x1, Pallas kernels: 11.2 us -> 9.81 us  [body(): call(weight_grad_kernel, [term_shape, grid_shape, jax.ShapeDtypeStruct((8...]
  transfers between devices with their start and end apart: 6 -> 6, of which waited for: 4 -> 3; matrix products, arithmetic and copies ran while one was open for 1% -> 1% of each run, Pallas kernels for 11% -> 12%
where the time goes in v6:
time: 140 us
  blocking collectives  68.6 us (49%)
  Pallas kernels  33.9 us (24%)
  waiting for transfers between devices  20.4 us (15%)
  starting transfers between devices  12.4 us (9%)
  between operations  1.7 us (1%)
  local copies, waits for them, and re-layouts  1.69 us (1%)
    all_to_all x1, blocking collectives, body(): plane = lax.all_to_all(plane, PLANE, 0, 0, tiled=True)  28.4 us
    all_to_all x1, blocking collectives, body(): table = lax.all_to_all(sent, SLABS, 0, 0, tiled=True)  26.5 us
    pallas_call x1, Pallas kernels, body(): call(act_grad_kernel, [jax.ShapeDtypeStruct((voxels, slots, width), F32),...  15.6 us
    all_to_all x1, blocking collectives, body(): part = jnp.sum(lax.all_to_all(part, 'z', 0, 0, tiled=True), axis=0)  13.8 us
    all_to_all x1, waiting for transfers between devices, body(): lax.all_to_all(weight_term.reshape(n_plane, piece, 2 * width), PLANE, 0,...  10.2 us
    pallas_call x1, Pallas kernels, body(): call(weight_grad_kernel, [term_shape, grid_shape, jax.ShapeDtypeStruct((8...  9.81 us
    all_to_all x1, waiting for transfers between devices, body(): line = lax.all_to_all(line, 'z', 0, 0, tiled=True).reshape(piece, 2 * width)  8.98 us
    all_to_all x1, starting transfers between devices, body(): lax.all_to_all(weight_term.reshape(n_plane, piece, 2 * width), PLANE, 0,...  4.94 us
  transfers between devices with their start and end apart: 6, of which 3 were waited for; matrix products, arithmetic and copies ran while one was open for 1% of the time, Pallas kernels for 12%

profile of v6, /device:TPU:2, one launch (start us, length us, event | category | flops | bytes accessed | tf_op | source)
XLA Modules:
  0.0 139.9 jit_solution(6075352466388000149)
XLA Ops:
  0.6 0.0 copy-start.9
  1.3 3.8 %shard_map.102 = (bf16[64,48,128]{2,1,0:T(8,128)(2,1)}, bf16[16,48,128]{2,1,0:T(8,128)(2,1)}, bf16[16,48,128]{2,1,0:T(8,128)(2,1)}, f32[128,1,128]{2,1,0:T(1,128)}) custom-call(s32[1]{0:T(128)S(6)} %copy.15.counts_ref, s32[1]{0:T(128)} %bitcast.core_ref, bf16[3072,128]{1,0:T(8,128)(2,1)} %bitcast.19, bf16[3072,128]{1,0:T(8,128)(2,1)} %bitcast.21), custom_call_target="tpu_custom_call" | custom-call | tf_op jit(solution)/shard_map/pallas_call | solution.py:442
  5.2 0.1 collective-permute-start
  5.3 0.5 collective-permute-start.3
  5.8 1.1 collective-permute-done
  6.9 1.0 pad_maximum_fusion
  7.9 3.5 %collective-permute-start.1 = (bf16[2,16,48,128]{3,2,1,0:T(8,128)(2,1)S(1)}, bf16[2,16,48,128]{3,2,1,0:T(8,128)(2,1)S(1)}, u32[]{:S(2)}, u32[]{:S(2)}) collective-permute-start(bf16[2,16,48,128]{3,2,1,0:T(8,128)(2,1)S(1)} %pad_maximum_fusion), channel_id=1, source_target_pairs={{0,2},{2,4},{4,6},{6,8},{8,10},{10,12},{12,14},{14,16},{16,18},{18... | collective-permute-start | bytes 1179656 | tf_op jit(solution)/shard_map/ppermute | solution.py:467
  11.4 26.5 %all_to_all.25.table_ref = f32[128,1,128]{2,1,0:T(1,128)S(1)} all-to-all(f32[128,1,128]{2,1,0:T(1,128)} %get-tuple-element.19), channel_id=1, replica_groups=mesh['z'=8,'x'=4,'y'=4,'ch'=2] {'z','x','y'}, dimensions={0} | all-to-all | bytes 131072 | tf_op jit(solution)/shard_map/all_to_all | solution.py:461
  37.8 0.0 collective-permute-done.1
  37.8 0.0 collective-permute-start.2
  37.9 0.0 copy-done.9
  37.9 0.1 copy.14.near_ref
  37.9 0.0 collective-permute-done.3
  37.9 0.0 copy-start.1
  38.0 0.0 copy-start.6
  38.0 0.0 copy-start.8
  38.0 1.9 %shard_map.103.middle_ref = bf16[4,6,6,48,256]{4,3,2,1,0:T(8,128)(2,1)S(1)} custom-call(s32[1]{0:T(128)} %bitcast.core_ref, s32[48,27]{1,0:T(8,128)S(1)} %copy.14.near_ref, bf16[4,4,4,48,128]{4,3,2,1,0:T(8,128)(2,1)} %bitcast.34, bf16[4,4,4,48,128]{4,3,2,1,0:T(8,128)(2,1)S(1)} %bitcast.26), custom_call_target="tpu_custom_call" | custom-call | flops 1000000000 | tf_op jit(solution)/shard_map/pallas_call | solution.py:472
  39.9 0.0 collective-permute-done.2
  39.9 0.0 copy-done.1
  39.9 0.0 copy-done.6
  39.9 0.0 copy-done.8
  39.9 9.8 %shard_map.104 = (bf16[3,9,128,256]{3,2,1,0:T(8,128)(2,1)}, bf16[6,6,6,48,256]{4,3,2,1,0:T(8,128)(2,1)}, f32[8,128]{1,0:T(8,128)S(1)}) custom-call(s32[1]{0:T(128)S(6)} %copy.15.counts_ref, s32[1]{0:T(128)} %bitcast.core_ref, s32[48,27]{1,0:T(8,128)S(1)} %copy.14.near_ref, f32[128,1,128]{2,1,0:T(1,128)S(1)} %all_to_all.25.table_ref, f32[1,128]{1,0:T(1,128)S(1)} %bitcast.28, ...), custom_call_target="tpu_custom_call" | custom-call | flops 5435817984 | tf_op jit(solution)/shard_map/pallas_call | solution.py:491
  49.7 0.0 copy-start.4
  49.7 0.6 copy-done.4
  50.3 4.9 %all-to-all-start.1 = ((bf16[16,216,256]{2,1,0:T(8,128)(2,1)}), bf16[16,216,256]{2,1,0:T(8,128)(2,1)S(1)}, u32[]{:S(2)}, u32[]{:S(2)}) async-start(bf16[16,216,256]{2,1,0:T(8,128)(2,1)} %bitcast.11), calls=%async_computation.1 | async-start | bytes 3538944 | tf_op jit(solution)/shard_map/all_to_all | solution.py:522
  55.3 15.6 %shard_map.105 = (f32[64,48,128]{2,1,0:T(8,128)}, f32[1,256]{1,0:T(1,128)}) custom-call(s32[1]{0:T(128)S(6)} %copy.15.counts_ref, f32[8,128]{1,0:T(8,128)} %copy-done.4, f32[1,128]{1,0:T(1,128)} %bitcast.27, f32[1,128]{1,0:T(1,128)} %bitcast.32, bf16[3072,128]{1,0:T(8,128)(2,1)} %bitcast.22, bf16[3,9,128,256]{3,2,1,0:T(8,128)(2,1)} %bitcast.39, ...), custom_call_target="tpu_custom_call" | custom-call | flops 5435817984 | tf_op jit(solution)/shard_map/pallas_call | solution.py:526
  70.8 0.0 copy-start.10
  70.9 10.2 %all-to-all-done.1 = bf16[16,216,256]{2,1,0:T(8,128)(2,1)S(1)} async-done(((bf16[16,216,256]{2,1,0:T(8,128)(2,1)}), bf16[16,216,256]{2,1,0:T(8,128)(2,1)S(1)}, u32[]{:S(2)}, u32[]{:S(2)}) %all-to-all-start.1) | async-done | bytes 1769504 | tf_op jit(solution)/shard_map/all_to_all | solution.py:522
  81.1 0.3 convert_reduce_fusion
  81.4 0.0 copy-done.10
  81.4 13.8 %all_to_all.26 = f32[8,28,256]{2,1,0:T(8,128)S(1)} all-to-all(f32[8,28,256]{2,1,0:T(8,128)S(1)} %pad_maximum_fusion.1), channel_id=1, replica_groups=mesh['z'=8,'x'=4,'y'=4,'ch'=2] {'z'}, dimensions={0} | all-to-all | bytes 458752 | tf_op jit(solution)/shard_map/all_to_all | solution.py:550
  95.2 0.7 broadcast_in_dim.24
  95.9 3.4 %all-to-all-start.3 = ((bf16[8,27,256]{2,1,0:T(8,128)(2,1)}), bf16[8,27,256]{2,1,0:T(8,128)(2,1)S(1)}, u32[]{:S(2)}, u32[]{:S(2)}) async-start(bf16[8,27,256]{2,1,0:T(8,128)(2,1)} %broadcast_in_dim.24), calls=%async_computation.3 | async-start | bytes 262144 | tf_op jit(solution)/shard_map/all_to_all | solution.py:553
  99.3 9.0 %all-to-all-done.3 = bf16[8,27,256]{2,1,0:T(8,128)(2,1)S(1)} async-done(((bf16[8,27,256]{2,1,0:T(8,128)(2,1)}), bf16[8,27,256]{2,1,0:T(8,128)(2,1)S(1)}, u32[]{:S(2)}, u32[]{:S(2)}) %all-to-all-start.3) | async-done | bytes 110624 | tf_op jit(solution)/shard_map/all_to_all | solution.py:553
  108.3 0.1 reshape.80
  108.4 0.2 broadcast_in_dim.26
  108.5 0.0 copy-start
  108.6 0.0 copy-start.2
  108.6 0.0 copy-start.3
  108.6 0.0 copy-start.5
  108.6 0.0 copy-start.7
  108.6 28.4 %all_to_all.27.plane_ref = bf16[16,224,256]{2,1,0:T(8,128)(2,1)S(1)} all-to-all(bf16[16,224,256]{2,1,0:T(8,128)(2,1)S(1)} %broadcast_in_dim.26), channel_id=1, replica_groups=mesh['z'=8,'x'=4,'y'=4,'ch'=2] {'x','y'}, dimensions={0} | all-to-all | bytes 3670016 | tf_op jit(solution)/shard_map/all_to_all | solution.py:562
  137.0 0.0 copy-done
  137.0 0.0 copy-done.2
  137.0 0.0 copy-done.3
  137.0 0.0 copy-done.5
  137.0 0.0 copy-done.7
  137.0 2.8 %shard_map.106 = (bf16[3072,128]{1,0:T(8,128)(2,1)}, f32[3456,256]{1,0:T(8,128)}, f32[1,128]{1,0:T(1,128)}, f32[1,128]{1,0:T(1,128)}) custom-call(s32[1]{0:T(128)S(6)} %copy.15.counts_ref, f32[8,128]{1,0:T(8,128)S(1)} %copy-done.5, f32[1,128]{1,0:T(1,128)S(1)} %bitcast.29, bf16[16,224,256]{2,1,0:T(8,128)(2,1)S(1)} %all_to_all.27.plane_ref, ...), custom_call_target="tpu_custom_call" | custom-call | tf_op jit(solution)/shard_map/pallas_call | solution.py:563
  (8 shorter events, 0.1 us)
Async XLA Ops:
  0.6 37.2 %copy-start.9 = (s32[48,27]{0,1:T(8,128)S(1)}, s32[48,27]{0,1:T(8,128)}, u32[]{:S(2)}) copy-start(s32[48,27]{0,1:T(8,128)} %param.13) | copy-start | bytes 15556
  5.2 1.7 %collective-permute-start = (bf16[16,48,128]{2,1,0:T(8,128)(2,1)}, bf16[16,48,128]{2,1,0:T(8,128)(2,1)S(1)}, u32[]{:S(2)}, u32[]{:S(2)}) collective-permute-start(bf16[16,48,128]{2,1,0:T(8,128)(2,1)} %get-tuple-element.21), channel_id=1, source_target_pairs={{0,1},{1,0},{2,3},{3,2},{4,5},{5,4},{6,7},{7,6},{8,9},{9,8},{10,11... | collective-permute-start | bytes 589832 | tf_op jit(solution)/shard_map/ppermute | solution.py:465
  5.3 32.7 %collective-permute-start.3 = (bf16[64,48,128]{2,1,0:T(8,128)(2,1)}, bf16[64,48,128]{2,1,0:T(8,128)(2,1)S(1)}, u32[]{:S(2)}, u32[]{:S(2)}) collective-permute-start(bf16[64,48,128]{2,1,0:T(8,128)(2,1)} %get-tuple-element.24), channel_id=1, source_target_pairs={{0,1},{1,0},{2,3},{3,2},{4,5},{5,4},{6,7},{7,6},{8,9},{9,8},{10,11... | collective-permute-start | bytes 2359304 | tf_op jit(solution)/shard_map/ppermute | solution.py:466
  7.9 30.0 %collective-permute-start.1 = (bf16[2,16,48,128]{3,2,1,0:T(8,128)(2,1)S(1)}, bf16[2,16,48,128]{3,2,1,0:T(8,128)(2,1)S(1)}, u32[]{:S(2)}, u32[]{:S(2)}) collective-permute-start(bf16[2,16,48,128]{3,2,1,0:T(8,128)(2,1)S(1)} %pad_maximum_fusion), channel_id=1, source_target_pairs={{0,2},{2,4},{4,6},{6,8},{8,10},{10,12},{12,14},{14,16},{16,18},{18... | collective-permute-start | bytes 1179656 | tf_op jit(solution)/shard_map/ppermute | solution.py:467
  37.8 2.0 %collective-permute-start.2 = (bf16[2,16,48,128]{3,2,1,0:T(8,128)(2,1)S(1)}, bf16[2,16,48,128]{3,2,1,0:T(8,128)(2,1)S(1)}, u32[]{:S(2)}, u32[]{:S(2)}) collective-permute-start(bf16[2,16,48,128]{3,2,1,0:T(8,128)(2,1)S(1)} %collective-permute-done.1), channel_id=1, source_target_pairs={{0,1},{1,0},{2,3},{3,2},{4,5},{5,4},{6,7},{7,6},{8,9},{9,8},{10,11... | collective-permute-start | bytes 1179656 | tf_op jit(solution)/shard_map/ppermute | solution.py:487
  37.9 1.9 %copy-start.1 = (bf16[48,64,128]{2,1,0:T(8,128)(2,1)S(1)}, bf16[48,64,128]{2,1,0:T(8,128)(2,1)}, u32[]{:S(2)}) copy-start(bf16[48,64,128]{2,1,0:T(8,128)(2,1)} %param.7) | copy-start | bytes 2359300
  38.0 1.9 %copy-start.6 = (f32[128]{0:T(128)S(1)}, f32[128]{0:T(128)}, u32[]{:S(2)}) copy-start(f32[128]{0:T(128)} %param.10) | copy-start | bytes 1540
  38.0 1.9 %copy-start.8 = (f32[128]{0:T(128)S(1)}, f32[128]{0:T(128)}, u32[]{:S(2)}) copy-start(f32[128]{0:T(128)} %param.11) | copy-start | bytes 1540
  49.7 0.6 copy-start.4
  50.3 30.8 %all-to-all-start.1 = ((bf16[16,216,256]{2,1,0:T(8,128)(2,1)}), bf16[16,216,256]{2,1,0:T(8,128)(2,1)S(1)}, u32[]{:S(2)}, u32[]{:S(2)}) async-start(bf16[16,216,256]{2,1,0:T(8,128)(2,1)} %bitcast.11), calls=%async_computation.1 | async-start | bytes 3538944 | tf_op jit(solution)/shard_map/all_to_all | solution.py:522
  70.8 10.5 %copy-start.10 = (f32[1,256]{1,0:T(1,128)S(1)}, f32[1,256]{1,0:T(1,128)}, u32[]{:S(2)}) copy-start(f32[1,256]{1,0:T(1,128)} %get-tuple-element.28) | copy-start | bytes 3076
  95.9 12.4 %all-to-all-start.3 = ((bf16[8,27,256]{2,1,0:T(8,128)(2,1)}), bf16[8,27,256]{2,1,0:T(8,128)(2,1)S(1)}, u32[]{:S(2)}, u32[]{:S(2)}) async-start(bf16[8,27,256]{2,1,0:T(8,128)(2,1)} %broadcast_in_dim.24), calls=%async_computation.3 | async-start | bytes 262144 | tf_op jit(solution)/shard_map/all_to_all | solution.py:553
  108.5 28.4 %copy-start = (bf16[48,64,128]{2,1,0:T(8,128)(2,1)S(1)}, bf16[48,64,128]{2,1,0:T(8,128)(2,1)}, u32[]{:S(2)}) copy-start(bf16[48,64,128]{2,1,0:T(8,128)(2,1)} %param.8) | copy-start | bytes 2359300
  108.6 28.4 %copy-start.2 = (bf16[48,64,128]{2,1,0:T(8,128)(2,1)S(1)}, bf16[48,64,128]{2,1,0:T(8,128)(2,1)}, u32[]{:S(2)}) copy-start(bf16[48,64,128]{2,1,0:T(8,128)(2,1)} %param.7) | copy-start | bytes 2359300
  108.6 28.4 %copy-start.3 = (f32[64,48,128]{2,1,0:T(8,128)S(1)}, f32[64,48,128]{2,1,0:T(8,128)}, u32[]{:S(2)}) copy-start(f32[64,48,128]{2,1,0:T(8,128)} %get-tuple-element.29) | copy-start | bytes 4718596
  108.6 28.4 %copy-start.5 = (f32[8,128]{1,0:T(8,128)S(1)}, f32[8,128]{1,0:T(8,128)}, u32[]{:S(2)}) copy-start(f32[8,128]{1,0:T(8,128)} %copy-done.4) | copy-start | bytes 12292
  108.6 28.4 %copy-start.7 = (f32[128]{0:T(128)S(1)}, f32[128]{0:T(128)}, u32[]{:S(2)}) copy-start(f32[128]{0:T(128)} %param.10) | copy-start | bytes 1540

commit v7 on v6

--- a/solution.py
+++ b/solution.py
@@ -9,6 +9,8 @@
 from jax.sharding import PartitionSpec as P
 
 GROUP_CH = 8
+PITCH = 72
+BATCHES = (3, 6, 8)
 CUT = {128: (8, 4, 4), 8: (2, 2, 2), 4: (2, 2, 1)}
 SLABS = ("z", "x", "y")
 PLANE = ("x", "y")
@@ -46,7 +48,7 @@
 def turned(rows_ref, out_ref):
     slots = out_ref.shape[1]
     for voxel in range(64):
-        out_ref[voxel] = rows_ref[pl.ds(voxel, slots, stride=64), :].astype(out_ref.dtype)
+        out_ref[voxel] = rows_ref[pl.ds(voxel, slots, stride=PITCH), :].astype(out_ref.dtype)
 
 
 def fetch(source, target, sems, pieces):
@@ -62,12 +64,14 @@
     return copies
 
 
-def widen(copies, held_ref, rows_ref):
-    step = held_ref.shape[0] // len(copies)
-    for at, copy in enumerate(copies):
-        copy.wait()
-        rows = slice(at * step, at * step + step)
-        rows_ref[rows, :] = held_ref[rows, :].astype(F32)
+def widen(held_ref, rows_ref, copies=()):
+    slots = held_ref.shape[0] // 64
+    step = slots // max(len(copies), 1)
+    for slot in range(slots):
+        if copies and slot % step == 0:
+            copies[slot // step].wait()
+        rows = held_ref[slot * 64 : slot * 64 + 64, :].astype(F32)
+        rows_ref[slot * PITCH : slot * PITCH + 64, :] = rows
 
 
 def prepare_kernel(
@@ -90,7 +94,7 @@
     copies = fetch(values_hbm, held_ref.at[1], sems.at[1], 4)
     core = core_ref[0]
     count = counts_ref[0]
-    widen(turns, held_ref.at[0], rows_ref)
+    widen(held_ref.at[0], rows_ref, turns)
     turned(rows_ref, own_ref)
     sends = [
         pltpu.make_async_copy(own_ref.at[pl.ds(48 * core, 16)], give_hbm, out_sems.at[0]),
@@ -99,12 +103,12 @@
     ]
     for send in sends:
         send.start()
-    widen(copies, held_ref.at[1], rows_ref)
+    widen(held_ref.at[1], rows_ref, copies)
 
     def over_slots(term):
         total = jnp.zeros((8, 128), F32)
         for slot in range(slots):
-            rows = term(rows_ref[slot * 64 : slot * 64 + 64, :]).reshape(8, 8, 128).sum(axis=0)
+            rows = term(rows_ref[slot * PITCH : slot * PITCH + 64, :]).reshape(8, 8, 128).sum(axis=0)
             total = total + jnp.where(slot < count, rows, 0.0)
         return jnp.broadcast_to(jnp.sum(total, axis=0, keepdims=True), (8, 128))
 
@@ -246,11 +250,11 @@
     norm_ref[3:8, :] = jnp.zeros((5, 128), F32)
     gain, shift = gain_ref[...], shift_ref[...]
     live = iota((slots, 128), 0) < counts_ref[0]
-    rows_ref[...] = values_ref[...].astype(F32)
+    widen(values_ref, rows_ref)
     for plane in range(4):
         pieces = []
         for voxel in range(plane * 16, plane * 16 + 16):
-            normed = (rows_ref[pl.ds(voxel, slots, stride=64), :] - mean) * rstd
+            normed = (rows_ref[pl.ds(voxel, slots, stride=PITCH), :] - mean) * rstd
             pre = normed * gain + shift
             pieces.append(jnp.where(live, pre / (1.0 + jnp.exp(-pre)), 0.0))
         rows = jnp.concatenate(pieces, axis=0)
@@ -298,12 +302,14 @@
                     seen.add(step)
         for step in range(3):
             out_ref[step, turn] = total_ref[step].astype(BF16)
-        if turn in (5, 8):
-            part = pl.ds(0, 6) if turn == 5 else pl.ds(6, 3)
+        if turn in BATCHES:
+            batch = BATCHES.index(turn)
+            first = BATCHES[batch - 1] + 1 if batch else 0
+            part = pl.ds(first, turn + 1 - first)
             for step in range(3):
                 sends.append(
                     pltpu.make_async_copy(
-                        out_ref.at[step, part], out_hbm.at[step, part], out_sems.at[step, turn // 8]
+                        out_ref.at[step, part], out_hbm.at[step, part], out_sems.at[step, batch]
                     )
                 )
                 sends[-1].start()
@@ -317,16 +323,19 @@
     gain_ref,
     shift_ref,
     values_ref,
+    cotangent_ref,
     weight_ref,
     grid_ref,
     out_ref,
     sums_ref,
     total_ref,
     rows_ref,
+    cotangent_rows_ref,
 ):
     slots = grid_ref.shape[3]
     total_ref[...] = jnp.zeros_like(total_ref)
-    rows_ref[...] = values_ref[...].astype(F32)
+    widen(values_ref, rows_ref)
+    widen(cotangent_ref, cotangent_rows_ref)
 
     @pl.loop(0, 9)
     def _(turn):
@@ -346,15 +355,17 @@
     mean, rstd = norm_ref[0:1, :], norm_ref[1:2, :]
     gain, shift = gain_ref[...], shift_ref[...]
     live = iota((slots, 128), 0) < counts_ref[0]
+    scale = rstd * gain
     shift_sum = jnp.zeros((8, 128), F32)
     gain_sum = jnp.zeros((8, 128), F32)
     for voxel in range(64):
-        normed = (rows_ref[pl.ds(voxel, slots, stride=64), :] - mean) * rstd
+        normed = (rows_ref[pl.ds(voxel, slots, stride=PITCH), :] - mean) * rstd
         pre = normed * gain + shift
         sig = 1.0 / (1.0 + jnp.exp(-pre))
         grad = total_ref[voxel // 16, voxel % 16] * sig * (1.0 + pre * (1.0 - sig))
         grad = jnp.where(live, grad, 0.0)
-        out_ref[voxel] = grad
+        places = pl.ds(voxel, slots, stride=PITCH)
+        out_ref[places, :] = cotangent_rows_ref[places, :] + scale * grad
         shift_sum = shift_sum + grad.reshape(slots // 8, 8, 128).sum(axis=0)
         gain_sum = gain_sum + (grad * normed).reshape(slots // 8, 8, 128).sum(axis=0)
     sums_ref[:, 0:128] = jnp.sum(shift_sum, axis=0, keepdims=True)
@@ -367,8 +378,7 @@
     gain_ref,
     plane_ref,
     values_ref,
-    cotangent_ref,
-    grad_ref,
+    part_ref,
     out_hbm,
     weight_hbm,
     gain_out,
@@ -378,7 +388,7 @@
     out_sems,
     weight_sems,
 ):
-    slots = grad_ref.shape[0] // 64
+    slots = values_ref.shape[0] // 64
     pieces = plane_ref.shape[0]
     piece = weight_ref.shape[0] // pieces
     copies = []
@@ -405,14 +415,12 @@
         [gain * shift_sum, gain * gain_sum, jnp.zeros((6, 128), F32)], axis=0
     )
     grouped = exact_dot(stacked, same) / voxels
-    first, second = grouped[0:1], grouped[1:2]
+    constant, slope = rstd * grouped[0:1], rstd * rstd * grouped[1:2]
     chunk = slots // 4
     for slot in range(slots):
         rows = slice(slot * 64, slot * 64 + 64)
-        normed = (values_ref[rows, :].astype(F32) - mean) * rstd
-        grad = grad_ref[pl.ds(slot, 64, stride=slots), :]
-        inner = gain * grad - first - normed * second
-        result = cotangent_ref[rows, :].astype(F32) + rstd * inner
+        centred = values_ref[rows, :].astype(F32) - mean
+        result = part_ref[slot * PITCH : slot * PITCH + 64, :] - constant - centred * slope
         out_ref[rows, :] = jnp.where(slot < counts_ref[0], result, 0.0).astype(BF16)
         if slot % chunk == chunk - 1:
             at = slot // chunk
@@ -450,7 +458,7 @@
         [SMEM, SMEM, HBM, HBM],
         [
             pltpu.VMEM((2, rows, width), BF16),
-            pltpu.VMEM((rows, width), F32),
+            pltpu.VMEM((slots * PITCH, width), F32),
             pltpu.VMEM(turned_shape.shape, BF16),
             pltpu.SemaphoreType.DMA((2, 4)),
             pltpu.SemaphoreType.DMA((3,)),
@@ -490,10 +498,10 @@
     term_shape = jax.ShapeDtypeStruct((3, 9, width, 2 * width), BF16)
     weight_term, grid, norm = call(
         weight_grad_kernel,
-        [term_shape, grid_shape, jax.ShapeDtypeStruct((8, 128), F32)],
+        [term_shape, grid_shape, pltpu.HBM((8, 128), F32)],
         [SMEM, SMEM, VMEM, VMEM, VMEM, VMEM, ANY, ANY, VMEM, VMEM],
         [
-            pltpu.VMEM((rows, width), F32),
+            pltpu.VMEM((slots * PITCH, width), F32),
             pltpu.VMEM((2, 6, 6, slots, 2 * width), BF16),
             pltpu.VMEM((2, 4, 4, slots, 2 * width), BF16),
             pltpu.VMEM((4 * width, 16 * slots), BF16),
@@ -501,7 +509,7 @@
             pltpu.VMEM(term_shape.shape, BF16),
             pltpu.SemaphoreType.DMA((4,)),
             pltpu.SemaphoreType.DMA((6,)),
-            pltpu.SemaphoreType.DMA((3, 2)),
+            pltpu.SemaphoreType.DMA((3, len(BATCHES))),
         ],
         [HBM, HBM, VMEM],
         flops=work,
@@ -523,14 +531,14 @@
         weight_term.reshape(n_plane, piece, 2 * width), PLANE, 0, 0, tiled=True
     )
 
-    grad_pre, sums = call(
+    feature_part, sums = call(
         act_grad_kernel,
         [
-            jax.ShapeDtypeStruct((voxels, slots, width), F32),
+            jax.ShapeDtypeStruct((slots * PITCH, width), F32),
             jax.ShapeDtypeStruct((1, 2 * width), F32),
         ],
-        [SMEM] + [VMEM] * 6,
-        [pltpu.VMEM((4, 16, slots, width), F32), pltpu.VMEM((rows, width), F32)],
+        [SMEM] + [VMEM] * 7,
+        [pltpu.VMEM((4, 16, slots, width), F32)] + [pltpu.VMEM((slots * PITCH, width), F32)] * 2,
         flops=work,
         mib=58,
     )(
@@ -539,6 +547,7 @@
         gain_row,
         shift_row,
         value_rows,
+        cotangent_rows,
         weight.reshape(3, 9, width, 2 * width),
         grid,
     )
@@ -548,11 +557,12 @@
         [part, jnp.broadcast_to(sums.reshape(1, 1, 2 * width), (n_line, 1, 2 * width))], axis=1
     )
     part = jnp.sum(lax.all_to_all(part, "z", 0, 0, tiled=True), axis=0)
-    final, line_sums = part[:-1].astype(BF16), part[-1:]
+    final = part[:-1].astype(BF16)
     line = jnp.broadcast_to(final[None], (n_line,) + final.shape)
     line = lax.all_to_all(line, "z", 0, 0, tiled=True).reshape(piece, 2 * width)
+    line, part = lax.optimization_barrier((line, part))
+    rest = part[-1:]
     split = []
-    rest = line_sums
     for _ in range(3):
         top = lax.reduce_precision(rest, 8, 7)
         split.append(top.astype(BF16))
@@ -568,7 +578,7 @@
             jax.ShapeDtypeStruct((1, width), F32),
             jax.ShapeDtypeStruct((1, width), F32),
         ],
-        [SMEM] + [VMEM] * 6,
+        [SMEM] + [VMEM] * 5,
         [
             pltpu.VMEM((rows, width), BF16),
             pltpu.VMEM((27 * width, 2 * width), F32),
@@ -583,8 +593,7 @@
         gain_row,
         plane,
         value_rows,
-        cotangent_rows,
-        grad_pre.reshape(rows, width),
+        feature_part,
     )
     return (
         grad_features.reshape(features.shape),

time: 140 us -> 137 us (0.979)
  blocking collectives: 68.6 us -> 79.9 us
  waiting for transfers between devices: 20.4 us -> 11.2 us
  starting transfers between devices: 12.4 us -> 9.06 us
    all_to_all x0 -> x1, blocking collectives: none -> 11.5 us  [body(): line = lax.all_to_all(line, 'z', 0, 0, tiled=True).reshape(piece, 2 * width)]
    all_to_all x1 -> x0, waiting for transfers between devices: 8.98 us -> none  [body(): line = lax.all_to_all(line, 'z', 0, 0, tiled=True).reshape(piece, 2 * width)]
    all_to_all x1 -> x0, starting transfers between devices: 3.37 us -> none  [body(): line = lax.all_to_all(line, 'z', 0, 0, tiled=True).reshape(piece, 2 * width)]
  transfers between devices with their start and end apart: 6 -> 5, of which waited for: 3 -> 2; matrix products, arithmetic and copies ran while one was open for 1% -> 1% of each run, Pallas kernels for 12% -> 13%
where the time goes in v7:
time: 137 us
  blocking collectives  79.9 us (58%)
  Pallas kernels  33.2 us (24%)
  waiting for transfers between devices  11.2 us (8%)
  starting transfers between devices  9.06 us (7%)
  between operations  1.68 us (1%)
    all_to_all x1, blocking collectives, body(): plane = lax.all_to_all(plane, PLANE, 0, 0, tiled=True)  28.2 us
    all_to_all x1, blocking collectives, body(): table = lax.all_to_all(sent, SLABS, 0, 0, tiled=True)  26.5 us
    pallas_call x1, Pallas kernels, body(): call(act_grad_kernel, [jax.ShapeDtypeStruct((slots * PITCH, width), F32),...  15.8 us
    all_to_all x1, blocking collectives, body(): part = jnp.sum(lax.all_to_all(part, 'z', 0, 0, tiled=True), axis=0)  13.8 us
    all_to_all x1, blocking collectives, body(): line = lax.all_to_all(line, 'z', 0, 0, tiled=True).reshape(piece, 2 * width)  11.5 us
    all_to_all x1, waiting for transfers between devices, body(): lax.all_to_all(weight_term.reshape(n_plane, piece, 2 * width), PLANE, 0,...  10.1 us
    pallas_call x1, Pallas kernels, body(): call(weight_grad_kernel, [term_shape, grid_shape, pltpu.HBM((8, 128), F32...  9.57 us
    all_to_all x1, starting transfers between devices, body(): lax.all_to_all(weight_term.reshape(n_plane, piece, 2 * width), PLANE, 0,...  4.98 us
  transfers between devices with their start and end apart: 5, of which 2 were waited for; matrix products, arithmetic and copies ran while one was open for 1% of the time, Pallas kernels for 13%

profile of v7, /device:TPU:2, one launch (start us, length us, event | category | flops | bytes accessed | tf_op | source)
XLA Modules:
  0.0 136.8 jit_solution(16732448017802417455)
XLA Ops:
  0.6 0.0 copy-start.7
  1.3 3.2 %shard_map.102 = (bf16[64,48,128]{2,1,0:T(8,128)(2,1)}, bf16[16,48,128]{2,1,0:T(8,128)(2,1)}, bf16[16,48,128]{2,1,0:T(8,128)(2,1)}, f32[128,1,128]{2,1,0:T(1,128)}) custom-call(s32[1]{0:T(128)S(6)} %copy.15.counts_ref, s32[1]{0:T(128)} %bitcast.core_ref, bf16[3072,128]{1,0:T(8,128)(2,1)} %bitcast.30, bf16[3072,128]{1,0:T(8,128)(2,1)} %bitcast.18), custom_call_target="tpu_custom_call" | custom-call | tf_op jit(solution)/shard_map/pallas_call | solution.py:450
  4.5 0.1 collective-permute-start
  4.6 0.5 collective-permute-start.3
  5.1 1.1 collective-permute-done
  6.3 1.0 pad_maximum_fusion
  7.2 3.5 %collective-permute-start.1 = (bf16[2,16,48,128]{3,2,1,0:T(8,128)(2,1)S(1)}, bf16[2,16,48,128]{3,2,1,0:T(8,128)(2,1)S(1)}, u32[]{:S(2)}, u32[]{:S(2)}) collective-permute-start(bf16[2,16,48,128]{3,2,1,0:T(8,128)(2,1)S(1)} %pad_maximum_fusion), channel_id=1, source_target_pairs={{0,2},{2,4},{4,6},{6,8},{8,10},{10,12},{12,14},{14,16},{16,18},{18... | collective-permute-start | bytes 1179656 | tf_op jit(solution)/shard_map/ppermute | solution.py:475
  10.7 26.5 %all_to_all.25.table_ref = f32[128,1,128]{2,1,0:T(1,128)S(1)} all-to-all(f32[128,1,128]{2,1,0:T(1,128)} %get-tuple-element.21), channel_id=1, replica_groups=mesh['z'=8,'x'=4,'y'=4,'ch'=2] {'z','x','y'}, dimensions={0} | all-to-all | bytes 131072 | tf_op jit(solution)/shard_map/all_to_all | solution.py:469
  37.2 0.0 collective-permute-done.1
  37.2 0.0 collective-permute-start.2
  37.2 0.0 copy-done.7
  37.2 0.1 copy.14.near_ref
  37.3 0.0 collective-permute-done.3
  37.3 0.0 copy-start
  37.3 0.0 copy-start.4
  37.3 0.0 copy-start.6
  37.3 1.9 %shard_map.103.middle_ref = bf16[4,6,6,48,256]{4,3,2,1,0:T(8,128)(2,1)S(1)} custom-call(s32[1]{0:T(128)} %bitcast.core_ref, s32[48,27]{1,0:T(8,128)S(1)} %copy.14.near_ref, bf16[4,4,4,48,128]{4,3,2,1,0:T(8,128)(2,1)} %bitcast.32, bf16[4,4,4,48,128]{4,3,2,1,0:T(8,128)(2,1)S(1)} %bitcast.22), custom_call_target="tpu_custom_call" | custom-call | flops 1000000000 | tf_op jit(solution)/shard_map/pallas_call | solution.py:480
  39.2 0.0 collective-permute-done.2
  39.2 0.0 copy-done
  39.3 0.0 copy-done.4
  39.3 0.0 copy-done.6
  39.3 9.6 %shard_map.104 = (bf16[3,9,128,256]{3,2,1,0:T(8,128)(2,1)}, bf16[6,6,6,48,256]{4,3,2,1,0:T(8,128)(2,1)}, f32[8,128]{1,0:T(8,128)}) custom-call(s32[1]{0:T(128)S(6)} %copy.15.counts_ref, s32[1]{0:T(128)} %bitcast.core_ref, s32[48,27]{1,0:T(8,128)S(1)} %copy.14.near_ref, f32[128,1,128]{2,1,0:T(1,128)S(1)} %all_to_all.25.table_ref, f32[1,128]{1,0:T(1,128)S(1)} %bitcast.24, ...), custom_call_target="tpu_custom_call" | custom-call | flops 5435817984 | tf_op jit(solution)/shard_map/pallas_call | solution.py:499
  48.9 5.0 %all-to-all-start.1 = ((bf16[16,216,256]{2,1,0:T(8,128)(2,1)}), bf16[16,216,256]{2,1,0:T(8,128)(2,1)S(1)}, u32[]{:S(2)}, u32[]{:S(2)}) async-start(bf16[16,216,256]{2,1,0:T(8,128)(2,1)} %bitcast.11), calls=%async_computation.1 | async-start | bytes 3538944 | tf_op jit(solution)/shard_map/all_to_all | solution.py:530
  53.8 15.8 %shard_map.105 = (f32[3456,128]{1,0:T(8,128)}, f32[1,256]{1,0:T(1,128)}) custom-call(s32[1]{0:T(128)S(6)} %copy.15.counts_ref, f32[8,128]{1,0:T(8,128)} %get-tuple-element.27.norm_ref, f32[1,128]{1,0:T(1,128)} %bitcast.23, f32[1,128]{1,0:T(1,128)} %bitcast.28, bf16[3072,128]{1,0:T(8,128)(2,1)} %bitcast.19, bf16[3072,128]{1,0:T(8,128)(2,1)} %bitcast.31, ...), custom_call_target="tpu_custom_call" | custom-call | flops 5435817984 | tf_op jit(solution)/shard_map/pallas_call | solution.py:534
  69.6 0.0 copy-start.8
  69.6 10.1 %all-to-all-done.1 = bf16[16,216,256]{2,1,0:T(8,128)(2,1)S(1)} async-done(((bf16[16,216,256]{2,1,0:T(8,128)(2,1)}), bf16[16,216,256]{2,1,0:T(8,128)(2,1)S(1)}, u32[]{:S(2)}, u32[]{:S(2)}) %all-to-all-start.1) | async-done | bytes 1769504 | tf_op jit(solution)/shard_map/all_to_all | solution.py:530
  79.7 0.3 convert_reduce_fusion
  80.0 0.0 copy-done.8
  80.0 13.8 %all_to_all.26 = f32[8,28,256]{2,1,0:T(8,128)S(1)} all-to-all(f32[8,28,256]{2,1,0:T(8,128)S(1)} %pad_maximum_fusion.1), channel_id=1, replica_groups=mesh['z'=8,'x'=4,'y'=4,'ch'=2] {'z'}, dimensions={0} | all-to-all | bytes 458752 | tf_op jit(solution)/shard_map/all_to_all | solution.py:559
  93.8 11.5 %all_to_all.27 = bf16[8,27,256]{2,1,0:T(8,128)(2,1)S(1)} all-to-all(bf16[8,27,256]{2,1,0:T(8,128)(2,1)S(1)} %broadcast_in_dim.24), channel_id=1, replica_groups=mesh['z'=8,'x'=4,'y'=4,'ch'=2] {'z'}, dimensions={0} | all-to-all | bytes 221184 | tf_op jit(solution)/shard_map/all_to_all | solution.py:562
  105.3 0.1 reshape.77
  105.4 0.2 broadcast_in_dim.26
  105.6 0.0 copy-start.1
  105.6 0.0 copy-start.2
  105.6 0.0 copy-start.3
  105.6 0.0 copy-start.5
  105.6 28.2 %all_to_all.28.plane_ref = bf16[16,224,256]{2,1,0:T(8,128)(2,1)S(1)} all-to-all(bf16[16,224,256]{2,1,0:T(8,128)(2,1)S(1)} %broadcast_in_dim.26), channel_id=1, replica_groups=mesh['z'=8,'x'=4,'y'=4,'ch'=2] {'x','y'}, dimensions={0} | all-to-all | bytes 3670016 | tf_op jit(solution)/shard_map/all_to_all | solution.py:572
  133.9 0.0 copy-done.1
  133.9 0.0 copy-done.2
  133.9 0.0 copy-done.3
  133.9 0.0 copy-done.5
  133.9 2.8 %shard_map.106 = (bf16[3072,128]{1,0:T(8,128)(2,1)}, f32[3456,256]{1,0:T(8,128)}, f32[1,128]{1,0:T(1,128)}, f32[1,128]{1,0:T(1,128)}) custom-call(s32[1]{0:T(128)S(6)} %copy.15.counts_ref, f32[8,128]{1,0:T(8,128)S(1)} %copy-done.3, f32[1,128]{1,0:T(1,128)S(1)} %bitcast.25, bf16[16,224,256]{2,1,0:T(8,128)(2,1)S(1)} %all_to_all.28.plane_ref, ...), custom_call_target="tpu_custom_call" | custom-call | tf_op jit(solution)/shard_map/pallas_call | solution.py:573
  (9 shorter events, 0.1 us)
Async XLA Ops:
  0.6 36.6 %copy-start.7 = (s32[48,27]{0,1:T(8,128)S(1)}, s32[48,27]{0,1:T(8,128)}, u32[]{:S(2)}) copy-start(s32[48,27]{0,1:T(8,128)} %param.13) | copy-start | bytes 15556
  4.5 1.7 %collective-permute-start = (bf16[16,48,128]{2,1,0:T(8,128)(2,1)}, bf16[16,48,128]{2,1,0:T(8,128)(2,1)S(1)}, u32[]{:S(2)}, u32[]{:S(2)}) collective-permute-start(bf16[16,48,128]{2,1,0:T(8,128)(2,1)} %get-tuple-element.23), channel_id=1, source_target_pairs={{0,1},{1,0},{2,3},{3,2},{4,5},{5,4},{6,7},{7,6},{8,9},{9,8},{10,11... | collective-permute-start | bytes 589832 | tf_op jit(solution)/shard_map/ppermute | solution.py:473
  4.6 32.7 %collective-permute-start.3 = (bf16[64,48,128]{2,1,0:T(8,128)(2,1)}, bf16[64,48,128]{2,1,0:T(8,128)(2,1)S(1)}, u32[]{:S(2)}, u32[]{:S(2)}) collective-permute-start(bf16[64,48,128]{2,1,0:T(8,128)(2,1)} %get-tuple-element.26), channel_id=1, source_target_pairs={{0,1},{1,0},{2,3},{3,2},{4,5},{5,4},{6,7},{7,6},{8,9},{9,8},{10,11... | collective-permute-start | bytes 2359304 | tf_op jit(solution)/shard_map/ppermute | solution.py:474
  7.2 30.0 %collective-permute-start.1 = (bf16[2,16,48,128]{3,2,1,0:T(8,128)(2,1)S(1)}, bf16[2,16,48,128]{3,2,1,0:T(8,128)(2,1)S(1)}, u32[]{:S(2)}, u32[]{:S(2)}) collective-permute-start(bf16[2,16,48,128]{3,2,1,0:T(8,128)(2,1)S(1)} %pad_maximum_fusion), channel_id=1, source_target_pairs={{0,2},{2,4},{4,6},{6,8},{8,10},{10,12},{12,14},{14,16},{16,18},{18... | collective-permute-start | bytes 1179656 | tf_op jit(solution)/shard_map/ppermute | solution.py:475
  37.2 2.0 %collective-permute-start.2 = (bf16[2,16,48,128]{3,2,1,0:T(8,128)(2,1)S(1)}, bf16[2,16,48,128]{3,2,1,0:T(8,128)(2,1)S(1)}, u32[]{:S(2)}, u32[]{:S(2)}) collective-permute-start(bf16[2,16,48,128]{3,2,1,0:T(8,128)(2,1)S(1)} %collective-permute-done.1), channel_id=1, source_target_pairs={{0,1},{1,0},{2,3},{3,2},{4,5},{5,4},{6,7},{7,6},{8,9},{9,8},{10,11... | collective-permute-start | bytes 1179656 | tf_op jit(solution)/shard_map/ppermute | solution.py:495
  37.3 1.9 %copy-start = (bf16[48,64,128]{2,1,0:T(8,128)(2,1)S(1)}, bf16[48,64,128]{2,1,0:T(8,128)(2,1)}, u32[]{:S(2)}) copy-start(bf16[48,64,128]{2,1,0:T(8,128)(2,1)} %param.7) | copy-start | bytes 2359300
  37.3 1.9 %copy-start.4 = (f32[128]{0:T(128)S(1)}, f32[128]{0:T(128)}, u32[]{:S(2)}) copy-start(f32[128]{0:T(128)} %param.10) | copy-start | bytes 1540
  37.3 1.9 %copy-start.6 = (f32[128]{0:T(128)S(1)}, f32[128]{0:T(128)}, u32[]{:S(2)}) copy-start(f32[128]{0:T(128)} %param.11) | copy-start | bytes 1540
  48.9 30.8 %all-to-all-start.1 = ((bf16[16,216,256]{2,1,0:T(8,128)(2,1)}), bf16[16,216,256]{2,1,0:T(8,128)(2,1)S(1)}, u32[]{:S(2)}, u32[]{:S(2)}) async-start(bf16[16,216,256]{2,1,0:T(8,128)(2,1)} %bitcast.11), calls=%async_computation.1 | async-start | bytes 3538944 | tf_op jit(solution)/shard_map/all_to_all | solution.py:530
  69.6 10.4 %copy-start.8 = (f32[1,256]{1,0:T(1,128)S(1)}, f32[1,256]{1,0:T(1,128)}, u32[]{:S(2)}) copy-start(f32[1,256]{1,0:T(1,128)} %get-tuple-element.30) | copy-start | bytes 3076
  105.6 28.3 %copy-start.1 = (bf16[48,64,128]{2,1,0:T(8,128)(2,1)S(1)}, bf16[48,64,128]{2,1,0:T(8,128)(2,1)}, u32[]{:S(2)}) copy-start(bf16[48,64,128]{2,1,0:T(8,128)(2,1)} %param.7) | copy-start | bytes 2359300
  105.6 28.3 %copy-start.2 = (f32[3456,128]{1,0:T(8,128)S(1)}, f32[3456,128]{1,0:T(8,128)}, u32[]{:S(2)}) copy-start(f32[3456,128]{1,0:T(8,128)} %get-tuple-element.33.part_ref) | copy-start | bytes 5308420
  105.6 28.3 %copy-start.3 = (f32[8,128]{1,0:T(8,128)S(1)}, f32[8,128]{1,0:T(8,128)}, u32[]{:S(2)}) copy-start(f32[8,128]{1,0:T(8,128)} %get-tuple-element.27.norm_ref) | copy-start | bytes 12292
  105.6 28.3 %copy-start.5 = (f32[128]{0:T(128)S(1)}, f32[128]{0:T(128)}, u32[]{:S(2)}) copy-start(f32[128]{0:T(128)} %param.10) | copy-start | bytes 1540

commit v8 on v7

--- a/solution.py
+++ b/solution.py
@@ -155,6 +155,19 @@
     return (near[:, offset : offset + 1] == columns).astype(F32).astype(BF16)
 
 
+def sources(places):
+    readers = {}
+    for b, c in places:
+        readers.setdefault((source(b), source(c)), []).append((b, c))
+    return readers
+
+
+def gathered(picks, table):
+    rows = jnp.dot(jnp.concatenate(picks, axis=0), table, preferred_element_type=F32).astype(BF16)
+    slots = picks[0].shape[0]
+    return [rows[at * slots : at * slots + slots] for at in range(len(picks))]
+
+
 def halo_kernel(core_ref, near_ref, own_ref, own_other_ref, middle_ref, sems):
     slots = near_ref.shape[0]
     mine, other = lanes_of(core_ref[0])
@@ -174,12 +187,10 @@
     for copy in copies:
         copy.wait()
     for plane in range(4):
-        for b, c in places:
-            middle_ref[plane, b, c] = jnp.dot(
-                picks[offset_of(0, b, c)],
-                middle_ref[plane, source(b), source(c)],
-                preferred_element_type=F32,
-            ).astype(BF16)
+        for (b, c), readers in sources(places).items():
+            rows = gathered([picks[offset_of(0, *at)] for at in readers], middle_ref[plane, b, c])
+            for at, block in zip(readers, rows):
+                middle_ref[plane, at[0], at[1]] = block
 
 
 def window(plane_ref, turn):
@@ -270,15 +281,13 @@
             offset: choose(near, offset, lowest, lowest + 2 * slots)
             for offset in sorted({offset_of(dx, b, c) for b, c in places})
         }
-        for b, c in places:
-            outer = face_ref[which, source(b) - 1, source(c) - 1]
-            inner = middle_ref[3 - 3 * which, source(b), source(c)]
-            table = [outer, inner] if which == 0 else [inner, outer]
-            sides_ref[which, b, c] = jnp.dot(
-                picks[offset_of(dx, b, c)],
-                jnp.concatenate(table, axis=0),
-                preferred_element_type=F32,
-            ).astype(BF16)
+        for (b, c), readers in sources(places).items():
+            outer = face_ref[which, b - 1, c - 1]
+            inner = middle_ref[3 - 3 * which, b, c]
+            table = jnp.concatenate([outer, inner] if which == 0 else [inner, outer], axis=0)
+            rows = gathered([picks[offset_of(dx, *at)] for at in readers], table)
+            for at, block in zip(readers, rows):
+                sides_ref[which, at[0], at[1]] = block
     planes = [sides_ref.at[0]] + [middle_ref.at[at] for at in range(4)] + [sides_ref.at[1]]
     for at, plane in enumerate(planes):
         sends.append(pltpu.make_async_copy(plane, grid_hbm.at[at], plane_sems.at[at]))
@@ -464,8 +473,13 @@
             pltpu.SemaphoreType.DMA((3,)),
         ],
         [HBM, HBM, HBM, VMEM],
-        mib=60,
-    )(counts, core, cotangent_rows, value_rows)
+        mib=36,
+    )(
+        counts,
+        core,
+        pltpu.with_memory_space_constraint(cotangent_rows, pltpu.HBM),
+        pltpu.with_memory_space_constraint(value_rows, pltpu.HBM),
+    )
     table = lax.all_to_all(sent, SLABS, 0, 0, tiled=True)
     cores = [(0, 1), (1, 0)]
     ups = [(i, i + 1) for i in range(n_slab - 1)]
@@ -487,7 +501,7 @@
     )(
         core,
         neighbours,
-        pltpu.with_memory_space_constraint(own.reshape(cube), pltpu.HBM),
+        own.reshape(cube),
         own_other.reshape(cube),
     )
 

time: 137 us -> 133 us (0.971)
    all_to_all x1, waiting for transfers between devices: 10.1 us -> 8.48 us  [body(): lax.all_to_all(weight_term.reshape(n_plane, piece, 2 * width), PLANE, 0,...]
  transfers between devices with their start and end apart: 5 -> 5, of which waited for: 2 -> 3; matrix products, arithmetic and copies ran while one was open for 1% -> 0% of each run, Pallas kernels for 13% -> 13%
where the time goes in v8:
time: 133 us
  blocking collectives  79.3 us (60%)
  Pallas kernels  32.3 us (24%)
  waiting for transfers between devices  9.94 us (7%)
  starting transfers between devices  9.05 us (7%)
  between operations  1.65 us (1%)
    all_to_all x1, blocking collectives, body(): plane = lax.all_to_all(plane, PLANE, 0, 0, tiled=True)  28.6 us
    all_to_all x1, blocking collectives, body(): table = lax.all_to_all(sent, SLABS, 0, 0, tiled=True)  26.3 us
    pallas_call x1, Pallas kernels, body(): call(act_grad_kernel, [jax.ShapeDtypeStruct((slots * PITCH, width), F32),...  15.8 us
    all_to_all x1, blocking collectives, body(): part = jnp.sum(lax.all_to_all(part, 'z', 0, 0, tiled=True), axis=0)  12.9 us
    all_to_all x1, blocking collectives, body(): line = lax.all_to_all(line, 'z', 0, 0, tiled=True).reshape(piece, 2 * width)  11.5 us
    pallas_call x1, Pallas kernels, body(): call(weight_grad_kernel, [term_shape, grid_shape, pltpu.HBM((8, 128), F32...  9.59 us
    all_to_all x1, waiting for transfers between devices, body(): lax.all_to_all(weight_term.reshape(n_plane, piece, 2 * width), PLANE, 0,...  8.48 us
    all_to_all x1, starting transfers between devices, body(): lax.all_to_all(weight_term.reshape(n_plane, piece, 2 * width), PLANE, 0,...  4.97 us
  transfers between devices with their start and end apart: 5, of which 3 were waited for; matrix products, arithmetic and copies ran while one was open for 0% of the time, Pallas kernels for 13%

profile of v8, /device:TPU:2, one launch (start us, length us, event | category | flops | bytes accessed | tf_op | source)
XLA Modules:
  0.0 133.0 jit_solution(10870607407663151996)
XLA Ops:
  0.6 0.0 copy-start.7
  1.3 3.0 %shard_map.102 = (bf16[64,48,128]{2,1,0:T(8,128)(2,1)S(1)}, bf16[16,48,128]{2,1,0:T(8,128)(2,1)S(1)}, bf16[16,48,128]{2,1,0:T(8,128)(2,1)S(1)}, f32[128,1,128]{2,1,0:T(1,128)S(1)}) custom-call(s32[1]{0:T(128)S(6)} %copy.15.counts_ref, s32[1]{0:T(128)} %bitcast.core_ref, bf16[3072,128]{1,0:T(8,128)(2,1)} %bitcast.32, bf16[3072,128]{1,0:T(8,128)(2,1)} %bitcast.18), custom_call_target="tpu_custom_call" | custom-call | tf_op jit(solution)/shard_map/pallas_call | solution.py:459
  4.3 0.1 collective-permute-start
  4.4 0.5 collective-permute-start.3
  4.9 0.9 collective-permute-done
  5.9 3.5 %collective-permute-start.1 = (bf16[2,16,48,128]{3,2,1,0:T(8,128)(2,1)S(1)}, bf16[2,16,48,128]{3,2,1,0:T(8,128)(2,1)S(1)}, u32[]{:S(2)}, u32[]{:S(2)}) collective-permute-start(bf16[2,16,48,128]{3,2,1,0:T(8,128)(2,1)S(1)} %pad_maximum_fusion), channel_id=1, source_target_pairs={{0,2},{2,4},{4,6},{6,8},{8,10},{10,12},{12,14},{14,16},{16,18},{18... | collective-permute-start | bytes 1179656 | tf_op jit(solution)/shard_map/ppermute | solution.py:489
  9.4 26.3 %all_to_all.25.table_ref = f32[128,1,128]{2,1,0:T(1,128)S(1)} all-to-all(f32[128,1,128]{2,1,0:T(1,128)S(1)} %get-tuple-element.21), channel_id=1, replica_groups=mesh['z'=8,'x'=4,'y'=4,'ch'=2] {'z','x','y'}, dimensions={0} | all-to-all | bytes 131072 | tf_op jit(solution)/shard_map/all_to_all | solution.py:483
  35.7 0.0 collective-permute-done.1
  35.7 0.0 collective-permute-start.2
  35.7 0.0 copy-done.7
  35.7 0.1 copy.14.near_ref
  35.8 0.0 collective-permute-done.3
  35.8 0.0 copy-start
  35.8 0.0 copy-start.4
  35.8 0.0 copy-start.6
  35.8 1.1 shard_map.103.middle_ref
  36.9 0.5 collective-permute-done.2
  37.4 0.0 copy-done
  37.4 0.0 copy-done.4
  37.4 0.0 copy-done.6
  37.4 9.6 %shard_map.104 = (bf16[3,9,128,256]{3,2,1,0:T(8,128)(2,1)}, bf16[6,6,6,48,256]{4,3,2,1,0:T(8,128)(2,1)}, f32[8,128]{1,0:T(8,128)}) custom-call(s32[1]{0:T(128)S(6)} %copy.15.counts_ref, s32[1]{0:T(128)} %bitcast.core_ref, s32[48,27]{1,0:T(8,128)S(1)} %copy.14.near_ref, f32[128,1,128]{2,1,0:T(1,128)S(1)} %all_to_all.25.table_ref, f32[1,128]{1,0:T(1,128)S(1)} %bitcast.26, ...), custom_call_target="tpu_custom_call" | custom-call | flops 5435817984 | tf_op jit(solution)/shard_map/pallas_call | solution.py:513
  47.0 5.0 %all-to-all-start.1 = ((bf16[16,216,256]{2,1,0:T(8,128)(2,1)}), bf16[16,216,256]{2,1,0:T(8,128)(2,1)S(1)}, u32[]{:S(2)}, u32[]{:S(2)}) async-start(bf16[16,216,256]{2,1,0:T(8,128)(2,1)} %bitcast.11), calls=%async_computation.1 | async-start | bytes 3538944 | tf_op jit(solution)/shard_map/all_to_all | solution.py:544
  52.0 15.8 %shard_map.105 = (f32[3456,128]{1,0:T(8,128)}, f32[1,256]{1,0:T(1,128)}) custom-call(s32[1]{0:T(128)S(6)} %copy.15.counts_ref, f32[8,128]{1,0:T(8,128)} %get-tuple-element.27.norm_ref, f32[1,128]{1,0:T(1,128)} %bitcast.25, f32[1,128]{1,0:T(1,128)} %bitcast.30, bf16[3072,128]{1,0:T(8,128)(2,1)} %bitcast.19, bf16[3072,128]{1,0:T(8,128)(2,1)} %bitcast.33, ...), custom_call_target="tpu_custom_call" | custom-call | flops 5435817984 | tf_op jit(solution)/shard_map/pallas_call | solution.py:548
  67.8 0.0 copy-start.8
  67.8 8.5 %all-to-all-done.1 = bf16[16,216,256]{2,1,0:T(8,128)(2,1)S(1)} async-done(((bf16[16,216,256]{2,1,0:T(8,128)(2,1)}), bf16[16,216,256]{2,1,0:T(8,128)(2,1)S(1)}, u32[]{:S(2)}, u32[]{:S(2)}) %all-to-all-start.1) | async-done | bytes 1769504 | tf_op jit(solution)/shard_map/all_to_all | solution.py:544
  76.3 0.3 convert_reduce_fusion
  76.5 0.0 copy-done.8
  76.6 12.9 %all_to_all.26 = f32[8,28,256]{2,1,0:T(8,128)S(1)} all-to-all(f32[8,28,256]{2,1,0:T(8,128)S(1)} %pad_maximum_fusion.1), channel_id=1, replica_groups=mesh['z'=8,'x'=4,'y'=4,'ch'=2] {'z'}, dimensions={0} | all-to-all | bytes 458752 | tf_op jit(solution)/shard_map/all_to_all | solution.py:573
  89.5 11.5 %all_to_all.27 = bf16[8,27,256]{2,1,0:T(8,128)(2,1)S(1)} all-to-all(bf16[8,27,256]{2,1,0:T(8,128)(2,1)S(1)} %broadcast_in_dim.24), channel_id=1, replica_groups=mesh['z'=8,'x'=4,'y'=4,'ch'=2] {'z'}, dimensions={0} | all-to-all | bytes 221184 | tf_op jit(solution)/shard_map/all_to_all | solution.py:576
  101.0 0.1 reshape.77
  101.1 0.2 broadcast_in_dim.26
  101.3 0.0 copy-start.1
  101.3 0.0 copy-start.2
  101.3 0.0 copy-start.3
  101.3 0.0 copy-start.5
  101.3 28.6 %all_to_all.28.plane_ref = bf16[16,224,256]{2,1,0:T(8,128)(2,1)S(1)} all-to-all(bf16[16,224,256]{2,1,0:T(8,128)(2,1)S(1)} %broadcast_in_dim.26), channel_id=1, replica_groups=mesh['z'=8,'x'=4,'y'=4,'ch'=2] {'x','y'}, dimensions={0} | all-to-all | bytes 3670016 | tf_op jit(solution)/shard_map/all_to_all | solution.py:586
  130.0 0.0 copy-done.1
  130.0 0.0 copy-done.2
  130.0 0.0 copy-done.3
  130.0 0.0 copy-done.5
  130.0 2.8 %shard_map.106 = (bf16[3072,128]{1,0:T(8,128)(2,1)}, f32[3456,256]{1,0:T(8,128)}, f32[1,128]{1,0:T(1,128)}, f32[1,128]{1,0:T(1,128)}) custom-call(s32[1]{0:T(128)S(6)} %copy.15.counts_ref, f32[8,128]{1,0:T(8,128)S(1)} %copy-done.3, f32[1,128]{1,0:T(1,128)S(1)} %bitcast.27, bf16[16,224,256]{2,1,0:T(8,128)(2,1)S(1)} %all_to_all.28.plane_ref, ...), custom_call_target="tpu_custom_call" | custom-call | tf_op jit(solution)/shard_map/pallas_call | solution.py:587
  (10 shorter events, 0.2 us)
Async XLA Ops:
  0.6 35.1 %copy-start.7 = (s32[48,27]{0,1:T(8,128)S(1)}, s32[48,27]{0,1:T(8,128)}, u32[]{:S(2)}) copy-start(s32[48,27]{0,1:T(8,128)} %param.13) | copy-start | bytes 15556
  4.3 1.5 %collective-permute-start = (bf16[16,48,128]{2,1,0:T(8,128)(2,1)S(1)}, bf16[16,48,128]{2,1,0:T(8,128)(2,1)S(1)}, u32[]{:S(2)}, u32[]{:S(2)}) collective-permute-start(bf16[16,48,128]{2,1,0:T(8,128)(2,1)S(1)} %get-tuple-element.23), channel_id=1, source_target_pairs={{0,1},{1,0},{2,3},{3,2},{4,5},{5,4},{6,7},{7,6},{8,9},{9,8},{10,11... | collective-permute-start | bytes 589832 | tf_op jit(solution)/shard_map/ppermute | solution.py:487
  4.4 31.3 %collective-permute-start.3 = (bf16[64,48,128]{2,1,0:T(8,128)(2,1)S(1)}, bf16[64,48,128]{2,1,0:T(8,128)(2,1)S(1)}, u32[]{:S(2)}, u32[]{:S(2)}) collective-permute-start(bf16[64,48,128]{2,1,0:T(8,128)(2,1)S(1)} %get-tuple-element.26), channel_id=1, source_target_pairs={{0,1},{1,0},{2,3},{3,2},{4,5},{5,4},{6,7},{7,6},{8,9},{9,8},{10,11... | collective-permute-start | bytes 2359304 | tf_op jit(solution)/shard_map/ppermute | solution.py:488
  5.9 29.8 %collective-permute-start.1 = (bf16[2,16,48,128]{3,2,1,0:T(8,128)(2,1)S(1)}, bf16[2,16,48,128]{3,2,1,0:T(8,128)(2,1)S(1)}, u32[]{:S(2)}, u32[]{:S(2)}) collective-permute-start(bf16[2,16,48,128]{3,2,1,0:T(8,128)(2,1)S(1)} %pad_maximum_fusion), channel_id=1, source_target_pairs={{0,2},{2,4},{4,6},{6,8},{8,10},{10,12},{12,14},{14,16},{16,18},{18... | collective-permute-start | bytes 1179656 | tf_op jit(solution)/shard_map/ppermute | solution.py:489
  35.7 1.7 %collective-permute-start.2 = (bf16[2,16,48,128]{3,2,1,0:T(8,128)(2,1)S(1)}, bf16[2,16,48,128]{3,2,1,0:T(8,128)(2,1)S(1)}, u32[]{:S(2)}, u32[]{:S(2)}) collective-permute-start(bf16[2,16,48,128]{3,2,1,0:T(8,128)(2,1)S(1)} %collective-permute-done.1), channel_id=1, source_target_pairs={{0,1},{1,0},{2,3},{3,2},{4,5},{5,4},{6,7},{7,6},{8,9},{9,8},{10,11... | collective-permute-start | bytes 1179656 | tf_op jit(solution)/shard_map/ppermute | solution.py:509
  35.8 1.6 %copy-start = (bf16[48,64,128]{2,1,0:T(8,128)(2,1)S(1)}, bf16[48,64,128]{2,1,0:T(8,128)(2,1)}, u32[]{:S(2)}) copy-start(bf16[48,64,128]{2,1,0:T(8,128)(2,1)} %param.7) | copy-start | bytes 2359300
  35.8 1.6 %copy-start.4 = (f32[128]{0:T(128)S(1)}, f32[128]{0:T(128)}, u32[]{:S(2)}) copy-start(f32[128]{0:T(128)} %param.10) | copy-start | bytes 1540
  35.8 1.6 %copy-start.6 = (f32[128]{0:T(128)S(1)}, f32[128]{0:T(128)}, u32[]{:S(2)}) copy-start(f32[128]{0:T(128)} %param.11) | copy-start | bytes 1540
  47.0 29.2 %all-to-all-start.1 = ((bf16[16,216,256]{2,1,0:T(8,128)(2,1)}), bf16[16,216,256]{2,1,0:T(8,128)(2,1)S(1)}, u32[]{:S(2)}, u32[]{:S(2)}) async-start(bf16[16,216,256]{2,1,0:T(8,128)(2,1)} %bitcast.11), calls=%async_computation.1 | async-start | bytes 3538944 | tf_op jit(solution)/shard_map/all_to_all | solution.py:544
  67.8 8.8 %copy-start.8 = (f32[1,256]{1,0:T(1,128)S(1)}, f32[1,256]{1,0:T(1,128)}, u32[]{:S(2)}) copy-start(f32[1,256]{1,0:T(1,128)} %get-tuple-element.30) | copy-start | bytes 3076
  101.3 28.7 %copy-start.1 = (bf16[48,64,128]{2,1,0:T(8,128)(2,1)S(1)}, bf16[48,64,128]{2,1,0:T(8,128)(2,1)}, u32[]{:S(2)}) copy-start(bf16[48,64,128]{2,1,0:T(8,128)(2,1)} %param.7) | copy-start | bytes 2359300
  101.3 28.7 %copy-start.2 = (f32[3456,128]{1,0:T(8,128)S(1)}, f32[3456,128]{1,0:T(8,128)}, u32[]{:S(2)}) copy-start(f32[3456,128]{1,0:T(8,128)} %get-tuple-element.33.part_ref) | copy-start | bytes 5308420
  101.3 28.7 %copy-start.3 = (f32[8,128]{1,0:T(8,128)S(1)}, f32[8,128]{1,0:T(8,128)}, u32[]{:S(2)}) copy-start(f32[8,128]{1,0:T(8,128)} %get-tuple-element.27.norm_ref) | copy-start | bytes 12292
  101.3 28.7 %copy-start.5 = (f32[128]{0:T(128)S(1)}, f32[128]{0:T(128)}, u32[]{:S(2)}) copy-start(f32[128]{0:T(128)} %param.10) | copy-start | bytes 1540

commit v9 on v8

--- a/solution.py
+++ b/solution.py
@@ -10,7 +10,7 @@
 
 GROUP_CH = 8
 PITCH = 72
-BATCHES = (3, 6, 8)
+BATCHES = (2, 5, 7, 8)
 CUT = {128: (8, 4, 4), 8: (2, 2, 2), 4: (2, 2, 1)}
 SLABS = ("z", "x", "y")
 PLANE = ("x", "y")
@@ -125,7 +125,7 @@
         return apart * apart
 
     squares = over_slots(centred)
-    row = exact_dot(total, to_sum) + exact_dot(squares, to_square)
+    row = exact_dot(total, to_sum) / entries + exact_dot(squares, to_square)
     row = row + jnp.where(iota((8, 128), 1) == 32, count.astype(F32), 0.0)
     sent_ref[...] = jnp.broadcast_to(row[0:1].reshape(1, 1, 128), sent_ref.shape)
     for send in sends:
@@ -243,8 +243,8 @@
     held = jnp.sum(table, axis=0)
     voxels = held[:, 32:33] * (64.0 * GROUP_CH)
     entries = table[:, :, 32:33] * (64.0 * GROUP_CH)
-    mean = held / voxels
-    apart = table / entries - mean.reshape(1, 1, 128)
+    mean = jnp.sum(table * entries, axis=0) / voxels
+    apart = table - mean.reshape(1, 1, 128)
     between = jnp.sum(apart * apart * entries, axis=0)
     lane_in, lane_out = iota((128, 128), 0), iota((128, 128), 1)
     from_sum = (lane_in == lane_out // GROUP_CH).astype(F32)

time: 133 us -> 134 us (level)
  no operation moved by 1% of the time
where the time goes in v9:
time: 134 us; the launch traced here: 133 us
  blocking collectives  79.3 us (59%)
  Pallas kernels  32.7 us (24%)
  waiting for transfers between devices  9.95 us (7%)
  starting transfers between devices  9.04 us (7%)
  between operations  1.65 us (1%)
    all_to_all x1, blocking collectives, body(): plane = lax.all_to_all(plane, PLANE, 0, 0, tiled=True)  28.7 us
    all_to_all x1, blocking collectives, body(): table = lax.all_to_all(sent, SLABS, 0, 0, tiled=True)  26.3 us
    pallas_call x1, Pallas kernels, body(): call(act_grad_kernel, [jax.ShapeDtypeStruct((slots * PITCH, width), F32),...  15.8 us
    all_to_all x1, blocking collectives, body(): part = jnp.sum(lax.all_to_all(part, 'z', 0, 0, tiled=True), axis=0)  12.9 us
    all_to_all x1, blocking collectives, body(): line = lax.all_to_all(line, 'z', 0, 0, tiled=True).reshape(piece, 2 * width)  11.5 us
    pallas_call x1, Pallas kernels, body(): call(weight_grad_kernel, [term_shape, grid_shape, pltpu.HBM((8, 128), F32...  10.2 us
    all_to_all x1, waiting for transfers between devices, body(): lax.all_to_all(weight_term.reshape(n_plane, piece, 2 * width), PLANE, 0,...  8.5 us
    all_to_all x1, starting transfers between devices, body(): lax.all_to_all(weight_term.reshape(n_plane, piece, 2 * width), PLANE, 0,...  4.96 us
  transfers between devices with their start and end apart: 5, of which 3 were waited for; matrix products, arithmetic and copies ran while one was open for 0% of the time, Pallas kernels for 13%

profile of v9, /device:TPU:2, one launch (start us, length us, event | category | flops | bytes accessed | tf_op | source)
XLA Modules:
  0.0 133.5 jit_solution(8236354426615357535)
XLA Ops:
  0.6 0.0 copy-start.7
  1.3 2.9 %shard_map.102 = (bf16[64,48,128]{2,1,0:T(8,128)(2,1)S(1)}, bf16[16,48,128]{2,1,0:T(8,128)(2,1)S(1)}, bf16[16,48,128]{2,1,0:T(8,128)(2,1)S(1)}, f32[128,1,128]{2,1,0:T(1,128)S(1)}) custom-call(s32[1]{0:T(128)S(6)} %copy.15.counts_ref, s32[1]{0:T(128)} %bitcast.core_ref, bf16[3072,128]{1,0:T(8,128)(2,1)} %bitcast.32, bf16[3072,128]{1,0:T(8,128)(2,1)} %bitcast.18), custom_call_target="tpu_custom_call" | custom-call | tf_op jit(solution)/shard_map/pallas_call | solution.py:459
  4.2 0.1 collective-permute-start
  4.3 0.5 collective-permute-start.3
  4.8 0.9 collective-permute-done
  5.8 3.5 %collective-permute-start.1 = (bf16[2,16,48,128]{3,2,1,0:T(8,128)(2,1)S(1)}, bf16[2,16,48,128]{3,2,1,0:T(8,128)(2,1)S(1)}, u32[]{:S(2)}, u32[]{:S(2)}) collective-permute-start(bf16[2,16,48,128]{3,2,1,0:T(8,128)(2,1)S(1)} %pad_maximum_fusion), channel_id=1, source_target_pairs={{0,2},{2,4},{4,6},{6,8},{8,10},{10,12},{12,14},{14,16},{16,18},{18... | collective-permute-start | bytes 1179656 | tf_op jit(solution)/shard_map/ppermute | solution.py:489
  9.3 26.3 %all_to_all.25.table_ref = f32[128,1,128]{2,1,0:T(1,128)S(1)} all-to-all(f32[128,1,128]{2,1,0:T(1,128)S(1)} %get-tuple-element.21), channel_id=1, replica_groups=mesh['z'=8,'x'=4,'y'=4,'ch'=2] {'z','x','y'}, dimensions={0} | all-to-all | bytes 131072 | tf_op jit(solution)/shard_map/all_to_all | solution.py:483
  35.6 0.0 collective-permute-done.1
  35.6 0.0 collective-permute-start.2
  35.6 0.0 copy-done.7
  35.6 0.1 copy.14.near_ref
  35.7 0.0 collective-permute-done.3
  35.7 0.0 copy-start
  35.7 0.0 copy-start.4
  35.7 0.0 copy-start.6
  35.7 1.1 shard_map.103.middle_ref
  36.8 0.5 collective-permute-done.2
  37.3 0.0 copy-done
  37.3 0.0 copy-done.4
  37.3 0.0 copy-done.6
  37.3 10.2 %shard_map.104 = (bf16[3,9,128,256]{3,2,1,0:T(8,128)(2,1)}, bf16[6,6,6,48,256]{4,3,2,1,0:T(8,128)(2,1)}, f32[8,128]{1,0:T(8,128)}) custom-call(s32[1]{0:T(128)S(6)} %copy.15.counts_ref, s32[1]{0:T(128)} %bitcast.core_ref, s32[48,27]{1,0:T(8,128)S(1)} %copy.14.near_ref, f32[128,1,128]{2,1,0:T(1,128)S(1)} %all_to_all.25.table_ref, f32[1,128]{1,0:T(1,128)S(1)} %bitcast.26, ...), custom_call_target="tpu_custom_call" | custom-call | flops 5435817984 | tf_op jit(solution)/shard_map/pallas_call | solution.py:513
  47.5 5.0 %all-to-all-start.1 = ((bf16[16,216,256]{2,1,0:T(8,128)(2,1)}), bf16[16,216,256]{2,1,0:T(8,128)(2,1)S(1)}, u32[]{:S(2)}, u32[]{:S(2)}) async-start(bf16[16,216,256]{2,1,0:T(8,128)(2,1)} %bitcast.11), calls=%async_computation.1 | async-start | bytes 3538944 | tf_op jit(solution)/shard_map/all_to_all | solution.py:544
  52.5 15.8 %shard_map.105 = (f32[3456,128]{1,0:T(8,128)}, f32[1,256]{1,0:T(1,128)}) custom-call(s32[1]{0:T(128)S(6)} %copy.15.counts_ref, f32[8,128]{1,0:T(8,128)} %get-tuple-element.27.norm_ref, f32[1,128]{1,0:T(1,128)} %bitcast.25, f32[1,128]{1,0:T(1,128)} %bitcast.30, bf16[3072,128]{1,0:T(8,128)(2,1)} %bitcast.19, bf16[3072,128]{1,0:T(8,128)(2,1)} %bitcast.33, ...), custom_call_target="tpu_custom_call" | custom-call | flops 5435817984 | tf_op jit(solution)/shard_map/pallas_call | solution.py:548
  68.2 0.0 copy-start.8
  68.2 8.5 %all-to-all-done.1 = bf16[16,216,256]{2,1,0:T(8,128)(2,1)S(1)} async-done(((bf16[16,216,256]{2,1,0:T(8,128)(2,1)}), bf16[16,216,256]{2,1,0:T(8,128)(2,1)S(1)}, u32[]{:S(2)}, u32[]{:S(2)}) %all-to-all-start.1) | async-done | bytes 1769504 | tf_op jit(solution)/shard_map/all_to_all | solution.py:544
  76.7 0.3 convert_reduce_fusion
  77.0 0.0 copy-done.8
  77.1 12.9 %all_to_all.26 = f32[8,28,256]{2,1,0:T(8,128)S(1)} all-to-all(f32[8,28,256]{2,1,0:T(8,128)S(1)} %pad_maximum_fusion.1), channel_id=1, replica_groups=mesh['z'=8,'x'=4,'y'=4,'ch'=2] {'z'}, dimensions={0} | all-to-all | bytes 458752 | tf_op jit(solution)/shard_map/all_to_all | solution.py:573
  90.0 11.5 %all_to_all.27 = bf16[8,27,256]{2,1,0:T(8,128)(2,1)S(1)} all-to-all(bf16[8,27,256]{2,1,0:T(8,128)(2,1)S(1)} %broadcast_in_dim.24), channel_id=1, replica_groups=mesh['z'=8,'x'=4,'y'=4,'ch'=2] {'z'}, dimensions={0} | all-to-all | bytes 221184 | tf_op jit(solution)/shard_map/all_to_all | solution.py:576
  101.5 0.1 reshape.77
  101.6 0.2 broadcast_in_dim.26
  101.8 0.0 copy-start.1
  101.8 0.0 copy-start.2
  101.8 0.0 copy-start.3
  101.8 0.0 copy-start.5
  101.8 28.7 %all_to_all.28.plane_ref = bf16[16,224,256]{2,1,0:T(8,128)(2,1)S(1)} all-to-all(bf16[16,224,256]{2,1,0:T(8,128)(2,1)S(1)} %broadcast_in_dim.26), channel_id=1, replica_groups=mesh['z'=8,'x'=4,'y'=4,'ch'=2] {'x','y'}, dimensions={0} | all-to-all | bytes 3670016 | tf_op jit(solution)/shard_map/all_to_all | solution.py:586
  130.5 0.0 copy-done.1
  130.5 0.0 copy-done.2
  130.5 0.0 copy-done.3
  130.5 0.0 copy-done.5
  130.5 2.8 %shard_map.106 = (bf16[3072,128]{1,0:T(8,128)(2,1)}, f32[3456,256]{1,0:T(8,128)}, f32[1,128]{1,0:T(1,128)}, f32[1,128]{1,0:T(1,128)}) custom-call(s32[1]{0:T(128)S(6)} %copy.15.counts_ref, f32[8,128]{1,0:T(8,128)S(1)} %copy-done.3, f32[1,128]{1,0:T(1,128)S(1)} %bitcast.27, bf16[16,224,256]{2,1,0:T(8,128)(2,1)S(1)} %all_to_all.28.plane_ref, ...), custom_call_target="tpu_custom_call" | custom-call | tf_op jit(solution)/shard_map/pallas_call | solution.py:587
  (10 shorter events, 0.2 us)
Async XLA Ops:
  0.6 35.0 %copy-start.7 = (s32[48,27]{0,1:T(8,128)S(1)}, s32[48,27]{0,1:T(8,128)}, u32[]{:S(2)}) copy-start(s32[48,27]{0,1:T(8,128)} %param.13) | copy-start | bytes 15556
  4.2 1.5 %collective-permute-start = (bf16[16,48,128]{2,1,0:T(8,128)(2,1)S(1)}, bf16[16,48,128]{2,1,0:T(8,128)(2,1)S(1)}, u32[]{:S(2)}, u32[]{:S(2)}) collective-permute-start(bf16[16,48,128]{2,1,0:T(8,128)(2,1)S(1)} %get-tuple-element.23), channel_id=1, source_target_pairs={{0,1},{1,0},{2,3},{3,2},{4,5},{5,4},{6,7},{7,6},{8,9},{9,8},{10,11... | collective-permute-start | bytes 589832 | tf_op jit(solution)/shard_map/ppermute | solution.py:487
  4.3 31.3 %collective-permute-start.3 = (bf16[64,48,128]{2,1,0:T(8,128)(2,1)S(1)}, bf16[64,48,128]{2,1,0:T(8,128)(2,1)S(1)}, u32[]{:S(2)}, u32[]{:S(2)}) collective-permute-start(bf16[64,48,128]{2,1,0:T(8,128)(2,1)S(1)} %get-tuple-element.26), channel_id=1, source_target_pairs={{0,1},{1,0},{2,3},{3,2},{4,5},{5,4},{6,7},{7,6},{8,9},{9,8},{10,11... | collective-permute-start | bytes 2359304 | tf_op jit(solution)/shard_map/ppermute | solution.py:488
  5.8 29.8 %collective-permute-start.1 = (bf16[2,16,48,128]{3,2,1,0:T(8,128)(2,1)S(1)}, bf16[2,16,48,128]{3,2,1,0:T(8,128)(2,1)S(1)}, u32[]{:S(2)}, u32[]{:S(2)}) collective-permute-start(bf16[2,16,48,128]{3,2,1,0:T(8,128)(2,1)S(1)} %pad_maximum_fusion), channel_id=1, source_target_pairs={{0,2},{2,4},{4,6},{6,8},{8,10},{10,12},{12,14},{14,16},{16,18},{18... | collective-permute-start | bytes 1179656 | tf_op jit(solution)/shard_map/ppermute | solution.py:489
  35.6 1.7 %collective-permute-start.2 = (bf16[2,16,48,128]{3,2,1,0:T(8,128)(2,1)S(1)}, bf16[2,16,48,128]{3,2,1,0:T(8,128)(2,1)S(1)}, u32[]{:S(2)}, u32[]{:S(2)}) collective-permute-start(bf16[2,16,48,128]{3,2,1,0:T(8,128)(2,1)S(1)} %collective-permute-done.1), channel_id=1, source_target_pairs={{0,1},{1,0},{2,3},{3,2},{4,5},{5,4},{6,7},{7,6},{8,9},{9,8},{10,11... | collective-permute-start | bytes 1179656 | tf_op jit(solution)/shard_map/ppermute | solution.py:509
  35.7 1.6 %copy-start = (bf16[48,64,128]{2,1,0:T(8,128)(2,1)S(1)}, bf16[48,64,128]{2,1,0:T(8,128)(2,1)}, u32[]{:S(2)}) copy-start(bf16[48,64,128]{2,1,0:T(8,128)(2,1)} %param.7) | copy-start | bytes 2359300
  35.7 1.6 %copy-start.4 = (f32[128]{0:T(128)S(1)}, f32[128]{0:T(128)}, u32[]{:S(2)}) copy-start(f32[128]{0:T(128)} %param.10) | copy-start | bytes 1540
  35.7 1.6 %copy-start.6 = (f32[128]{0:T(128)S(1)}, f32[128]{0:T(128)}, u32[]{:S(2)}) copy-start(f32[128]{0:T(128)} %param.11) | copy-start | bytes 1540
  47.5 29.2 %all-to-all-start.1 = ((bf16[16,216,256]{2,1,0:T(8,128)(2,1)}), bf16[16,216,256]{2,1,0:T(8,128)(2,1)S(1)}, u32[]{:S(2)}, u32[]{:S(2)}) async-start(bf16[16,216,256]{2,1,0:T(8,128)(2,1)} %bitcast.11), calls=%async_computation.1 | async-start | bytes 3538944 | tf_op jit(solution)/shard_map/all_to_all | solution.py:544
  68.2 8.8 %copy-start.8 = (f32[1,256]{1,0:T(1,128)S(1)}, f32[1,256]{1,0:T(1,128)}, u32[]{:S(2)}) copy-start(f32[1,256]{1,0:T(1,128)} %get-tuple-element.30) | copy-start | bytes 3076
  101.8 28.7 %copy-start.1 = (bf16[48,64,128]{2,1,0:T(8,128)(2,1)S(1)}, bf16[48,64,128]{2,1,0:T(8,128)(2,1)}, u32[]{:S(2)}) copy-start(bf16[48,64,128]{2,1,0:T(8,128)(2,1)} %param.7) | copy-start | bytes 2359300
  101.8 28.7 %copy-start.2 = (f32[3456,128]{1,0:T(8,128)S(1)}, f32[3456,128]{1,0:T(8,128)}, u32[]{:S(2)}) copy-start(f32[3456,128]{1,0:T(8,128)} %get-tuple-element.33.part_ref) | copy-start | bytes 5308420
  101.8 28.7 %copy-start.3 = (f32[8,128]{1,0:T(8,128)S(1)}, f32[8,128]{1,0:T(8,128)}, u32[]{:S(2)}) copy-start(f32[8,128]{1,0:T(8,128)} %get-tuple-element.27.norm_ref) | copy-start | bytes 12292
  101.8 28.7 %copy-start.5 = (f32[128]{0:T(128)S(1)}, f32[128]{0:T(128)}, u32[]{:S(2)}) copy-start(f32[128]{0:T(128)} %param.10) | copy-start | bytes 1540

commit v10 on v8

--- a/solution.py
+++ b/solution.py
@@ -10,7 +10,7 @@
 
 GROUP_CH = 8
 PITCH = 72
-BATCHES = (3, 6, 8)
+BATCHES = (5, 8)
 CUT = {128: (8, 4, 4), 8: (2, 2, 2), 4: (2, 2, 1)}
 SLABS = ("z", "x", "y")
 PLANE = ("x", "y")

time: 133 us -> 134 us (level)
  no operation moved by 1% of the time
where the time goes in v10:
time: 134 us; the launch traced here: 133 us
  blocking collectives  79.3 us (59%)
  Pallas kernels  32.5 us (24%)
  waiting for transfers between devices  9.94 us (7%)
  starting transfers between devices  9.05 us (7%)
  between operations  1.65 us (1%)
    all_to_all x1, blocking collectives, body(): plane = lax.all_to_all(plane, PLANE, 0, 0, tiled=True)  28.6 us
    all_to_all x1, blocking collectives, body(): table = lax.all_to_all(sent, SLABS, 0, 0, tiled=True)  26.3 us
    pallas_call x1, Pallas kernels, body(): call(act_grad_kernel, [jax.ShapeDtypeStruct((slots * PITCH, width), F32),...  15.8 us
    all_to_all x1, blocking collectives, body(): part = jnp.sum(lax.all_to_all(part, 'z', 0, 0, tiled=True), axis=0)  12.9 us
    all_to_all x1, blocking collectives, body(): line = lax.all_to_all(line, 'z', 0, 0, tiled=True).reshape(piece, 2 * width)  11.5 us
    pallas_call x1, Pallas kernels, body(): call(weight_grad_kernel, [term_shape, grid_shape, pltpu.HBM((8, 128), F32...  9.82 us
    all_to_all x1, waiting for transfers between devices, body(): lax.all_to_all(weight_term.reshape(n_plane, piece, 2 * width), PLANE, 0,...  8.48 us
    all_to_all x1, starting transfers between devices, body(): lax.all_to_all(weight_term.reshape(n_plane, piece, 2 * width), PLANE, 0,...  4.97 us
  transfers between devices with their start and end apart: 5, of which 3 were waited for; matrix products, arithmetic and copies ran while one was open for 0% of the time, Pallas kernels for 13%

profile of v10, /device:TPU:2, one launch (start us, length us, event | category | flops | bytes accessed | tf_op | source)
XLA Modules:
  0.0 133.2 jit_solution(5847970330276671520)
XLA Ops:
  0.6 0.0 copy-start.7
  1.3 3.0 %shard_map.102 = (bf16[64,48,128]{2,1,0:T(8,128)(2,1)S(1)}, bf16[16,48,128]{2,1,0:T(8,128)(2,1)S(1)}, bf16[16,48,128]{2,1,0:T(8,128)(2,1)S(1)}, f32[128,1,128]{2,1,0:T(1,128)S(1)}) custom-call(s32[1]{0:T(128)S(6)} %copy.15.counts_ref, s32[1]{0:T(128)} %bitcast.core_ref, bf16[3072,128]{1,0:T(8,128)(2,1)} %bitcast.32, bf16[3072,128]{1,0:T(8,128)(2,1)} %bitcast.18), custom_call_target="tpu_custom_call" | custom-call | tf_op jit(solution)/shard_map/pallas_call | solution.py:459
  4.3 0.1 collective-permute-start
  4.4 0.5 collective-permute-start.3
  4.9 0.9 collective-permute-done
  5.9 3.5 %collective-permute-start.1 = (bf16[2,16,48,128]{3,2,1,0:T(8,128)(2,1)S(1)}, bf16[2,16,48,128]{3,2,1,0:T(8,128)(2,1)S(1)}, u32[]{:S(2)}, u32[]{:S(2)}) collective-permute-start(bf16[2,16,48,128]{3,2,1,0:T(8,128)(2,1)S(1)} %pad_maximum_fusion), channel_id=1, source_target_pairs={{0,2},{2,4},{4,6},{6,8},{8,10},{10,12},{12,14},{14,16},{16,18},{18... | collective-permute-start | bytes 1179656 | tf_op jit(solution)/shard_map/ppermute | solution.py:489
  9.4 26.3 %all_to_all.25.table_ref = f32[128,1,128]{2,1,0:T(1,128)S(1)} all-to-all(f32[128,1,128]{2,1,0:T(1,128)S(1)} %get-tuple-element.21), channel_id=1, replica_groups=mesh['z'=8,'x'=4,'y'=4,'ch'=2] {'z','x','y'}, dimensions={0} | all-to-all | bytes 131072 | tf_op jit(solution)/shard_map/all_to_all | solution.py:483
  35.7 0.0 collective-permute-done.1
  35.7 0.0 collective-permute-start.2
  35.7 0.0 copy-done.7
  35.7 0.1 copy.14.near_ref
  35.8 0.0 collective-permute-done.3
  35.8 0.0 copy-start
  35.8 0.0 copy-start.4
  35.8 0.0 copy-start.6
  35.8 1.1 shard_map.103.middle_ref
  36.9 0.5 collective-permute-done.2
  37.4 0.0 copy-done
  37.4 0.0 copy-done.4
  37.4 0.0 copy-done.6
  37.4 9.8 %shard_map.104 = (bf16[3,9,128,256]{3,2,1,0:T(8,128)(2,1)}, bf16[6,6,6,48,256]{4,3,2,1,0:T(8,128)(2,1)}, f32[8,128]{1,0:T(8,128)}) custom-call(s32[1]{0:T(128)S(6)} %copy.15.counts_ref, s32[1]{0:T(128)} %bitcast.core_ref, s32[48,27]{1,0:T(8,128)S(1)} %copy.14.near_ref, f32[128,1,128]{2,1,0:T(1,128)S(1)} %all_to_all.25.table_ref, f32[1,128]{1,0:T(1,128)S(1)} %bitcast.26, ...), custom_call_target="tpu_custom_call" | custom-call | flops 5435817984 | tf_op jit(solution)/shard_map/pallas_call | solution.py:513
  47.3 5.0 %all-to-all-start.1 = ((bf16[16,216,256]{2,1,0:T(8,128)(2,1)}), bf16[16,216,256]{2,1,0:T(8,128)(2,1)S(1)}, u32[]{:S(2)}, u32[]{:S(2)}) async-start(bf16[16,216,256]{2,1,0:T(8,128)(2,1)} %bitcast.11), calls=%async_computation.1 | async-start | bytes 3538944 | tf_op jit(solution)/shard_map/all_to_all | solution.py:544
  52.2 15.8 %shard_map.105 = (f32[3456,128]{1,0:T(8,128)}, f32[1,256]{1,0:T(1,128)}) custom-call(s32[1]{0:T(128)S(6)} %copy.15.counts_ref, f32[8,128]{1,0:T(8,128)} %get-tuple-element.27.norm_ref, f32[1,128]{1,0:T(1,128)} %bitcast.25, f32[1,128]{1,0:T(1,128)} %bitcast.30, bf16[3072,128]{1,0:T(8,128)(2,1)} %bitcast.19, bf16[3072,128]{1,0:T(8,128)(2,1)} %bitcast.33, ...), custom_call_target="tpu_custom_call" | custom-call | flops 5435817984 | tf_op jit(solution)/shard_map/pallas_call | solution.py:548
  68.0 0.0 copy-start.8
  68.0 8.5 %all-to-all-done.1 = bf16[16,216,256]{2,1,0:T(8,128)(2,1)S(1)} async-done(((bf16[16,216,256]{2,1,0:T(8,128)(2,1)}), bf16[16,216,256]{2,1,0:T(8,128)(2,1)S(1)}, u32[]{:S(2)}, u32[]{:S(2)}) %all-to-all-start.1) | async-done | bytes 1769504 | tf_op jit(solution)/shard_map/all_to_all | solution.py:544
  76.5 0.3 convert_reduce_fusion
  76.8 0.0 copy-done.8
  76.8 12.9 %all_to_all.26 = f32[8,28,256]{2,1,0:T(8,128)S(1)} all-to-all(f32[8,28,256]{2,1,0:T(8,128)S(1)} %pad_maximum_fusion.1), channel_id=1, replica_groups=mesh['z'=8,'x'=4,'y'=4,'ch'=2] {'z'}, dimensions={0} | all-to-all | bytes 458752 | tf_op jit(solution)/shard_map/all_to_all | solution.py:573
  89.8 11.5 %all_to_all.27 = bf16[8,27,256]{2,1,0:T(8,128)(2,1)S(1)} all-to-all(bf16[8,27,256]{2,1,0:T(8,128)(2,1)S(1)} %broadcast_in_dim.24), channel_id=1, replica_groups=mesh['z'=8,'x'=4,'y'=4,'ch'=2] {'z'}, dimensions={0} | all-to-all | bytes 221184 | tf_op jit(solution)/shard_map/all_to_all | solution.py:576
  101.2 0.1 reshape.77
  101.3 0.2 broadcast_in_dim.26
  101.5 0.0 copy-start.1
  101.5 0.0 copy-start.2
  101.5 0.0 copy-start.3
  101.6 0.0 copy-start.5
  101.6 28.6 %all_to_all.28.plane_ref = bf16[16,224,256]{2,1,0:T(8,128)(2,1)S(1)} all-to-all(bf16[16,224,256]{2,1,0:T(8,128)(2,1)S(1)} %broadcast_in_dim.26), channel_id=1, replica_groups=mesh['z'=8,'x'=4,'y'=4,'ch'=2] {'x','y'}, dimensions={0} | all-to-all | bytes 3670016 | tf_op jit(solution)/shard_map/all_to_all | solution.py:586
  130.2 0.0 copy-done.1
  130.2 0.0 copy-done.2
  130.2 0.0 copy-done.3
  130.2 0.0 copy-done.5
  130.2 2.8 %shard_map.106 = (bf16[3072,128]{1,0:T(8,128)(2,1)}, f32[3456,256]{1,0:T(8,128)}, f32[1,128]{1,0:T(1,128)}, f32[1,128]{1,0:T(1,128)}) custom-call(s32[1]{0:T(128)S(6)} %copy.15.counts_ref, f32[8,128]{1,0:T(8,128)S(1)} %copy-done.3, f32[1,128]{1,0:T(1,128)S(1)} %bitcast.27, bf16[16,224,256]{2,1,0:T(8,128)(2,1)S(1)} %all_to_all.28.plane_ref, ...), custom_call_target="tpu_custom_call" | custom-call | tf_op jit(solution)/shard_map/pallas_call | solution.py:587
  (10 shorter events, 0.2 us)
Async XLA Ops:
  0.6 35.1 %copy-start.7 = (s32[48,27]{0,1:T(8,128)S(1)}, s32[48,27]{0,1:T(8,128)}, u32[]{:S(2)}) copy-start(s32[48,27]{0,1:T(8,128)} %param.13) | copy-start | bytes 15556
  4.3 1.5 %collective-permute-start = (bf16[16,48,128]{2,1,0:T(8,128)(2,1)S(1)}, bf16[16,48,128]{2,1,0:T(8,128)(2,1)S(1)}, u32[]{:S(2)}, u32[]{:S(2)}) collective-permute-start(bf16[16,48,128]{2,1,0:T(8,128)(2,1)S(1)} %get-tuple-element.23), channel_id=1, source_target_pairs={{0,1},{1,0},{2,3},{3,2},{4,5},{5,4},{6,7},{7,6},{8,9},{9,8},{10,11... | collective-permute-start | bytes 589832 | tf_op jit(solution)/shard_map/ppermute | solution.py:487
  4.4 31.3 %collective-permute-start.3 = (bf16[64,48,128]{2,1,0:T(8,128)(2,1)S(1)}, bf16[64,48,128]{2,1,0:T(8,128)(2,1)S(1)}, u32[]{:S(2)}, u32[]{:S(2)}) collective-permute-start(bf16[64,48,128]{2,1,0:T(8,128)(2,1)S(1)} %get-tuple-element.26), channel_id=1, source_target_pairs={{0,1},{1,0},{2,3},{3,2},{4,5},{5,4},{6,7},{7,6},{8,9},{9,8},{10,11... | collective-permute-start | bytes 2359304 | tf_op jit(solution)/shard_map/ppermute | solution.py:488
  5.9 29.8 %collective-permute-start.1 = (bf16[2,16,48,128]{3,2,1,0:T(8,128)(2,1)S(1)}, bf16[2,16,48,128]{3,2,1,0:T(8,128)(2,1)S(1)}, u32[]{:S(2)}, u32[]{:S(2)}) collective-permute-start(bf16[2,16,48,128]{3,2,1,0:T(8,128)(2,1)S(1)} %pad_maximum_fusion), channel_id=1, source_target_pairs={{0,2},{2,4},{4,6},{6,8},{8,10},{10,12},{12,14},{14,16},{16,18},{18... | collective-permute-start | bytes 1179656 | tf_op jit(solution)/shard_map/ppermute | solution.py:489
  35.7 1.7 %collective-permute-start.2 = (bf16[2,16,48,128]{3,2,1,0:T(8,128)(2,1)S(1)}, bf16[2,16,48,128]{3,2,1,0:T(8,128)(2,1)S(1)}, u32[]{:S(2)}, u32[]{:S(2)}) collective-permute-start(bf16[2,16,48,128]{3,2,1,0:T(8,128)(2,1)S(1)} %collective-permute-done.1), channel_id=1, source_target_pairs={{0,1},{1,0},{2,3},{3,2},{4,5},{5,4},{6,7},{7,6},{8,9},{9,8},{10,11... | collective-permute-start | bytes 1179656 | tf_op jit(solution)/shard_map/ppermute | solution.py:509
  35.8 1.6 %copy-start = (bf16[48,64,128]{2,1,0:T(8,128)(2,1)S(1)}, bf16[48,64,128]{2,1,0:T(8,128)(2,1)}, u32[]{:S(2)}) copy-start(bf16[48,64,128]{2,1,0:T(8,128)(2,1)} %param.7) | copy-start | bytes 2359300
  35.8 1.6 %copy-start.4 = (f32[128]{0:T(128)S(1)}, f32[128]{0:T(128)}, u32[]{:S(2)}) copy-start(f32[128]{0:T(128)} %param.10) | copy-start | bytes 1540
  35.8 1.6 %copy-start.6 = (f32[128]{0:T(128)S(1)}, f32[128]{0:T(128)}, u32[]{:S(2)}) copy-start(f32[128]{0:T(128)} %param.11) | copy-start | bytes 1540
  47.3 29.2 %all-to-all-start.1 = ((bf16[16,216,256]{2,1,0:T(8,128)(2,1)}), bf16[16,216,256]{2,1,0:T(8,128)(2,1)S(1)}, u32[]{:S(2)}, u32[]{:S(2)}) async-start(bf16[16,216,256]{2,1,0:T(8,128)(2,1)} %bitcast.11), calls=%async_computation.1 | async-start | bytes 3538944 | tf_op jit(solution)/shard_map/all_to_all | solution.py:544
  68.0 8.8 %copy-start.8 = (f32[1,256]{1,0:T(1,128)S(1)}, f32[1,256]{1,0:T(1,128)}, u32[]{:S(2)}) copy-start(f32[1,256]{1,0:T(1,128)} %get-tuple-element.30) | copy-start | bytes 3076
  101.5 28.7 %copy-start.1 = (bf16[48,64,128]{2,1,0:T(8,128)(2,1)S(1)}, bf16[48,64,128]{2,1,0:T(8,128)(2,1)}, u32[]{:S(2)}) copy-start(bf16[48,64,128]{2,1,0:T(8,128)(2,1)} %param.7) | copy-start | bytes 2359300
  101.5 28.7 %copy-start.2 = (f32[3456,128]{1,0:T(8,128)S(1)}, f32[3456,128]{1,0:T(8,128)}, u32[]{:S(2)}) copy-start(f32[3456,128]{1,0:T(8,128)} %get-tuple-element.33.part_ref) | copy-start | bytes 5308420
  101.5 28.7 %copy-start.3 = (f32[8,128]{1,0:T(8,128)S(1)}, f32[8,128]{1,0:T(8,128)}, u32[]{:S(2)}) copy-start(f32[8,128]{1,0:T(8,128)} %get-tuple-element.27.norm_ref) | copy-start | bytes 12292
  101.6 28.7 %copy-start.5 = (f32[128]{0:T(128)S(1)}, f32[128]{0:T(128)}, u32[]{:S(2)}) copy-start(f32[128]{0:T(128)} %param.10) | copy-start | bytes 1540
